TPU v7x, 32 devices: a whole 2x2x4 slice. The times are simulated.
32 devices in a mesh: seq: 8 (over y, x, core), head: 4 (over z).
Axes of the slice: x: 2, y: 2, z: 4, core: 2. Of those that a mesh axis runs over, the one named last changes fastest.
Arguments:
- layer_input: bfloat16 [16384, 768], P('seq'), may hold values from -6 to 6
- gain_in: float32 [768], replicated, may hold values from 0.5 to 1.5
- w_gate: bfloat16 [768, 1536], P(None, 'head'), may hold values from -0.21875 to 0.21875
- w_inner: bfloat16 [768, 1536], P(None, 'head'), may hold values from -0.21875 to 0.21875
- w_bc: bfloat16 [768, 256], replicated, may hold values from -0.21875 to 0.21875
- w_step: bfloat16 [768, 24], P(None, 'head'), may hold values from -0.21875 to 0.21875
- conv_inner: float32 [4, 1536], P(None, 'head'), may hold values from -3 to 3
- conv_inner_bias: float32 [1536], P('head'), may hold values from -1.5 to 1.5
- conv_bc: float32 [4, 256], replicated, may hold values from -3 to 3
- conv_bc_bias: float32 [256], replicated, may hold values from -1.5 to 1.5
- step_bias: float32 [24], P('head'), may hold values from -2 to 0.5
- decay_log: float32 [24], P('head')
- skip_gain: float32 [24], P('head'), may hold values from 0.5 to 1.5
- gain_out: float32 [1536], P('head'), may hold values from 0.5 to 1.5
- w_out: bfloat16 [1536, 768], P('head'), may hold values from -0.15625 to 0.15625
- output_grad: bfloat16 [16384, 768], P('seq', 'head'), may hold values from -6 to 6
Outputs:
- mixed: bfloat16 [16384, 768], P('seq', 'head')
- grad_input: float32 [16384, 768], P('seq')
- grad_gain_in: float32 [768], replicated
- grad_w_gate: float32 [768, 1536], P(None, 'head')
- grad_w_inner: float32 [768, 1536], P(None, 'head')
- grad_w_bc: float32 [768, 256], replicated
- grad_w_step: float32 [768, 24], P(None, 'head')
- grad_conv_inner: float32 [4, 1536], P(None, 'head')
- grad_conv_inner_bias: float32 [1536], P('head')
- grad_conv_bc: float32 [4, 256], replicated
- grad_conv_bc_bias: float32 [256], replicated
- grad_step_bias: float32 [24], P('head')
- grad_decay_log: float32 [24], P('head')
- grad_skip_gain: float32 [24], P('head')
- grad_gain_out: float32 [1536], P('head')
- grad_w_out: float32 [1536, 768], P('head')
All inputs are finite; a program needn't handle non-finite values.
Results may differ from a plain program's by a relative error of at most 0.012.
The roundings to bfloat16 on the way count: a program that leaves them out, or rounds other values in their place, can miss the bound.
Values may be sent and summed in bfloat16 or wider, within the bound.
No kernel may reach another device: no remote copies, remote signals or barrier semaphores. Data moves between devices by JAX's collectives and lax.ppermute only.
A program may use at most 192 MiB of HBM per device.

v0:
```python
import jax
import jax.numpy as jnp
from jax import lax
from jax.sharding import PartitionSpec as P

KERNEL = 4
GROUP = 256
DI = 1536


HIGH = lax.Precision.HIGHEST
eps = 1e-05


def shifted(block, axis, distance):
    devices = range(lax.axis_size(axis))
    route = [(i - distance, i) for i in devices if i - distance in devices]
    return lax.ppermute(block, axis, route)


def prefix(value, axis, join, neutral, backward):
    count, mine = (lax.axis_size(axis), lax.axis_index(axis))
    pieces = jax.tree.map(lambda part: lax.all_gather(part, axis), value)
    if backward:
        pieces = jax.tree.map(lambda part: part[::-1], pieces)
        mine = count - 1 - mine
    subtotal = jax.tree.map(
        lambda part, zero: jnp.full_like(part, 0) + jnp.asarray(zero, part.dtype), value, neutral
    )

    def lap(position, subtotal):
        longer = join(subtotal, jax.tree.map(lambda part: part[position], pieces))
        return jax.tree.map(lambda new, old: jnp.where(position < mine, new, old), longer, subtotal)

    return lax.fori_loop(0, count - 1, lap, subtotal)


def contract(left, right, left_dim, right_dim):
    return lax.dot_general(
        left, right, (((left_dim,), (right_dim,)), ((), ())), preferred_element_type=jnp.float32
    )


def contract_high(left, right, left_dim, right_dim):
    return lax.dot_general(
        left,
        right,
        (((left_dim,), (right_dim,)), ((), ())),
        precision=HIGH,
        preferred_element_type=jnp.float32,
    )


def conv_apply(pre, previous, weights, bias):
    count = pre.shape[0]
    padded = jnp.concatenate([previous, pre], 0)
    total = bias[None, :] + sum(
        (weights[tap][None, :] * padded[tap : tap + count] for tap in range(weights.shape[0]))
    )
    return jax.nn.silu(total)


def group_parts(inner3, keys3, step3, rate3):
    cum = jnp.cumsum(rate3, axis=1)
    tail = jnp.exp(cum[:, -1:, :] - cum) * step3
    local = jnp.einsum("klh,klhp,kln->khpn", tail, inner3, keys3, precision=HIGH)
    return (cum, local)


def carry_states(cum, local, start):
    starts = []
    state = start
    for block in range(cum.shape[0]):
        starts.append(state)
        state = jnp.exp(cum[block, -1])[:, None, None] * state + local[block]
    return (jnp.stack(starts), state)


def group_out(inner3, keys3, queries3, step3, cum, starts):
    length = cum.shape[1]
    scores = jnp.einsum("kin,kjn->kij", queries3, keys3, precision=HIGH)
    lower = (jnp.arange(length)[:, None] >= jnp.arange(length)[None, :])[None, :, :, None]
    diff = cum[:, :, None, :] - cum[:, None, :, :]
    decay = jnp.where(lower, jnp.exp(jnp.where(lower, diff, 0.0)), 0.0)
    mixing = scores[..., None] * decay * step3[:, None, :, :]
    output = jnp.einsum("kijh,kjhp->kihp", mixing, inner3, precision=HIGH)
    return output + jnp.exp(cum)[..., None] * jnp.einsum(
        "khpn,kin->kihp", starts, queries3, precision=HIGH
    )


def state_path(inner3, keys3, queries3, step3, rate3, start):
    cum, local = group_parts(inner3, keys3, step3, rate3)
    starts, final = carry_states(cum, local, start)
    return (group_out(inner3, keys3, queries3, step3, cum, starts), final)


def combine_states(earlier, later):
    return (earlier[0] + later[0], jnp.exp(later[0])[:, None, None] * earlier[1] + later[1])


def per_device(
    layer_input,
    gain_in,
    w_gate,
    w_inner,
    w_bc,
    w_step,
    conv_inner,
    conv_inner_bias,
    conv_bc,
    conv_bc_bias,
    step_bias,
    decay_log,
    skip_gain,
    gain_out,
    w_out,
    output_grad,
):
    count = layer_input.shape[0]
    heads_here = decay_log.shape[0]
    inner_width = w_gate.shape[1]
    head_dim = inner_width // heads_here
    states = w_bc.shape[1] // 2
    blocks = count // GROUP
    edge_rows = KERNEL - 1
    layer_x = layer_input.astype(jnp.float32)
    scale_in = lax.rsqrt(jnp.mean(layer_x * layer_x, -1, keepdims=True) + eps)
    normed = (layer_x * scale_in * gain_in).astype(jnp.bfloat16)
    gate = jnp.dot(normed, w_gate, preferred_element_type=jnp.float32)
    inner_pre = jnp.dot(normed, w_inner, preferred_element_type=jnp.float32)
    bc_pre = jnp.dot(normed, w_bc, preferred_element_type=jnp.float32)
    step_raw = jnp.dot(normed, w_step, preferred_element_type=jnp.float32)
    pre = jnp.concatenate([inner_pre, bc_pre], 1)
    previous = shifted(pre[count - edge_rows :], "seq", 1)
    conv_weights = jnp.concatenate([conv_inner, conv_bc], 1)
    conv_bias = jnp.concatenate([conv_inner_bias, conv_bc_bias], 0)
    acted = conv_apply(pre, previous, conv_weights, conv_bias)
    inner = acted[:, :inner_width]
    keys = acted[:, inner_width : inner_width + states]
    queries = acted[:, inner_width + states :]
    step = jax.nn.softplus(step_raw + step_bias)
    rate = -jnp.exp(decay_log) * step
    inner3 = inner.reshape(blocks, GROUP, heads_here, head_dim)
    keys3 = keys.reshape(blocks, GROUP, states)
    queries3 = queries.reshape(blocks, GROUP, states)
    step3 = step.reshape(blocks, GROUP, heads_here)
    rate3 = rate.reshape(blocks, GROUP, heads_here)
    cum, local = group_parts(inner3, keys3, step3, rate3)
    zero_state = jnp.zeros((heads_here, head_dim, states), jnp.float32)
    ignored, own_state = carry_states(cum, local, zero_state)
    own_decay = jnp.sum(cum[:, -1, :], 0)
    identity = (jnp.zeros_like(own_decay), zero_state)
    before_decay, incoming = prefix((own_decay, own_state), "seq", combine_states, identity, False)
    starts, ignored_final = carry_states(cum, local, incoming)
    ssd3 = (
        group_out(inner3, keys3, queries3, step3, cum, starts)
        + skip_gain[None, None, :, None] * inner3
    )
    ssd = ssd3.reshape(count, inner_width)
    gate_act = jax.nn.silu(gate)
    mixed_inner = ssd * gate_act
    squares = lax.psum(jnp.sum(mixed_inner * mixed_inner, -1), "head")
    scale_out = lax.rsqrt(squares / DI + eps)[:, None]
    normed_out = (mixed_inner * scale_out * gain_out).astype(jnp.bfloat16)
    summed = lax.psum_scatter(
        jnp.dot(normed_out, w_out, preferred_element_type=jnp.float32),
        "head",
        scatter_dimension=1,
        tiled=True,
    )
    piece = summed.shape[1]
    residual = lax.dynamic_slice_in_dim(layer_x, lax.axis_index("head") * piece, piece, 1)
    mixed = (residual + summed).astype(jnp.bfloat16)
    cotangent = lax.all_gather(output_grad, "head", axis=1, tiled=True)
    grad_w_out = contract(normed_out, cotangent, 0, 0)
    grad_normed_out = contract(cotangent, w_out, 1, 1)
    scaled = grad_normed_out * gain_out
    grad_gain_out = jnp.sum(grad_normed_out * mixed_inner * scale_out, 0)
    cross = lax.psum(jnp.sum(scaled * mixed_inner, -1), "head")
    grad_mixed = scaled * scale_out - mixed_inner * scale_out**3 * (cross / DI)[:, None]
    grad_ssd = grad_mixed * gate_act
    sigmoid_gate = jax.nn.sigmoid(gate)
    grad_gate = grad_mixed * ssd * sigmoid_gate * (1.0 + gate * (1.0 - sigmoid_gate))
    gate_round = grad_gate.astype(jnp.bfloat16)
    grad3 = grad_ssd.reshape(blocks, GROUP, heads_here, head_dim)
    grad_skip = jnp.sum(grad3 * inner3, (0, 1, 3))
    local_grads = jnp.einsum("kih,kihp,kin->khpn", jnp.exp(cum), grad3, queries3, precision=HIGH)
    carried = zero_state
    for block in range(blocks - 1, -1, -1):
        carried = local_grads[block] + jnp.exp(cum[block, -1])[:, None, None] * carried
    after_decay, outgoing = prefix((own_decay, carried), "seq", combine_states, identity, True)
    ignored_out, pull = jax.vjp(state_path, inner3, keys3, queries3, step3, rate3, incoming)
    grad_inner3, grad_keys, grad_queries, grad_step3, grad_rate3, ignored_start = pull(
        (grad3, outgoing)
    )
    grad_inner = (grad_inner3 + skip_gain[None, None, :, None] * grad3).reshape(count, inner_width)
    grad_rate = grad_rate3.reshape(count, heads_here)
    grad_step = grad_step3.reshape(count, heads_here) - jnp.exp(decay_log) * grad_rate
    grad_decay_log = jnp.sum(rate * grad_rate, 0)
    grad_step_raw = grad_step * jax.nn.sigmoid(step_raw + step_bias)
    grad_step_bias = jnp.sum(grad_step_raw, 0)
    grad_bc = jnp.concatenate(
        [grad_keys.reshape(count, states), grad_queries.reshape(count, states)], 1
    )
    grad_bc = lax.psum(grad_bc, "head")
    ignored_acted, conv_pull = jax.vjp(conv_apply, pre, previous, conv_weights, conv_bias)
    grad_pre, grad_previous, grad_weights, grad_bias = conv_pull(
        jnp.concatenate([grad_inner, grad_bc], 1)
    )
    arrived = shifted(grad_previous, "seq", -1)
    grad_pre = jnp.concatenate(
        [grad_pre[: count - edge_rows], grad_pre[count - edge_rows :] + arrived], 0
    )
    inner_round = grad_pre[:, :inner_width].astype(jnp.bfloat16)
    grad_bc_pre = grad_pre[:, inner_width:]
    normed_wide = normed.astype(jnp.float32)
    grad_w_gate = contract(normed, gate_round, 0, 0)
    grad_w_inner = contract(normed, inner_round, 0, 0)
    grad_w_step = contract_high(normed_wide, grad_step_raw, 0, 0)
    grad_w_bc = contract_high(normed_wide, grad_bc_pre, 0, 0)
    bc_term = contract_high(grad_bc_pre, w_bc.astype(jnp.float32), 1, 1)
    partial_grad = contract(gate_round, w_gate, 1, 1) + contract(inner_round, w_inner, 1, 1)
    partial_grad = partial_grad + contract_high(grad_step_raw, w_step.astype(jnp.float32), 1, 1)
    grad_conv_bc = grad_weights[:, inner_width:]
    grad_conv_bc_bias = grad_bias[inner_width:]
    spread_term = 0.0
    grad_normed = lax.psum(partial_grad + spread_term, "head") + bc_term
    scaled_in = grad_normed * gain_in
    grad_gain_in = jnp.sum(grad_normed * layer_x * scale_in, 0)
    grad_input = scaled_in * scale_in - layer_x * scale_in**3 * jnp.mean(
        scaled_in * layer_x, -1, keepdims=True
    )
    grad_input = grad_input + cotangent.astype(jnp.float32)
    totals = lax.psum(
        (
            grad_gain_in,
            grad_w_gate,
            grad_w_inner,
            grad_w_bc,
            grad_w_step,
            grad_weights[:, :inner_width],
            grad_bias[:inner_width],
            grad_conv_bc,
            grad_conv_bc_bias,
            grad_step_bias,
            grad_decay_log,
            grad_skip,
            grad_gain_out,
            grad_w_out,
        ),
        "seq",
    )
    return (
        mixed,
        grad_input,
        totals[0],
        totals[1],
        totals[2],
        totals[3],
        totals[4],
        totals[5],
        totals[6],
        totals[7],
        totals[8],
        totals[9],
        totals[10],
        totals[11],
        totals[12],
        totals[13],
    )


def solution(mesh):
    placed = (
        P("seq", None),
        P(),
        P(None, "head"),
        P(None, "head"),
        P(),
        P(None, "head"),
        P(None, "head"),
        P("head"),
        P(),
        P(),
        P("head"),
        P("head"),
        P("head"),
        P("head"),
        P("head", None),
        P("seq", "head"),
    )
    return jax.shard_map(
        per_device,
        mesh=mesh,
        in_specs=placed,
        out_specs=(
            P("seq", "head"),
            P("seq", None),
            P(),
            P(None, "head"),
            P(None, "head"),
            P(),
            P(None, "head"),
            P(None, "head"),
            P("head"),
            P(),
            P(),
            P("head"),
            P("head"),
            P("head"),
            P("head"),
            P("head", None),
        ),
        check_vma=False,
    )
```

profile of v0, /device:TPU:0, one launch (start us, length us, event | category | flops | bytes accessed | tf_op | source)
XLA Modules:
  0.0 801.6 jit_solution(9799903853271511920)
XLA Ops:
  7.2 4.8 copy.308
  24.7 6.1 reduce-window.14
  36.4 3.5 maximum_maximum_fusion
  40.0 6.8 fusion.35
  50.2 3.1 copy.395
  57.3 5.9 fusion.50
  68.8 14.9 %all-reduce.25 = f32[48]{0:T(128)S(1)} all-reduce(f32[48]{0:T(128)S(1)} %dynamic-update-slice), channel_id=2, replica_groups=mesh['seq'=8,'head'=4] {'seq'}, use_global_device_ids=true, to_apply=%add.25 | all-reduce | flops 48 | bytes 384
  94.0 4.7 fusion.122
  98.6 7.5 while.28
  118.7 15.5 %fusion.42 = f32[8,256,6,64]{1,3,2,0:T(8,128)S(1)} fusion(f32[8,256,6,64]{1,3,2,0:T(8,128)S(1)} %fusion.123, f32[8,256,6,64]{1,0,3,2:T(8,128)S(1)} %bitcast.270, f32[8,256,6]{1,2,0:T(8,128)S(1)} %bitcast.291, f32[8,256,6]{1,2,0:T(8,128)S(1)} %bitcast.312, f32[8,256,256]{2,1,0:T(8,128)S(1)} %copy-done.37, pred[256,256]{1,0:T(8,128)(4,1)S(1)} %copy-done.82, ...), kind=kOutput, calls=%fused_computation.72 | convolution fusion | flops 2434793472 | bytes 11747352 | tf_op jit(solution)/shard_map/kijh,kjhp->kihp/dot_general | solution.py:86
  137.9 4.8 multiply_reduce_fusion.10
  142.7 12.6 %psum.126 = f32[2048]{0:T(1024)S(1)} all-reduce(f32[2048]{0:T(1024)S(1)} %get-tuple-element.418), channel_id=1, replica_groups=mesh['seq'=8,'head'=4] {'head'}, use_global_device_ids=true, to_apply=%region_7.8 | all-reduce | flops 2048 | bytes 16384 | tf_op jit(solution)/shard_map/psum | solution.py:163
  155.3 4.1 all-gather.7.cloned.1.call-done
  159.4 6.9 multiply_reduce_fusion.6
  166.2 9.1 %psum.127 = f32[2048]{0:T(1024)S(1)} all-reduce(f32[2048]{0:T(1024)S(1)} %get-tuple-element.348), channel_id=1, replica_groups=mesh['seq'=8,'head'=4] {'head'}, use_global_device_ids=true, to_apply=%region_10.11 | all-reduce | flops 2048 | bytes 16384 | tf_op jit(solution)/shard_map/psum | solution.py:180
  175.4 8.6 %multiply_reduce_fusion.7 = (f32[384]{0:T(512)}, f32[2048,384]{0,1:T(8,128)S(1)}, bf16[2048,384]{0,1:T(8,128)(2,1)}) fusion(f32[2048,640]{0,1:T(8,128)} %copy-done.15, f32[2048,384]{0,1:T(8,128)} %get-tuple-element.463, f32[2048]{0:T(1024)S(1)} %broadcast_multiply_fusion.5, f32[2048,384]{0,1:T(8,128)} %get-tuple-element.419, ...), kind=kLoop, calls=%fused_computation.75 | loop fusion | flops 14941824 | bytes 20474880 | tf_op jit(solution)/shard_map/reduce_sum | solution.py:187
  187.1 3.7 fusion.46
  194.0 8.4 %fusion.76 = f32[8,256,128]{2,1,0:T(8,128)S(1)} fusion(f32[8,6,64,128]{3,2,1,0:T(8,128)} %copy-done.24, f32[8,256,6,64]{1,0,3,2:T(8,128)} %bitcast.264, f32[8,256,6]{1,2,0:T(8,128)} %get-tuple-element.454), kind=kOutput, calls=%fused_computation.115 | convolution fusion | flops 1208745984 | bytes 5816320 | tf_op jit(solution)/shard_map/transpose(jvp(khpn,kin->kihp))/dot_general | solution.py:87
  202.5 22.0 %fusion.11 = (f32[8,256,6]{1,2,0:T(8,128)}, f32[8,256,6]{1,2,0:T(8,128)}, f32[8,256,6]{1,2,0:T(8,128)}, f32[8,256,256]{2,1,0:T(8,128)S(1)}) fusion(f32[8,256,6]{1,2,0:T(8,128)S(1)} %bitcast.292, f32[8,256,6]{1,2,0:T(8,128)S(1)} %bitcast.313, f32[8,256,256]{2,1,0:T(8,128)} %fusion.122, pred[256,256]{1,0:T(8,128)(4,1)S(1)} %copy-done.83, ...), kind=kOutput, calls=%fused_computation.24 | convolution fusion | flops 2462543872 | bytes 10797056 | tf_op jit(solution)/shard_map/transpose(jvp(kijh,kjhp->kihp))/dot_general | solution.py:86
  232.9 15.9 %while.29 = (s32[]{:T(128)}, f32[6,64,128]{2,1,0:T(8,128)S(1)}, s32[]{:T(128)}, f32[8,6]{1,0:T(8,128)}, f32[8,6,64,128]{3,2,1,0:T(8,128)}, /*index=5*/s32[]{:T(128)}, s32[]{:T(128)}) while((s32[]{:T(128)}, f32[6,64,128]{2,1,0:T(8,128)S(1)}, s32[]{:T(128)}, f32[8,6]{1,0:T(8,128)}, f32[8,6,64,128]{3,2,1,0:T(8,128)}, ...), condition=%wide.region_12.13_spmd.clone, body=%wide.region_11.12_spmd.clone.sunk | while | flops 196612 | bytes 590001 | solution.py:35
  261.1 6.0 fusion.73
  267.2 4.5 convolution_add_fusion.3
  277.4 6.6 fusion.110
  284.3 4.9 multiply_reduce_fusion.8
  289.3 4.4 fusion.127
  296.7 12.9 %fusion.38 = f32[8,256,6,64]{1,3,2,0:T(8,128)S(1)} fusion(f32[8,256,6,64]{1,3,2,0:T(8,128)S(1)} %fusion.81, f32[8,256,6,64]{1,0,3,2:T(8,128)S(1)} %bitcast.267, f32[8,256,6]{1,2,0:T(8,128)S(1)} %bitcast.293, f32[8,256,6]{1,2,0:T(8,128)S(1)} %bitcast.314, f32[8,256,256]{2,1,0:T(8,128)S(1)} %copy-done.38, pred[256,256]{1,0:T(8,128)(4,1)S(1)} %copy-done.84, ...), kind=kOutput, calls=%fused_computation.67 | convolution fusion | flops 2434793472 | bytes 11747352 | tf_op jit(solution)/shard_map/transpose(jvp(kijh,kjhp->kihp))/dot_general | solution.py:86
  311.5 3.1 copy.401
  315.5 4.8 multiply_reduce_fusion.5
  321.0 15.0 %reduce-window.16 = f32[8,6,2,128]{3,0,1,2:T(8,128)S(1)} reduce-window(f32[8,6,2,128]{3,0,1,2:T(8,128)S(1)} %copy.356, f32[]{:T(128)} %constant.89.clone.1), window={size=1x1x1x128 pad=0_0x0_0x0_0x0_127}, to_apply=%region_28.29 | reduce-window | flops 1560576 | bytes 98308 | tf_op jit(solution)/shard_map/reduce-window.2
  336.6 4.0 constant_dynamic-update-slice_fusion.3
  340.5 4.5 fusion.124
  345.1 17.9 %all-reduce.32.cloned.1.call-done = f32[2048,256]{0,1:T(8,128)} async-done(((f32[2048,256]{0,1:T(8,128)}), f32[2048,256]{0,1:T(8,128)}) %all-reduce.32.cloned.1.call-update) | async-done | bytes 2097168 | tf_op jit(solution)/shard_map/psum | solution.py:206
  363.0 3.3 constant_dynamic-update-slice_fusion.2
  366.2 14.9 %multiply_reduce_fusion.3 = (f32[640]{0:T(1024)S(1)}, f32[640]{0:T(1024)S(1)}, f32[640]{0:T(1024)S(1)}, f32[640]{0:T(1024)S(1)}, f32[640]{0:T(1024)S(1)}, /*index=5*/f32[2048,640]{0,1:T(8,128)}) fusion(f32[2051,640]{0,1:T(8,128)} %copy-done.2, f32[2048,256]{0,1:T(8,128)S(1)} %fusion.121, f32[2048,384]{0,1:T(8,128)S(1)} %copy-done.14, ...), kind=kLoop, calls=%fused_computation.58 | loop fusion | flops 24900480 | bytes 36712960 | tf_op jit(solution)/shard_map/transpose(jvp())/reduce_sum | solution.py:58
  381.1 3.4 broadcast_multiply_fusion
  386.1 6.6 pad_add_fusion
  392.7 4.0 slice.285
  399.0 9.2 %add_add_fusion = f32[2048,768]{0,1:T(8,128)} fusion(f32[2048,768]{0,1:T(8,128)} %fusion.124, f32[2048,768]{0,1:T(8,128)} %fusion.127, bf16[768,384]{1,0:T(8,128)(2,1)S(1)} %copy-done.65, f32[2045,640]{0,1:T(8,128)S(1)} %slice.285, f32[3,640]{0,1:T(8,128)S(1)} %add_add_fusion.2), kind=kOutput, calls=%fused_computation.36 | convolution fusion | flops 1214251008 | bytes 24707072 | tf_op jit(solution)/shard_map/dot_general | solution.py:39
  408.5 5.5 convert_element_type.22
  414.3 4.9 fusion.125
  424.3 3.6 fusion.108
  430.8 44.6 %reduce-scatter.2.cloned.1.call-done = f32[2048,192]{0,1:T(8,128)} async-done(((f32[2048,768]{0,1:T(8,128)}), f32[2048,192]{0,1:T(8,128)}) %reduce-scatter.2.cloned.1.call-update) | async-done | bytes 1572880 | tf_op jit(solution)/shard_map/reduce_scatter | solution.py:166
  478.4 222.8 %all-reduce.34.cloned.1.call-done = f32[2048,768]{0,1:T(8,128)} async-done(((f32[2048,768]{0,1:T(8,128)}), f32[2048,768]{0,1:T(8,128)}) %all-reduce.34.cloned.1.call-update) | async-done | bytes 6291472 | tf_op jit(solution)/shard_map/psum | solution.py:228
  701.2 8.9 %fusion.20 = (f32[768]{0:T(1024)S(1)}, f32[2048]{0:T(1024)S(1)}, f32[2048,768]{0,1:T(8,128)S(1)}) fusion(bf16[2048,768]{0,1:T(8,128)(2,1)} %copy.308, f32[2048]{0:T(1024)S(1)} %copy-done.78, f32[768]{0:T(1024)S(1)} %copy-done.88, f32[2048,768]{0,1:T(8,128)} %all-reduce.34.cloned.1.call-done, bf16[768,256]{1,0:T(8,128)(2,1)S(1)} %copy-done.44, ...), kind=kOutput, calls=%fused_computation.35 | convolution fusion | flops 4844942336 | bytes 21387264 | tf_op jit(solution)/shard_map/dot_general | solution.py:45
  710.1 4.0 fusion.17
  714.1 6.6 copy.363
  720.8 26.3 %all-reduce.26 = (f32[768]{0:T(1024)}, f32[768,6]{0,1:T(8,128)}, f32[4,384]{1,0:T(4,128)}, f32[384]{0:T(512)}, f32[4,256]{1,0:T(4,128)}, /*index=5*/f32[256]{0:T...) all-reduce(f32[768]{0:T(1024)S(1)} %get-tuple-element.345, ...), channel_id=1, replica_groups=mesh['seq'=8,'head'=4] {'seq'}, use_global_device_ids=true, to_apply=%region_33.34 | all-reduce | flops 8978 | bytes 71824 | tf_op jit(solution)/shard_map/psum | solution.py:235
  747.0 42.0 %all-reduce.36.cloned.1.call-done = (f32[768,384]{1,0:T(8,128)}, f32[768,384]{1,0:T(8,128)}, f32[768,256]{1,0:T(8,128)}, f32[384,768]{1,0:T(8,128)}) async-done(((f32[768,384]{1,0:T(8,128)}, f32[768,384]{1,0:T(8,128)}, f32[768,256]{1,0:T(8,128)}, f32[384,768]{1,0:T(8,128)}), (f32[768,384]{1,0:T(8,128)}, f32[768,384]{1,0:T(8,128)}, f32[768,256]{1,0:T(8,128)}, ...) | async-done | bytes 4325392 | tf_op jit(solution)/shard_map/psum | solution.py:235
  (455 shorter events, 139.4 us)
Async XLA Ops:
  7.2 130.3 %copy-start = (bf16[768,384]{1,0:T(8,128)(2,1)S(1)}, bf16[768,384]{1,0:T(8,128)(2,1)}, u32[]{:S(2)}) copy-start(bf16[768,384]{1,0:T(8,128)(2,1)} %param.22) | copy-start | bytes 1769476
  7.2 91.4 %all-gather.5.cloned.1.call-start = ((), (), s32[]{:S(2)}) async-start(), calls=%async_computation.1 | async-start | bytes 1769472 | tf_op jit(solution)/shard_map/all_gather | solution.py:23
  19.8 15.1 %copy-start.124 = (f32[4,256]{1,0:T(4,128)S(1)}, f32[4,256]{1,0:T(4,128)}, u32[]{:S(2)}) copy-start(f32[4,256]{1,0:T(4,128)} %param.28) | copy-start | bytes 12292
  19.8 16.6 %collective-permute-start = (f32[3,640]{0,1:T(8,128)S(1)}, f32[3,640]{0,1:T(8,128)S(1)}, u32[]{:S(2)}, u32[]{:S(2)}) collective-permute-start(f32[3,640]{0,1:T(8,128)S(1)} %fusion.80), channel_id=1, source_target_pairs={{0,4},{4,8},{8,12},{12,16},{16,20},{20,24},{24,28},{1,5},{5,9},{9,... | collective-permute-start | bytes 23048 | tf_op jit(solution)/shard_map/ppermute | solution.py:18
  24.0 8.4 %copy-start.51 = (f32[2048,6]{0,1:T(8,128)}, f32[2048,6]{0,1:T(8,128)S(1)}, u32[]{:S(2)}) copy-start(f32[2048,6]{0,1:T(8,128)S(1)} %get-tuple-element.453) | copy-start | bytes 147460
  57.2 10.0 %copy-start.141 = (u32[32]{0:T(128)S(1)}, u32[32]{0:T(128)}, u32[]{:S(2)}) copy-start(u32[32]{0:T(128)} %constant.153) | copy-start | bytes 388
  57.3 11.3 %copy-start.137 = (f32[6]{0:T(128)S(1)}, f32[6]{0:T(128)}, u32[]{:S(2)}) copy-start(f32[6]{0:T(128)} %get-tuple-element.364) | copy-start | bytes 76
  65.3 94.1 %all-gather.7.cloned.1.call-start = ((), (), s32[]{:S(2)}) async-start(), calls=%async_computation.3 | async-start | bytes 3932160 | tf_op jit(solution)/shard_map/all_gather | solution.py:175
  66.0 164.1 %all-gather.9.cloned.1.call-start = ((), (), s32[]{:S(2)}) async-start(), calls=%async_computation.4 | async-start | bytes 1769472 | tf_op jit(solution)/shard_map/all_gather | solution.py:23
  94.0 12.2 %copy-start.122 = (f32[6]{0:T(128)S(1)}, f32[6]{0:T(128)}, u32[]{:S(2)}) copy-start(f32[6]{0:T(128)} %copy-done.121) | copy-start | bytes 76
  106.2 9.6 %copy-start.27 = (f32[8,256,128,1]{2,1,3,0:T(8,128)S(1)}, f32[8,256,128,1]{2,1,3,0:T(8,128)}, u32[]{:S(2)}) copy-start(f32[8,256,128,1]{2,1,3,0:T(8,128)} %copy.365) | copy-start | bytes 3145732
  109.4 9.2 %copy-start.39 = (f32[6,64,128]{2,1,0:T(8,128)}, f32[6,64,128]{2,1,0:T(8,128)S(1)}, u32[]{:S(2)}) copy-start(f32[6,64,128]{2,1,0:T(8,128)S(1)} %get-tuple-element.427) | copy-start | bytes 589828
  118.6 15.6 %copy-start.22 = (f32[8,256,6,64]{1,3,2,0:T(8,128)}, f32[8,256,6,64]{1,3,2,0:T(8,128)S(1)}, u32[]{:S(2)}) copy-start(f32[8,256,6,64]{1,3,2,0:T(8,128)S(1)} %fusion.123) | copy-start | bytes 9437188
  137.9 21.5 %copy-start.97 = (f32[384]{0:T(512)S(1)}, f32[384]{0:T(512)}, u32[]{:S(2)}) copy-start(f32[384]{0:T(512)} %param.33) | copy-start | bytes 4612
  192.9 170.0 %all-reduce.32.cloned.1.call-start = ((), (), s32[]{:S(2)}) async-start(), calls=%async_computation.5 | async-start | bytes 4194304 | tf_op jit(solution)/shard_map/psum | solution.py:206
  194.0 8.5 %copy-start.10 = (f32[48,8,8,256]{3,2,1,0:T(8,128)S(1)}, f32[48,8,8,256]{3,2,1,0:T(8,128)}, u32[]{:S(2)}) copy-start(f32[48,8,8,256]{3,2,1,0:T(8,128)} %copy-done.9) | copy-start | bytes 9437188
  194.0 8.5 %copy-start.17 = (f32[48,8,8,256]{3,2,1,0:T(8,128)S(1)}, f32[48,8,8,256]{3,2,1,0:T(8,128)}, u32[]{:S(2)}) copy-start(f32[48,8,8,256]{3,2,1,0:T(8,128)} %copy.395) | copy-start | bytes 9437188
  194.0 8.5 %copy-start.68 = (f32[8,6,256]{2,1,0:T(8,128)S(1)}, f32[8,6,256]{2,1,0:T(8,128)}, u32[]{:S(2)}) copy-start(f32[8,6,256]{2,1,0:T(8,128)} %copy-done.66) | copy-start | bytes 147460
  194.0 8.5 %copy-start.83 = (pred[256,256]{1,0:T(8,128)(4,1)S(1)}, pred[256,256]{1,0:T(8,128)(4,1)}, u32[]{:S(2)}) copy-start(pred[256,256]{1,0:T(8,128)(4,1)} %iota_compare_fusion) | copy-start | bytes 196612
  202.5 22.1 %copy-start.26 = (f32[8,256,128]{2,1,0:T(8,128)S(1)}, f32[8,256,128]{2,1,0:T(8,128)}, u32[]{:S(2)}) copy-start(f32[8,256,128]{2,1,0:T(8,128)} %copy.310) | copy-start | bytes 3145732
  248.8 7.6 copy-start.112
  248.8 9.3 %copy-start.104 = (f32[6]{0:T(128)S(1)}, f32[6]{0:T(128)}, u32[]{:S(2)}) copy-start(f32[6]{0:T(128)} %get-tuple-element.357) | copy-start | bytes 76
  248.8 9.3 %copy-start.109 = (f32[6]{0:T(128)S(1)}, f32[6]{0:T(128)}, u32[]{:S(2)}) copy-start(f32[6]{0:T(128)} %get-tuple-element.358) | copy-start | bytes 76
  248.8 12.2 %copy-start.18 = (f32[48,8,8,256]{3,2,1,0:T(8,128)S(1)}, f32[48,8,8,256]{3,2,1,0:T(8,128)}, u32[]{:S(2)}) copy-start(f32[48,8,8,256]{3,2,1,0:T(8,128)} %copy.395) | copy-start | bytes 9437188
  248.9 12.2 %copy-start.73 = (f32[8,256,6]{1,2,0:T(8,128)S(1)}, f32[8,256,6]{1,2,0:T(8,128)}, u32[]{:S(2)}) copy-start(f32[8,256,6]{1,2,0:T(8,128)} %get-tuple-element.455) | copy-start | bytes 147460
  250.9 16.2 %copy-start.62 = (f32[6,64,128]{2,1,0:T(8,128)}, f32[6,64,128]{2,1,0:T(8,128)S(1)}, u32[]{:S(2)}) copy-start(f32[6,64,128]{2,1,0:T(8,128)S(1)} %get-tuple-element.408) | copy-start | bytes 589828
  252.7 14.4 %copy-start.56 = (f32[6,64,128]{2,1,0:T(8,128)}, f32[6,64,128]{2,1,0:T(8,128)S(1)}, u32[]{:S(2)}) copy-start(f32[6,64,128]{2,1,0:T(8,128)S(1)} %get-tuple-element.410) | copy-start | bytes 589828
  254.5 12.6 %copy-start.58 = (f32[6,64,128]{2,1,0:T(8,128)}, f32[6,64,128]{2,1,0:T(8,128)S(1)}, u32[]{:S(2)}) copy-start(f32[6,64,128]{2,1,0:T(8,128)S(1)} %get-tuple-element.412) | copy-start | bytes 589828
  256.4 10.7 %copy-start.60 = (f32[6,64,128]{2,1,0:T(8,128)}, f32[6,64,128]{2,1,0:T(8,128)S(1)}, u32[]{:S(2)}) copy-start(f32[6,64,128]{2,1,0:T(8,128)S(1)} %get-tuple-element.414) | copy-start | bytes 589828
  258.1 9.0 %copy-start.54 = (f32[6,64,128]{2,1,0:T(8,128)}, f32[6,64,128]{2,1,0:T(8,128)S(1)}, u32[]{:S(2)}) copy-start(f32[6,64,128]{2,1,0:T(8,128)S(1)} %get-tuple-element.416) | copy-start | bytes 589828
  277.4 198.1 %reduce-scatter.2.cloned.1.call-start = ((), (), s32[]{:S(2)}) async-start(), calls=%async_computation.2 | async-start | bytes 7864320 | tf_op jit(solution)/shard_map/reduce_scatter | solution.py:166
  284.1 417.1 %all-reduce.34.cloned.1.call-start = ((), (), s32[]{:S(2)}) async-start(), calls=%async_computation.6 | async-start | bytes 12582912 | tf_op jit(solution)/shard_map/psum | solution.py:228
  296.7 13.0 %copy-start.34 = (f32[8,256,6,64]{1,3,2,0:T(8,128)}, f32[8,256,6,64]{1,3,2,0:T(8,128)S(1)}, u32[]{:S(2)}) copy-start(f32[8,256,6,64]{1,3,2,0:T(8,128)S(1)} %fusion.81) | copy-start | bytes 9437188
  315.4 20.9 %copy-start.52 = (f32[2048,6]{0,1:T(8,128)S(1)}, f32[2048,6]{0,1:T(8,128)}, u32[]{:S(2)}) copy-start(f32[2048,6]{0,1:T(8,128)} %copy-done.51) | copy-start | bytes 147460
  315.5 20.9 %copy-start.70 = (f32[2048,6]{0,1:T(8,128)S(1)}, f32[2048,6]{0,1:T(8,128)}, u32[]{:S(2)}) copy-start(f32[2048,6]{0,1:T(8,128)} %get-tuple-element.462) | copy-start | bytes 147460
  315.5 20.9 %copy-start.135 = (f32[6]{0:T(128)S(1)}, f32[6]{0:T(128)}, u32[]{:S(2)}) copy-start(f32[6]{0:T(128)} %get-tuple-element.460) | copy-start | bytes 76
  366.2 14.9 %copy-start.90 = (f32[640]{0:T(1024)S(1)}, f32[640]{0:T(1024)}, u32[]{:S(2)}) copy-start(f32[640]{0:T(1024)} %copy-done.89) | copy-start | bytes 7684
  366.2 14.9 %copy-start.92 = (f32[640]{0:T(1024)S(1)}, f32[640]{0:T(1024)}, u32[]{:S(2)}) copy-start(f32[640]{0:T(1024)} %copy-done.91) | copy-start | bytes 7684
  366.2 14.9 %copy-start.94 = (f32[640]{0:T(1024)S(1)}, f32[640]{0:T(1024)}, u32[]{:S(2)}) copy-start(f32[640]{0:T(1024)} %copy-done.93) | copy-start | bytes 7684
  384.8 11.9 %collective-permute-start.1 = (f32[3,640]{0,1:T(8,128)S(1)}, f32[3,640]{0,1:T(8,128)S(1)}, u32[]{:S(2)}, u32[]{:S(2)}) collective-permute-start(f32[3,640]{0,1:T(8,128)S(1)} %pad_add_fusion.2), channel_id=1, source_target_pairs={{4,0},{8,4},{12,8},{16,12},{20,16},{24,20},{28,24},{5,1},{9,5},{13... | collective-permute-start | bytes 23048 | tf_op jit(solution)/shard_map/ppermute | solution.py:18
  408.3 380.7 %all-reduce.36.cloned.1.call-start = ((), (), s32[]{:S(2)}) async-start(), calls=%async_computation.7 | async-start | bytes 8650752 | tf_op jit(solution)/shard_map/psum | solution.py:235
  414.2 10.1 %slice-start = ((s8[5242880]{0:T(1024)(128)(4,1)}), s8[4194304]{0:T(1024)(128)(4,1)S(1)}, s32[]{:S(2)}) async-start(s8[5242880]{0:T(1024)(128)(4,1)} %bitcast.261), calls=%async_computation.8 | async-start | bytes 8388608
  430.8 270.4 %copy-start.44 = (bf16[768,256]{1,0:T(8,128)(2,1)S(1)}, bf16[768,256]{1,0:T(8,128)(2,1)}, u32[]{:S(2)}) copy-start(bf16[768,256]{1,0:T(8,128)(2,1)} %param.24) | copy-start | bytes 1179652
  430.8 270.4 %copy-start.78 = (f32[2048]{0:T(1024)S(1)}, f32[2048]{0:T(1024)}, u32[]{:S(2)}) copy-start(f32[2048]{0:T(1024)} %copy-done.77) | copy-start | bytes 24580
  430.8 270.4 %copy-start.88 = (f32[768]{0:T(1024)S(1)}, f32[768]{0:T(1024)}, u32[]{:S(2)}) copy-start(f32[768]{0:T(1024)} %param.21) | copy-start | bytes 9220
  478.4 231.8 %copy-start.95 = (f32[2048]{0:T(1024)S(1)}, f32[2048]{0:T(1024)}, u32[]{:S(2)}) copy-start(f32[2048]{0:T(1024)} %get-tuple-element.456) | copy-start | bytes 24580
  701.2 9.0 %copy-start.7 = (bf16[2048,768]{0,1:T(8,128)(2,1)S(1)}, bf16[2048,768]{0,1:T(8,128)(2,1)}, u32[]{:S(2)}) copy-start(bf16[2048,768]{0,1:T(8,128)(2,1)} %copy.308) | copy-start | bytes 9437188
  701.2 9.0 %copy-start.36 = (bf16[2048,768]{0,1:T(8,128)(2,1)S(1)}, bf16[2048,768]{0,1:T(8,128)(2,1)}, u32[]{:S(2)}) copy-start(bf16[2048,768]{0,1:T(8,128)(2,1)} %all-gather.7.cloned.1.call-done) | copy-start | bytes 9437188
  (106 other events, 462.2 us)
Sparse Core Ops, SparseCore 0:
  65.4 28.2 all-gather.4
  95.3 64.0 all-gather.6
  193.1 24.6 all-gather.8
  277.5 85.4 all-reduce.31
  365.8 109.5 reduce-scatter.1
  477.8 223.3 all-reduce.33
  706.4 82.5 all-reduce.35
where the time goes:
time: 807 us; the launch traced here: 802 us
  waiting for transfers between devices  332 us (41%)
  matrix products  158 us (20%)
  other arithmetic  136 us (17%)
  local copies, waits for them, and re-layouts  91 us (11%)
  blocking collectives  62.8 us (8%)
  between operations  16.9 us (2%)
    psum x1, waiting for transfers between devices, per_device(): grad_normed = lax.psum(partial_grad + spread_term, 'head') + bc_term  223 us
    dot_general x3, matrix products, group_out(): output = jnp.einsum('kijh,kjhp->kihp', mixing, inner3, precision=HIGH)  50.5 us
    unnamed x309, local copies, waits for them, and re-layouts  47.1 us
    reduce_scatter x1, waiting for transfers between devices, per_device(): lax.psum_scatter(jnp.dot(normed_out, w_out, preferred_element_type=jnp.fl...  44.6 us
    psum x1, waiting for transfers between devices, per_device(): lax.psum((grad_gain_in, grad_w_gate, grad_w_inner, grad_w_bc, grad_w_step...  42 us
    dot_general x6, matrix products, contract(): lax.dot_general(left, right, (((left_dim,), (right_dim,)), ((), ())), pre...  30.7 us
    psum x1, blocking collectives, per_device(): lax.psum((grad_gain_in, grad_w_gate, grad_w_inner, grad_w_bc, grad_w_step...  26.3 us
    another operation x6, other arithmetic  21.4 us
  transfers between devices with their start and end apart: 9, of which 5 were waited for; matrix products, arithmetic and copies ran while one was open for 33% of the time, Pallas kernels for 0%

commit v1 on v0

v1 whole, which is shorter than its diff:
```python
import functools
import jax
import jax.numpy as jnp
from jax import lax
from jax.experimental import pallas as pl
from jax.experimental.pallas import tpu as pltpu
from jax.sharding import PartitionSpec as P

BLOCK = 256
LANES = 128
EDGE = 16
F32, BF16 = jnp.float32, jnp.bfloat16
eps = 1e-05


def turn(block, axis, distance):
    count = lax.axis_size(axis)
    return lax.ppermute(block, axis, [(i, (i + distance) % count) for i in range(count)])


def shifted(block, axis, distance):
    devices = range(lax.axis_size(axis))
    return lax.ppermute(block, axis, [(i - distance, i) for i in devices if i - distance in devices])


def ring_gather(block, axis):
    pieces = [block]
    for _ in range(lax.axis_size(axis) - 1):
        pieces.append(turn(pieces[-1], axis, 1))
    return pieces


def ring_scatter(parts, axis):
    count, mine = lax.axis_size(axis), lax.axis_index(axis)
    total = parts((mine - 1) % count)
    for step in range(count - 1):
        arrived = turn(total, axis, 1)
        own = parts((mine - 2 - step) % count)
        total = arrived.astype(F32) + own.astype(F32)
        if step < count - 2:
            total = total.astype(BF16)
    return total


def small_sum(value, axis):
    total = value
    for step in range(1, lax.axis_size(axis)):
        total = total + turn(value, axis, step)
    return total


def butterfly(value, axis):
    count, reach = lax.axis_size(axis), 1
    while reach < count:
        value = value + lax.ppermute(value, axis, [(i, i ^ reach) for i in range(count)])
        reach *= 2
    return value


def joined_states(payload, axis, width, heads, backward):
    count, mine = lax.axis_size(axis), lax.axis_index(axis)
    pieces = [lax.all_gather(part, axis).astype(F32) for part in payload]
    pieces = pieces[0] + pieces[1]
    logs = pieces[:, width, :heads]
    states = pieces[:, :width]
    place = jnp.arange(count)
    k, m = place[:, None], place[None, :]
    if backward:
        between, counted = (m > mine) & (m < k), place > mine
    else:
        between, counted = (m > k) & (m < mine), place < mine
    passed = jnp.sum(jnp.where(between[:, :, None], logs[None], 0.0), 1)
    weight = jnp.where(counted[:, None], jnp.exp(passed), 0.0)
    weight = jnp.repeat(weight, width // heads, 1)
    return jnp.sum(weight[:, :, None] * states, 0)


def dot(left, right, left_dim=1, right_dim=0, precision=None):
    return lax.dot_general(
        left, right, (((left_dim,), (right_dim,)), ((), ())), precision=precision, preferred_element_type=F32
    )


def silu(value):
    return value * jax.nn.sigmoid(value)


def silu_slope(value):
    s = jax.nn.sigmoid(value)
    return s * (1.0 + value * (1.0 - s))


def halves(value):
    coarse = value.astype(BF16)
    return coarse, (value - coarse.astype(F32)).astype(BF16)


def dot_left(left, right, left_dim=1, right_dim=0):
    coarse, fine = halves(left)
    return dot(coarse, right, left_dim, right_dim) + dot(fine, right, left_dim, right_dim)


def dot_right(left, right, left_dim=1, right_dim=0):
    coarse, fine = halves(right)
    return dot(left, coarse, left_dim, right_dim) + dot(left, fine, left_dim, right_dim)


def dot_both(left, right, left_dim=1, right_dim=0):
    coarse, fine = halves(left)
    return dot_right(coarse, right, left_dim, right_dim) + dot(fine, right.astype(BF16), left_dim, right_dim)


def steps(raw, step_bias):
    moved = raw + step_bias
    return moved, jnp.maximum(moved, 0.0) + jnp.log1p(jnp.exp(-jnp.abs(moved)))


def widen(value, spread):
    return dot_left(value, spread)


def narrow(value, spread):
    return dot_left(value, spread, 1, 1)


def state_decay(last, spread):
    return dot_right(spread, jnp.broadcast_to(jnp.exp(last), (LANES, LANES)).T, 0, 0)


def as_columns(rows, width):
    return dot_left(rows, jnp.full((rows.shape[0], width), 1.0 / rows.shape[0], BF16), 0, 0)


def as_rows(value):
    return dot_right(jnp.ones((8, value.shape[1]), BF16), value, 1, 1)


def row_sum(value):
    return jnp.sum(value, 0, keepdims=True)


def forward_kernel(
    x, halo, gain, w_gate, w_inner, w_bc, w_step, taps, bias, step_bias, decay_log, lower, spread,
    normed_o, gate_o, pre_o, tot_o, raw_o, cum_o, cum_rows_o, local_o, payload_o,
    before, state, passed,
):
    here, length, width = pl.program_id(0), x.shape[0], w_gate.shape[1]

    def norm(rows):
        rows = rows.astype(F32)
        return (rows * lax.rsqrt(jnp.mean(rows * rows, -1, keepdims=True) + eps) * gain[...]).astype(BF16)

    @pl.when(here == 0)
    def _():
        edge = norm(halo[...])
        before[:, :width] = dot(edge, w_inner[...])[EDGE - 8 :]
        before[:, width:] = dot(edge, w_bc[...])[EDGE - 8 :]
        state[...] = jnp.zeros_like(state)
        passed[...] = jnp.zeros_like(passed)

    normed = norm(x[...])
    normed_o[...] = normed
    gate_o[...] = dot(normed, w_gate[...])
    pre = jnp.concatenate([dot(normed, w_inner[...]), dot(normed, w_bc[...])], 1)
    pre_o[...] = pre
    raw = dot(normed, w_step[...])
    raw_o[...] = raw
    padded = jnp.concatenate([before[...], pre], 0)
    kernel = taps.shape[0]
    first = 8 - (kernel - 1)
    total = bias[...] + sum(taps[k : k + 1, :] * padded[first + k : first + k + length] for k in range(kernel))
    before[...] = pre[length - 8 :]
    tot_o[...] = total
    inner = silu(total[:, :width])
    keys = silu(total[:, width : width + LANES]).astype(BF16)
    _, step = steps(raw, step_bias[...])
    rate = -jnp.exp(decay_log[...]) * step
    cum = dot_right(lower[...], rate)
    cum_o[...] = cum
    cum_rows_o[0] = cum.T[:8]
    last = cum[length - 1 : length]
    tail = widen(jnp.exp(last - cum) * step, spread[...])
    local = dot((tail * inner).astype(BF16), keys, 0, 0)
    local_o[0] = local
    state[...] = state_decay(last, spread[...]) * state[...] + local
    passed[...] = passed[...] + last
    write_payload(payload_o, state, passed)


def write_payload(payload_o, state, passed):
    width = state.shape[0]

    @pl.when(pl.program_id(0) == pl.num_programs(0) - 1)
    def _():
        coarse, fine = halves(state[...])
        payload_o[0, :width] = coarse
        payload_o[1, :width] = fine
        coarse, fine = halves(passed[...])
        payload_o[0, width:] = coarse
        payload_o[1, width:] = fine


def state_kernel(
    tot, raw, cum_in, cum_rows, gate, local, incoming, step_bias, skip, hide, spread,
    ssd_o, start_o, squares_o,
    state,
):
    width = gate.shape[1]

    @pl.when(pl.program_id(0) == 0)
    def _():
        state[...] = incoming[...]

    inner = silu(tot[:, :width])
    keys = silu(tot[:, width : width + LANES]).astype(BF16)
    queries = silu(tot[:, width + LANES :])
    _, step = steps(raw[...], step_bias[...])
    cum = cum_in[...]
    start = state[...]
    start_o[0] = start
    state[...] = state_decay(cum[cum.shape[0] - 1 :], spread[...]) * start + local[0]
    scores = dot_left(queries, keys, 1, 1)
    fed = (inner * widen(step, spread[...])).astype(BF16)
    carried = widen(jnp.exp(cum), spread[...]) * dot_both(queries, start, 1, 1)
    head_dim = width // HEADS_OF(width)
    outs = []
    for begin in range(0, width, LANES):
        size = min(LANES, width - begin)
        pair = fed[:, begin : begin + size]
        lane = lax.broadcasted_iota(jnp.int32, (1, size), 1)
        out = None
        for half in range(size // head_dim):
            h = begin // head_dim + half
            decay = jnp.exp(cum[:, h : h + 1] - cum_rows[0, h : h + 1, :] + hide[...])
            part = dot((scores * decay).astype(BF16), pair)
            out = part if out is None else jnp.where(lane < half * head_dim, out, part)
        outs.append(out)
    ssd = jnp.concatenate(outs, 1) + carried + skip[...] * inner
    ssd_o[...] = ssd
    mixed = ssd * silu(gate[...])
    squares_o[0] = as_rows(mixed * mixed)


HEAD_DIM = 64


def HEADS_OF(width):
    return width // HEAD_DIM


def scale_of(squares, width, all_width):
    return lax.rsqrt(as_columns(squares, width) / all_width + eps)


def out_kernel(all_width, ssd, gate, squares, gain, w_out, normed_o, part_o):
    width = ssd.shape[1]
    mixed = ssd[...] * silu(gate[...])
    normed = (mixed * scale_of(squares[0], width, all_width) * gain[...]).astype(BF16)
    normed_o[...] = normed
    for piece in range(w_out.shape[0]):
        part_o[piece] = dot(normed, w_out[piece]).astype(BF16)


def cross_kernel(pieces, *refs):
    grads, (w_out, ssd, gate, gain, dn_o, cross_o) = refs[:pieces], refs[pieces:]
    dn = sum(dot(grads[p][...], w_out[p], 1, 1) for p in range(pieces))
    dn_o[...] = dn
    cross_o[0] = as_rows(dn * gain[...] * (ssd[...] * silu(gate[...])))


def gate_kernel(pieces, all_width, *refs):
    grads = refs[:pieces]
    (
        ssd, gate, dn, tot, cum_in, normed, normed_out, squares, cross, gain, spread,
        dssd_o, dgate_o, local_o, payload_o, gw_out_o, gw_gate_o, sums_o,
        state, passed,
    ) = refs[pieces:]
    width, length = ssd.shape[1], ssd.shape[0]

    @pl.when(pl.program_id(0) == 0)
    def _():
        state[...] = jnp.zeros_like(state)
        passed[...] = jnp.zeros_like(passed)
        gw_out_o[...] = jnp.zeros_like(gw_out_o)
        gw_gate_o[...] = jnp.zeros_like(gw_gate_o)
        sums_o[...] = jnp.zeros_like(sums_o)

    g = gate[...]
    s = jax.nn.sigmoid(g)
    act = g * s
    mixed = ssd[...] * act
    scale = scale_of(squares[0], width, all_width)
    dscaled = dn[...] * scale
    along = as_columns(cross[0] / (squares[0] + all_width * eps), width)
    dmixed = scale * (dn[...] * gain[...] - mixed * along)
    dssd = dmixed * act
    dssd_o[...] = dssd
    dgate = (dmixed * ssd[...] * s * (1.0 + g * (1.0 - s))).astype(BF16)
    dgate_o[...] = dgate
    inner = silu(tot[:, :width])
    queries = silu(tot[:, width + LANES :])
    sums_o[0:1] = sums_o[0:1] + row_sum(dscaled * mixed)
    sums_o[1:2] = sums_o[1:2] + row_sum(dssd * inner)
    cum = cum_in[...]
    local = dot_both(widen(jnp.exp(cum), spread[...]) * dssd, queries, 0, 0)
    local_o[0] = local
    state[...] = state_decay(cum[length - 1 :], spread[...]) * state[...] + local
    passed[...] = passed[...] + cum[length - 1 :]
    for p in range(pieces):
        gw_out_o[p] = gw_out_o[p] + dot(normed_out[...], grads[p][...], 0, 0)
    gw_gate_o[...] = gw_gate_o[...] + dot(normed[...], dgate, 0, 0)
    write_payload(payload_o, state, passed)


def pull_kernel(
    tot, raw, cum_in, cum_rows, dssd, start, local, outgoing, step_bias, decay_log, skip, lower, hide, spread,
    d_o, draw_o, sums_o,
    state,
):
    width, length = dssd.shape[1], dssd.shape[0]

    @pl.when(pl.program_id(0) == 0)
    def _():
        state[...] = outgoing[...]
        sums_o[...] = jnp.zeros_like(sums_o)

    inner = silu(tot[:, :width])
    keys = silu(tot[:, width : width + LANES]).astype(BF16)
    queries = silu(tot[:, width + LANES :])
    shifted_raw, step = steps(raw[...], step_bias[...])
    rate = -jnp.exp(decay_log[...]) * step
    cum = cum_in[...]
    last = cum[length - 1 : length]
    ending = state[...]
    state[...] = state_decay(last, spread[...]) * ending + local[0]
    beginning = start[0]
    dy = dssd[...]
    dy16, dy_fine = halves(dy)
    ecum = jnp.exp(cum)
    tail = jnp.exp(last - cum)
    step_w = widen(step, spread[...])
    ecum_w = widen(ecum, spread[...])
    tail_w = widen(tail * step, spread[...])
    read = dot(queries.astype(BF16), beginning.astype(BF16), 1, 1)
    dqueries = dot_both(ecum_w * dy, beginning)
    taken = dot(keys, ending.astype(BF16), 1, 1)
    dkeys = dot_both(tail_w * inner, ending)
    from_start = ecum * narrow(dy * read, spread[...])
    to_end = tail * narrow(inner * taken, spread[...])
    both = as_rows(ending * beginning)
    through = jnp.exp(last) * narrow(both, spread[...])[0:1]
    scores = dot_left(queries, keys, 1, 1)
    fed, fed_fine = halves(inner * step_w)
    dscores = jnp.zeros_like(scores)
    crossing = jnp.zeros((length, LANES), F32)
    pulls, downs = [], []
    lanes_all = lax.broadcasted_iota(jnp.int32, (length, LANES), 1)
    for begin in range(0, width, LANES):
        size = min(LANES, width - begin)
        fed_pair, fed_low, dy_pair, dy_low = (v[:, begin : begin + size] for v in (fed, fed_fine, dy16, dy_fine))
        lane = lax.broadcasted_iota(jnp.int32, (1, size), 1)
        rows = []
        for half in range(size // HEAD_DIM):
            h = begin // HEAD_DIM + half
            inside = (lane >= half * HEAD_DIM) & (lane < (half + 1) * HEAD_DIM)
            fed_head = jnp.where(inside, fed_pair, jnp.zeros_like(fed_pair))
            low_head = jnp.where(inside, fed_low, jnp.zeros_like(fed_low))
            decay = jnp.exp(cum[:, h : h + 1] - cum_rows[0, h : h + 1, :] + hide[...])
            dweight = dot(dy_pair, fed_head, 1, 1) + dot(dy_low, fed_head, 1, 1) + dot(dy_pair, low_head, 1, 1)
            dweight = dweight * decay
            dscores = dscores + dweight
            weight = (scores * decay).astype(BF16)
            pulled = dot(dy_pair, weight, 0, 0)
            rows.append(pulled[half * HEAD_DIM : (half + 1) * HEAD_DIM])
            pair_terms = dweight * scores
            right = jnp.sum(pair_terms, 1, keepdims=True)
            downs.append(jnp.sum(pair_terms, 0, keepdims=True))
            crossing = jnp.where(lanes_all == h, right, crossing)
        pulls.append(jnp.concatenate(rows, 0).T)
    pulled = jnp.concatenate(pulls, 1)
    downs.append(jnp.zeros((LANES - len(downs), length), F32))
    crossing = crossing - jnp.concatenate(downs, 0).T
    coarse, fine = halves(dscores)
    dqueries = dqueries + dot(coarse, keys) + dot(fine, keys)
    dkeys = dkeys + (dot_left(queries, coarse, 0, 0) + dot(queries.astype(BF16), fine, 0, 0)).T
    dinner = (tail_w * taken + step_w * pulled) + skip[...] * dy
    dstep = narrow(inner * pulled, spread[...]) + to_end
    given = to_end * step
    drate = dot_right(lower[...], crossing + from_start, 0, 0) + (dot_right(lower[...], given) - given)
    drate = drate + through
    dstep = dstep - jnp.exp(decay_log[...]) * drate
    draw = dstep * jax.nn.sigmoid(shifted_raw)
    draw_o[...] = draw
    sums_o[0:1] = sums_o[0:1] + row_sum(draw)
    sums_o[1:2] = sums_o[1:2] + row_sum(rate * drate)
    d_o[:, :width] = dinner * silu_slope(tot[:, :width])
    d_o[:, width : width + LANES] = dkeys * silu_slope(tot[:, width : width + LANES])
    d_o[:, width + LANES :] = dqueries * silu_slope(tot[:, width + LANES :])


def project_kernel(
    d, halo, pre, normed, dgate, draw, taps, w_gate, w_inner, w_bc, w_step,
    part_o, gw_inner_o, gw_bc_o, gw_step_o, sums_o,
    after,
):
    width, length = w_gate.shape[1], d.shape[0]

    @pl.when(pl.program_id(0) == 0)
    def _():
        after[...] = halo[...]
        for out in (gw_inner_o, gw_bc_o, gw_step_o, sums_o):
            out[...] = jnp.zeros_like(out)

    kernel = taps.shape[0]
    grads = d[...]
    padded = jnp.concatenate([grads, after[...]], 0)
    after[...] = grads[:8]
    dpre = jnp.zeros_like(grads)
    for k in range(kernel):
        moved = padded[kernel - 1 - k : kernel - 1 - k + length]
        dpre = dpre + taps[k : k + 1, :] * moved
        sums_o[k : k + 1] = sums_o[k : k + 1] + row_sum(pre[...] * moved)
    sums_o[kernel : kernel + 1] = sums_o[kernel : kernel + 1] + row_sum(grads)
    dinner, dbc, dstep = dpre[:, :width].astype(BF16), dpre[:, width:], draw[...].astype(BF16)
    part = dot(dgate[...], w_gate[...], 1, 1) + dot(dinner, w_inner[...], 1, 1)
    part = part + dot_left(dbc, w_bc[...], 1, 1) + dot(dstep, w_step[...], 1, 1)
    part_o[...] = part.astype(BF16)
    gw_inner_o[...] = gw_inner_o[...] + dot(normed[...], dinner, 0, 0)
    gw_bc_o[...] = gw_bc_o[...] + dot_right(normed[...], dbc, 0, 0)
    gw_step_o[...] = gw_step_o[...] + dot(normed[...], dstep, 0, 0)


def call(kernel, blocks, ins, outs, scratch=(), backward=False, flops=10**9):
    def spec(shape, kind):
        def at(i):
            return blocks - 1 - i if backward else i

        if kind == "rows":
            return pl.BlockSpec((shape[0] // blocks,) + shape[1:], lambda i: (at(i), 0))
        if kind == "stack":
            return pl.BlockSpec((1,) + shape[1:], lambda i: (at(i), 0, 0))
        if kind == "mid":
            return pl.BlockSpec((shape[0], shape[1] // blocks, shape[2]), lambda i: (0, at(i), 0))
        return pl.BlockSpec(shape, lambda i: (0,) * len(shape))

    moved = sum(a.size * a.dtype.itemsize for a, _ in ins)
    return pl.pallas_call(
        kernel,
        grid=(blocks,),
        in_specs=[spec(a.shape, kind) for a, kind in ins],
        out_specs=[spec(shape, kind) for shape, _, kind in outs],
        out_shape=[jax.ShapeDtypeStruct(shape, dtype) for shape, dtype, _ in outs],
        scratch_shapes=[pltpu.VMEM(shape, F32) for shape in scratch],
        compiler_params=pltpu.CompilerParams(
            dimension_semantics=("arbitrary",), vmem_limit_bytes=48 * 1024 * 1024
        ),
        cost_estimate=pl.CostEstimate(flops=flops, bytes_accessed=moved, transcendentals=0),
    )(*[a for a, _ in ins])


def per_device(
    layer_input, gain_in, w_gate, w_inner, w_bc, w_step, conv_inner, conv_inner_bias, conv_bc, conv_bc_bias,
    step_bias, decay_log, skip_gain, gain_out, w_out, output_grad,
):
    count, features = layer_input.shape
    heads, width = decay_log.shape[0], w_gate.shape[1]
    states = w_bc.shape[1] // 2
    both = width + 2 * states
    blocks = count // BLOCK
    kernel = conv_inner.shape[0]
    pieces, mine = lax.axis_size("head"), lax.axis_index("head")
    all_width = width * pieces
    piece = output_grad.shape[1]
    rows = count // pieces
    heads_pad = ((0, 0), (0, LANES - heads))

    place = jnp.arange(BLOCK)
    keep = place[:, None] >= place[None, :]
    lower = keep.astype(BF16)
    hide = jnp.where(keep, 0.0, -1e30).astype(F32)
    spread = (jnp.arange(LANES)[:, None] == (jnp.arange(width) // (width // heads))[None, :]).astype(BF16)
    w_step_pad = jnp.pad(w_step, heads_pad)
    step_bias_pad = jnp.pad(step_bias[None], heads_pad)
    decay_pad = jnp.pad(decay_log[None], heads_pad)
    taps = jnp.concatenate([conv_inner, conv_bc], 1)
    bias = jnp.concatenate([conv_inner_bias, conv_bc_bias], 0)[None]
    skip = jnp.repeat(skip_gain, width // heads)[None]
    gain_out_row = gain_out[None]
    w_out_pieces = w_out.reshape(width, pieces, piece).transpose(1, 0, 2)
    owners = (mine - jnp.arange(pieces)) % pieces
    w_out_ring = jnp.take(w_out_pieces, owners, axis=0)

    halo = shifted(layer_input[count - EDGE :], "seq", 1)
    cotangents = ring_gather(output_grad, "head")

    whole = lambda *arrays: [(a, "whole") for a in arrays]
    normed, gate, pre, tot, raw, cum, cum_rows, local, payload = call(
        forward_kernel,
        blocks,
        [(layer_input, "rows")]
        + whole(halo, gain_in[None], w_gate, w_inner, w_bc, w_step_pad, taps, bias, step_bias_pad, decay_pad, lower, spread),
        [
            ((count, features), BF16, "rows"),
            ((count, width), F32, "rows"),
            ((count, both), F32, "rows"),
            ((count, both), F32, "rows"),
            ((count, LANES), F32, "rows"),
            ((count, LANES), F32, "rows"),
            ((blocks, 8, BLOCK), F32, "stack"),
            ((blocks, width, states), F32, "stack"),
            ((2, width + 16, states), BF16, "whole"),
        ],
        [(8, both), (width, states), (16, LANES)],
        flops=4 * 10**9,
    )
    incoming = joined_states(payload, "seq", width, heads, False)
    ssd, starts, squares = call(
        state_kernel,
        blocks,
        [(tot, "rows"), (raw, "rows"), (cum, "rows"), (cum_rows, "stack"), (gate, "rows"), (local, "stack")]
        + whole(incoming, step_bias_pad, skip, hide, spread),
        [
            ((count, width), F32, "rows"),
            ((blocks, width, states), F32, "stack"),
            ((blocks, 8, BLOCK), F32, "stack"),
        ],
        [(width, states)],
        flops=3 * 10**9,
    )
    squares = small_sum(squares, "head")
    normed_out, mixed_parts = call(
        functools.partial(out_kernel, all_width),
        blocks,
        [(ssd, "rows"), (gate, "rows"), (squares, "stack")] + whole(gain_out_row, w_out_pieces),
        [((count, width), BF16, "rows"), ((pieces, count, piece), BF16, "mid")],
        flops=2 * 10**9,
    )
    dn, cross = call(
        functools.partial(cross_kernel, pieces),
        blocks,
        [(c, "rows") for c in cotangents]
        + whole(w_out_ring)
        + [(ssd, "rows"), (gate, "rows")]
        + whole(gain_out_row),
        [((count, width), F32, "rows"), ((blocks, 8, BLOCK), F32, "stack")],
        flops=2 * 10**9,
    )
    cross = small_sum(cross, "head")
    summed = ring_scatter(lambda q: lax.dynamic_index_in_dim(mixed_parts, q, 0, False), "head")
    residual = lax.dynamic_slice_in_dim(layer_input, mine * piece, piece, 1).astype(F32)
    mixed = (residual + summed).astype(BF16)

    dssd, dgate, local_back, payload_back, gw_out, gw_gate, gate_sums = call(
        functools.partial(gate_kernel, pieces, all_width),
        blocks,
        [(c, "rows") for c in cotangents]
        + [(a, "rows") for a in (ssd, gate, dn, tot, cum, normed, normed_out)]
        + [(squares, "stack"), (cross, "stack")]
        + whole(gain_out_row, spread),
        [
            ((count, width), F32, "rows"),
            ((count, width), BF16, "rows"),
            ((blocks, width, states), F32, "stack"),
            ((2, width + 16, states), BF16, "whole"),
            ((pieces, width, piece), F32, "whole"),
            ((features, width), F32, "whole"),
            ((8, width), F32, "whole"),
        ],
        [(width, states), (16, LANES)],
        backward=True,
        flops=4 * 10**9,
    )
    gw_out, gw_gate = lax.psum((gw_out, gw_gate), "seq")
    outgoing = joined_states(payload_back, "seq", width, heads, True)
    d, draw, rate_sums = call(
        pull_kernel,
        blocks,
        [(tot, "rows"), (raw, "rows"), (cum, "rows"), (cum_rows, "stack"), (dssd, "rows"), (starts, "stack"), (local_back, "stack")]
        + whole(outgoing, step_bias_pad, decay_pad, skip, lower, hide, spread),
        [((count, both), F32, "rows"), ((count, LANES), F32, "rows"), ((8, LANES), F32, "whole")],
        [(width, states)],
        backward=True,
        flops=8 * 10**9,
    )
    d_halo = shifted(d[:8], "seq", -1)
    part, gw_inner, gw_bc, gw_step, conv_sums = call(
        project_kernel,
        blocks,
        [(d, "rows")]
        + whole(d_halo)
        + [(pre, "rows"), (normed, "rows"), (dgate, "rows"), (draw, "rows")]
        + whole(taps, w_gate, w_inner, w_bc, w_step_pad),
        [
            ((count, features), BF16, "rows"),
            ((features, width), F32, "whole"),
            ((features, 2 * states), F32, "whole"),
            ((features, LANES), F32, "whole"),
            ((8, both), F32, "whole"),
        ],
        [(8, both)],
        backward=True,
        flops=8 * 10**9,
    )
    dnormed = ring_scatter(lambda q: lax.dynamic_slice_in_dim(part, q * rows, rows, 0), "head")

    layer_x = lax.dynamic_slice_in_dim(layer_input, mine * rows, rows, 0).astype(F32)
    own = [lax.dynamic_slice_in_dim(c, mine * rows, rows, 0) for c in cotangents]
    cotangent = jnp.take(jnp.stack(own), owners, axis=0).transpose(1, 0, 2).reshape(rows, features).astype(F32)
    scale_in = lax.rsqrt(jnp.mean(layer_x * layer_x, -1, keepdims=True) + eps)
    scaled_in = dnormed * gain_in
    gain_part = jnp.sum(dnormed * layer_x * scale_in, 0)
    own_input = scaled_in * scale_in - layer_x * scale_in**3 * jnp.mean(scaled_in * layer_x, -1, keepdims=True)
    own_input = (own_input + cotangent).astype(BF16)
    grad_input = jnp.zeros((count, features), F32)
    for step, block in enumerate(ring_gather(own_input, "head")):
        owner = (mine - step) % pieces
        grad_input = lax.dynamic_update_slice_in_dim(grad_input, block.astype(F32), owner * rows, 0)

    gw_out = jnp.take(gw_out, owners, axis=0).transpose(1, 0, 2).reshape(width, features)
    (gw_inner, gw_bc, gw_step), gw_gate, gw_out = lax.optimization_barrier(
        ((gw_inner, gw_bc, gw_step), gw_gate, gw_out)
    )
    gw_inner, gw_bc, gw_step = lax.psum((gw_inner, gw_bc, gw_step[:, :heads]), "seq")
    seq_count, seq_mine = lax.axis_size("seq"), lax.axis_index("seq")
    share = features // seq_count
    bc_share = lax.dynamic_slice_in_dim(gw_bc, seq_mine * share, share, 0)
    gw_bc = lax.all_gather(small_sum(bc_share, "head"), "seq", axis=0, tiled=True)
    small = [conv_sums, gate_sums, rate_sums]
    packed = butterfly(jnp.concatenate([v.reshape(-1, LANES) for v in small], 0), "seq")
    split, at = [], 0
    for v in small:
        split.append(packed[at : at + v.size // LANES].reshape(v.shape))
        at += v.size // LANES
    conv_sums, gate_sums, rate_sums = split
    shared = jnp.concatenate([v.reshape(-1, LANES) for v in (conv_sums[:, width:] / seq_count, gain_part)], 0)
    shared = butterfly(butterfly(shared, "seq"), "head")
    bc_sums, grad_gain_in = shared[: 4 * states // LANES * 4].reshape(8, 2 * states), shared[16 * states // LANES :].reshape(-1)
    head_dim = width // heads
    return (
        mixed,
        grad_input,
        grad_gain_in,
        gw_gate,
        gw_inner,
        gw_bc,
        gw_step,
        conv_sums[:kernel, :width],
        conv_sums[kernel, :width],
        bc_sums[:kernel],
        bc_sums[kernel],
        rate_sums[0, :heads],
        rate_sums[1, :heads],
        gate_sums[1].reshape(heads, head_dim).sum(1),
        gate_sums[0],
        gw_out,
    )


def solution(mesh):
    placed = (
        P("seq", None),
        P(),
        P(None, "head"),
        P(None, "head"),
        P(),
        P(None, "head"),
        P(None, "head"),
        P("head"),
        P(),
        P(),
        P("head"),
        P("head"),
        P("head"),
        P("head"),
        P("head", None),
        P("seq", "head"),
    )
    return jax.shard_map(
        per_device,
        mesh=mesh,
        in_specs=placed,
        out_specs=(
            P("seq", "head"),
            P("seq", None),
            P(),
            P(None, "head"),
            P(None, "head"),
            P(),
            P(None, "head"),
            P(None, "head"),
            P("head"),
            P(),
            P(),
            P("head"),
            P("head"),
            P("head"),
            P("head"),
            P("head", None),
        ),
        check_vma=False,
    )
```

time: 807 us -> 494 us (0.61)
  waiting for transfers between devices: 332 us -> 130 us
  matrix products: 158 us -> 0 us
  Pallas kernels: 0 us -> 108 us
  other arithmetic: 136 us -> 44.2 us
  starting transfers between devices: 4.96 us -> 38 us
  blocking collectives: 62.8 us -> 78.9 us
  local copies, waits for them, and re-layouts: 91 us -> 76.9 us
    psum x3 -> x2, waiting for transfers between devices: 283 us -> 60 us  [the longest x1 30.2 us: per_device(): lax.psum((gw_inner, gw_bc, gw_step[:, :heads]), 'seq')]
    dot_general x27 -> x0, matrix products: 158 us -> none  [the longest x3 50.5 us: group_out(): output = jnp.einsum('kijh,kjhp->kihp', mixing, inner3, precision=HIGH)]
    pallas_call x0 -> x7, Pallas kernels: none -> 108 us  [call(): pl.pallas_call(kernel, grid=(blocks,), in_specs=[spec(a.shape, kind) for...]
    ppermute x2 -> x31, waiting for transfers between devices: 0.01 us -> 69.6 us  [the longest x21 66.8 us: turn(): lax.ppermute(block, axis, [(i, (i + distance) % count) for i in range(cou...]
    all_gather x0 -> x5, blocking collectives: none -> 52 us  [the longest x4 41.3 us: joined_states(): pieces = [lax.all_gather(part, axis).astype(F32) for part in payload]]
    reduce_scatter x1 -> x0, waiting for transfers between devices: 44.6 us -> none  [per_device(): lax.psum_scatter(jnp.dot(normed_out, w_out, preferred_element_type=jnp.fl...]
    ppermute x2 -> x31, starting transfers between devices: 3.85 us -> 37.7 us  [the longest x21 25.2 us: turn(): lax.ppermute(block, axis, [(i, (i + distance) % count) for i in range(cou...]
    reduce_sum x12 -> x6, other arithmetic: 40 us -> 6.99 us  [the longest x2 3.85 us: joined_states(): return jnp.sum(weight[:, :, None] * states, 0)]
  transfers between devices with their start and end apart: 9 -> 33, of which waited for: 5 -> 13; matrix products, arithmetic and copies ran while one was open for 33% -> 19% of each run, Pallas kernels for 0% -> 13%
where the time goes in v1:
time: 494 us; the launch traced here: 491 us
  waiting for transfers between devices  130 us (26%)
  Pallas kernels  108 us (22%)
  blocking collectives  78.9 us (16%)
  local copies, waits for them, and re-layouts  76.9 us (16%)
  other arithmetic  44.2 us (9%)
  starting transfers between devices  38 us (8%)
  between operations  14.9 us (3%)
    pallas_call x7, Pallas kernels, call(): pl.pallas_call(kernel, grid=(blocks,), in_specs=[spec(a.shape, kind) for...  108 us
    ppermute x21, waiting for transfers between devices, turn(): lax.ppermute(block, axis, [(i, (i + distance) % count) for i in range(cou...  66.8 us
    all_gather x4, blocking collectives, joined_states(): pieces = [lax.all_gather(part, axis).astype(F32) for part in payload]  41.3 us
    psum x1, waiting for transfers between devices, per_device(): lax.psum((gw_inner, gw_bc, gw_step[:, :heads]), 'seq')  30.2 us
    psum x1, waiting for transfers between devices, per_device(): gw_out, gw_gate = lax.psum((gw_out, gw_gate), 'seq')  29.8 us
    unnamed x124, local copies, waits for them, and re-layouts  28 us
    psum x1, blocking collectives, per_device(): lax.psum((gw_inner, gw_bc, gw_step[:, :heads]), 'seq')  26.8 us
    ppermute x21, starting transfers between devices, turn(): lax.ppermute(block, axis, [(i, (i + distance) % count) for i in range(cou...  25.2 us
  transfers between devices with their start and end apart: 33, of which 13 were waited for; matrix products, arithmetic and copies ran while one was open for 19% of the time, Pallas kernels for 13%

profile of v1, /device:TPU:0, one launch (start us, length us, event | category | flops | bytes accessed | tf_op | source)
XLA Modules:
  0.0 490.7 jit_solution(5149422186668998104)
XLA Ops:
  8.0 2.3 collective-permute-start
  10.4 2.5 collective-permute-start.7
  24.6 18.0 %shard_map.279 = (bf16[2048,768]{1,0:T(8,128)(2,1)}, f32[2048,384]{1,0:T(8,128)}, f32[2048,640]{1,0:T(8,128)}, f32[2048,640]{1,0:T(8,128)}, f32[2048,128]{1,0:T(...) custom-call(bf16[2048,768]{1,0:T(8,128)(2,1)} %x.7, ...), custom_call_target="tpu_custom_call" | custom-call | flops 4000000000 | bytes 5186048 | tf_op jit(solution)/shard_map/pallas_call | solution.py:447
  42.6 11.6 %all_gather.15 = bf16[8,400,128]{2,1,0:T(8,128)(2,1)S(1)} all-gather(bf16[1,400,128]{2,1,0:T(8,128)(2,1)S(1)} %get-tuple-element.210), channel_id=1, replica_groups=mesh['seq'=8,'head'=4] {'seq'}, dimensions={0}, use_global_device_ids=true | all-gather | bytes 921600 | tf_op jit(solution)/shard_map/all_gather | solution.py:62
  54.2 9.7 %all_gather.16 = bf16[8,400,128]{2,1,0:T(8,128)(2,1)S(1)} all-gather(bf16[1,400,128]{2,1,0:T(8,128)(2,1)S(1)} %get-tuple-element.211), channel_id=1, replica_groups=mesh['seq'=8,'head'=4] {'seq'}, dimensions={0}, use_global_device_ids=true | all-gather | bytes 921600 | tf_op jit(solution)/shard_map/all_gather | solution.py:62
  67.8 1.9 fusion.13.incoming
  71.0 11.8 %shard_map.280 = (f32[2048,384]{1,0:T(8,128)}, f32[8,384,128]{2,1,0:T(8,128)S(1)}, f32[8,8,256]{2,1,0:T(8,128)S(1)}) custom-call(f32[2048,640]{1,0:T(8,128)} %get-tuple-element.52.tot.refs_7_, f32[2048,128]{1,0:T(8,128)S(1)} %copy-done.11, f32[2048,128]{1,0:T(8,128)S(1)} %get-tuple-element.54.cum_in.refs_8_, f32[8,8,256]{2,1,0:T(8,128)S(1)} %copy-done.20, ...), custom_call_target="tpu_custom_call" | custom-call | flops 3000000000 | bytes 12683264 | tf_op jit(solution)/shard_map/pallas_call | solution.py:447
  90.8 2.0 collective-permute-done.2
  92.8 1.9 collective-permute-start.9
  94.7 1.9 copy-done
  96.6 8.9 %shard_map.281 = (bf16[2048,384]{1,0:T(8,128)(2,1)S(1)}, bf16[4,2048,192]{2,1,0:T(8,128)(2,1)}) custom-call(f32[2048,384]{1,0:T(8,128)S(1)} %copy-done, f32[2048,384]{1,0:T(8,128)} %get-tuple-element.56.gate.refs_6_.refs_5_, f32[8,8,256]{2,1,0:T(8,128)S(1)} %add_add_fusion.2.squares.refs_11_, f32[1,384]{1,0:T(1,128)S(1)} %broadcast_in_dim.145.gain.refs_7_.refs_13_, ...), custom_call_target="tpu_custom_call" | custom-call | flops 2000000000 | bytes 6948352 | tf_op jit(solution)/shard_map/pallas_call | solution.py:447
  114.9 2.2 copy.171.refs_3_
  119.4 8.5 %shard_map.282 = (f32[2048,384]{1,0:T(8,128)}, f32[8,8,256]{2,1,0:T(8,128)}) custom-call(bf16[2048,192]{1,0:T(8,128)(2,1)S(1)} %copy.168.refs_0_, bf16[2048,192]{1,0:T(8,128)(2,1)S(1)} %copy.169.refs_1_, bf16[2048,192]{1,0:T(8,128)(2,1)S(1)} %copy.170.refs_2_, bf16[2048,192]{1,0:T(8,128)(2,1)S(1)} %copy-done.1, bf16[4,384,192]{2,1,0:T(8,128)(2,1)S(1)} %copy-done.6, ...), custom_call_target="tpu_custom_call" | custom-call | flops 2000000000 | bytes 10028544 | tf_op jit(solution)/shard_map/pallas_call | solution.py:447
  128.6 2.2 collective-permute-start.11
  132.4 2.7 copy.159
  140.4 16.6 %shard_map.283 = (f32[2048,384]{1,0:T(8,128)}, bf16[2048,384]{1,0:T(8,128)(2,1)}, f32[8,384,128]{2,1,0:T(8,128)}, bf16[2,400,128]{2,1,0:T(8,128)(2,1)S(1)}, f32[...) custom-call(bf16[2048,192]{1,0:T(8,128)(2,1)S(1)} %copy.168.refs_0_, ...), custom_call_target="tpu_custom_call" | custom-call | flops 4000000000 | bytes 23823872 | tf_op jit(solution)/shard_map/pallas_call | solution.py:447
  157.0 10.4 %all_gather.17 = bf16[8,400,128]{2,1,0:T(8,128)(2,1)S(1)} all-gather(bf16[1,400,128]{2,1,0:T(8,128)(2,1)S(1)} %get-tuple-element.208), channel_id=1, replica_groups=mesh['seq'=8,'head'=4] {'seq'}, dimensions={0}, use_global_device_ids=true | all-gather | bytes 921600 | tf_op jit(solution)/shard_map/all_gather | solution.py:62
  167.4 9.7 %all_gather.18 = bf16[8,400,128]{2,1,0:T(8,128)(2,1)S(1)} all-gather(bf16[1,400,128]{2,1,0:T(8,128)(2,1)S(1)} %get-tuple-element.209), channel_id=1, replica_groups=mesh['seq'=8,'head'=4] {'seq'}, dimensions={0}, use_global_device_ids=true | all-gather | bytes 921600 | tf_op jit(solution)/shard_map/all_gather | solution.py:62
  179.6 1.9 fusion.12.outgoing
  182.9 25.7 %shard_map.284 = (f32[2048,640]{1,0:T(8,128)}, f32[2048,128]{1,0:T(8,128)S(1)}, f32[8,128]{1,0:T(8,128)S(1)}) custom-call(f32[2048,640]{1,0:T(8,128)} %get-tuple-element.52.tot.refs_7_, f32[2048,128]{1,0:T(8,128)S(1)} %copy-done.12, f32[2048,128]{1,0:T(8,128)S(1)} %copy-done.5, f32[8,8,256]{2,1,0:T(8,128)S(1)} %copy-done.21, ...), custom_call_target="tpu_custom_call" | custom-call | flops 8000000000 | bytes 14387712 | tf_op jit(solution)/shard_map/pallas_call | solution.py:447
  211.7 2.6 fusion.3
  214.3 2.3 copy.160
  217.9 18.6 %shard_map.285 = (bf16[2048,768]{1,0:T(8,128)(2,1)}, f32[768,384]{1,0:T(8,128)}, f32[768,256]{1,0:T(8,128)}, f32[768,128]{1,0:T(8,128)S(1)}, f32[8,640]{1,0:T(8,128)S(1)}) custom-call(f32[2048,640]{1,0:T(8,128)} %get-tuple-element.70.d, f32[8,640]{1,0:T(8,128)S(1)} %collective-permute-done.13.halo, f32[2048,640]{1,0:T(8,128)} %get-tuple-element.71.pre, ...), custom_call_target="tpu_custom_call" | custom-call | flops 8000000000 | bytes 18053120 | tf_op jit(solution)/shard_map/pallas_call | solution.py:447
  236.5 2.1 constant_dynamic-slice_fusion
  245.1 2.5 fusion.2
  247.6 2.2 copy.162
  249.8 2.0 collective-permute-start.6
  251.8 9.1 %collective-permute-done.14 = bf16[512,768]{1,0:T(8,128)(2,1)S(1)} collective-permute-done((bf16[512,768]{1,0:T(8,128)(2,1)}, bf16[512,768]{1,0:T(8,128)(2,1)S(1)}, u32[]{:S(2)}, u32[]{:S(2)}) %collective-permute-start.14) | collective-permute-done | bytes 786464 | tf_op jit(solution)/shard_map/ppermute | solution.py:18
  261.0 2.2 add_convert_fusion.1
  266.5 2.6 collective-permute-start.21
  269.8 8.1 %collective-permute-done.6 = bf16[2048,192]{0,1:T(8,128)(2,1)} collective-permute-done((bf16[2048,192]{0,1:T(8,128)(2,1)}, bf16[2048,192]{0,1:T(8,128)(2,1)}, u32[]{:S(2)}, u32[]{:S(2)}) %collective-permute-start.6) | collective-permute-done | bytes 786464 | tf_op jit(solution)/shard_map/ppermute | solution.py:18
  280.2 3.5 collective-permute-start.22
  283.7 11.0 %collective-permute-done.15 = bf16[512,768]{1,0:T(8,128)(2,1)} collective-permute-done((bf16[512,768]{1,0:T(8,128)(2,1)}, bf16[512,768]{1,0:T(8,128)(2,1)}, u32[]{:S(2)}, u32[]{:S(2)}) %collective-permute-start.15) | collective-permute-done | bytes 786464 | tf_op jit(solution)/shard_map/ppermute | solution.py:18
  294.7 2.4 add_convert_fusion
  297.1 3.6 fusion.1
  300.7 2.2 copy.179
  303.5 29.8 %all-reduce.10.cloned.1.call-done = (f32[768,384]{1,0:T(8,128)}, f32[4,384,192]{2,1,0:T(8,128)}) async-done(((f32[768,384]{1,0:T(8,128)}, f32[4,384,192]{2,1,0:T(8,128)}), (f32[768,384]{1,0:T(8,128)}, f32[4,384,192]{2,1,0:T(8,128)})) %all-reduce.10.cloned.1.call-update) | async-done | bytes 2359312 | tf_op jit(solution)/shard_map/psum | solution.py:573
  333.3 2.1 gather_fusion.2
  339.3 2.3 fusion.11
  341.6 3.1 broadcast_in_dim.146
  344.8 3.6 convert_dynamic-update-slice_fusion.3
  354.5 14.9 %collective-permute-done.17 = bf16[512,768]{1,0:T(8,128)(2,1)S(1)} collective-permute-done((bf16[512,768]{1,0:T(8,128)(2,1)}, bf16[512,768]{1,0:T(8,128)(2,1)S(1)}, u32[]{:S(2)}, u32[]{:S(2)}) %collective-permute-start.17) | collective-permute-done | bytes 786464 | tf_op jit(solution)/shard_map/ppermute | solution.py:18
  369.4 30.2 %all-reduce.8.cloned.1.call-done = (f32[768,384]{1,0:T(8,128)}, f32[768,256]{1,0:T(8,128)}) async-done(((f32[768,384]{1,0:T(8,128)}, f32[768,256]{1,0:T(8,128)}), (f32[768,384]{1,0:T(8,128)}, f32[768,256]{1,0:T(8,128)})) %all-reduce.8.cloned.1.call-update) | async-done | bytes 1966096 | tf_op jit(solution)/shard_map/psum | solution.py:623
  402.0 2.4 collective-permute-start.29
  413.0 26.8 %psum.39 = f32[768,6]{1,0:T(8,128)S(1)} all-reduce(f32[768,6]{1,0:T(8,128)S(1)} %bitcast.50), channel_id=1, replica_groups=mesh['seq'=8,'head'=4] {'seq'}, use_global_device_ids=true, to_apply=%region_11.12 | all-reduce | flops 4608 | bytes 36864 | tf_op jit(solution)/shard_map/psum | solution.py:623
  442.9 2.3 collective-permute-done.26
  445.4 10.7 %all_gather.19 = f32[768,256]{1,0:T(8,128)S(1)} all-gather(f32[96,256]{1,0:T(8,128)S(1)} %add_add_fusion), channel_id=1, replica_groups=mesh['seq'=8,'head'=4] {'seq'}, dimensions={0}, use_global_device_ids=true | all-gather | bytes 884736 | tf_op jit(solution)/shard_map/all_gather | solution.py:627
  461.1 17.9 %collective-permute-done.19 = bf16[512,768]{1,0:T(8,128)(2,1)S(1)} collective-permute-done((bf16[512,768]{1,0:T(8,128)(2,1)S(1)}, bf16[512,768]{1,0:T(8,128)(2,1)S(1)}, u32[]{:S(2)}, u32[]{:S(2)}) %collective-permute-start.19) | collective-permute-done | bytes 786464 | tf_op jit(solution)/shard_map/ppermute | solution.py:18
  (264 shorter events, 100.1 us)
Async XLA Ops:
  7.2 11.6 %copy-start.34 = (bf16[2048,192]{0,1:T(8,128)(2,1)S(1)}, bf16[2048,192]{0,1:T(8,128)(2,1)}, u32[]{:S(2)}) copy-start(bf16[2048,192]{0,1:T(8,128)(2,1)} %param.31) | copy-start | bytes 2359300
  7.2 326.1 %all-reduce.10.cloned.1.call-start = ((), (), s32[]{:S(2)}) async-start(), calls=%async_computation.1 | async-start | bytes 5505024 | tf_op jit(solution)/shard_map/psum | solution.py:573
  8.0 12.4 %collective-permute-start = (bf16[16,768]{1,0:T(8,128)(2,1)S(1)}, bf16[16,768]{1,0:T(8,128)(2,1)S(1)}, u32[]{:S(2)}, u32[]{:S(2)}) collective-permute-start(bf16[16,768]{1,0:T(8,128)(2,1)S(1)} %slice.69), channel_id=1, source_target_pairs={{0,4},{4,8},{8,12},{12,16},{16,20},{20,24},{24,28},{1,5},{5,9},{9,... | collective-permute-start | bytes 73736 | tf_op jit(solution)/shard_map/ppermute | solution.py:23
  10.4 55.7 %collective-permute-start.7 = (bf16[2048,192]{0,1:T(8,128)(2,1)}, bf16[2048,192]{0,1:T(8,128)(2,1)}, u32[]{:S(2)}, u32[]{:S(2)}) collective-permute-start(bf16[2048,192]{0,1:T(8,128)(2,1)} %param.31), channel_id=1, source_target_pairs={{0,1},{1,2},{2,3},{3,0},{4,5},{5,6},{6,7},{7,4},{8,9},{9,10},{10,1... | collective-permute-start | bytes 2359304 | tf_op jit(solution)/shard_map/ppermute | solution.py:18
  12.9 6.5 %copy-start.44 = (bf16[768,6]{0,1:T(8,128)(2,1)S(1)}, bf16[768,6]{0,1:T(8,128)(2,1)}, u32[]{:S(2)}) copy-start(bf16[768,6]{0,1:T(8,128)(2,1)} %param.21) | copy-start | bytes 27652
  13.6 6.2 %copy-start.40 = (bf16[384,768]{1,0:T(8,128)(2,1)S(1)}, bf16[384,768]{1,0:T(8,128)(2,1)}, u32[]{:S(2)}) copy-start(bf16[384,768]{1,0:T(8,128)(2,1)} %param.30) | copy-start | bytes 1769476
  20.4 22.1 %copy-start.15 = (bf16[768,128]{1,0:T(8,128)(2,1)}, bf16[768,128]{1,0:T(8,128)(2,1)S(1)}, u32[]{:S(2)}) copy-start(bf16[768,128]{1,0:T(8,128)(2,1)S(1)} %pad.11.w_step) | copy-start | bytes 589828
  42.5 22.7 %copy-start.7 = (f32[8,384,128]{2,1,0:T(8,128)}, f32[8,384,128]{2,1,0:T(8,128)S(1)}, u32[]{:S(2)}) copy-start(f32[8,384,128]{2,1,0:T(8,128)S(1)} %get-tuple-element.57.local) | copy-start | bytes 4718596
  42.5 22.7 %copy-start.10 = (f32[2048,128]{1,0:T(8,128)}, f32[2048,128]{1,0:T(8,128)S(1)}, u32[]{:S(2)}) copy-start(f32[2048,128]{1,0:T(8,128)S(1)} %get-tuple-element.53.raw) | copy-start | bytes 3145732
  42.6 22.7 %copy-start.19 = (f32[8,8,256]{2,1,0:T(8,128)}, f32[8,8,256]{2,1,0:T(8,128)S(1)}, u32[]{:S(2)}) copy-start(f32[8,8,256]{2,1,0:T(8,128)S(1)} %get-tuple-element.55.cum_rows) | copy-start | bytes 196612
  42.6 27.1 %copy-start.3 = (f32[2048,128]{1,0:T(8,128)}, f32[2048,128]{1,0:T(8,128)S(1)}, u32[]{:S(2)}) copy-start(f32[2048,128]{1,0:T(8,128)S(1)} %get-tuple-element.54.cum_in.refs_8_) | copy-start | bytes 3145732
  66.1 26.7 %collective-permute-start.8 = (bf16[2048,192]{0,1:T(8,128)(2,1)}, bf16[2048,192]{0,1:T(8,128)(2,1)}, u32[]{:S(2)}, u32[]{:S(2)}) collective-permute-start(bf16[2048,192]{0,1:T(8,128)(2,1)} %collective-permute-done.7), channel_id=1, source_target_pairs={{0,1},{1,2},{2,3},{3,0},{4,5},{5,6},{6,7},{7,4},{8,9},{9,10},{10,1... | collective-permute-start | bytes 2359304 | tf_op jit(solution)/shard_map/ppermute | solution.py:18
  71.0 17.3 %copy-start.53 = (s32[4]{0:T(128)S(1)}, s32[4]{0:T(128)}, u32[]{:S(2)}) copy-start(s32[4]{0:T(128)} %fusion.25) | copy-start | bytes 52
  84.0 6.8 %collective-permute-start.1 = (f32[8,8,256]{2,1,0:T(8,128)S(1)}, f32[8,8,256]{2,1,0:T(8,128)S(1)}, u32[]{:S(2)}, u32[]{:S(2)}) collective-permute-start(f32[8,8,256]{2,1,0:T(8,128)S(1)} %get-tuple-element.60), channel_id=1, source_target_pairs={{0,1},{1,2},{2,3},{3,0},{4,5},{5,6},{6,7},{7,4},{8,9},{9,10},{10,1... | collective-permute-start | bytes 196616 | tf_op jit(solution)/shard_map/ppermute | solution.py:18
  85.6 7.2 %collective-permute-start.2 = (f32[8,8,256]{2,1,0:T(8,128)S(1)}, f32[8,8,256]{2,1,0:T(8,128)S(1)}, u32[]{:S(2)}, u32[]{:S(2)}) collective-permute-start(f32[8,8,256]{2,1,0:T(8,128)S(1)} %get-tuple-element.60), channel_id=1, source_target_pairs={{0,2},{1,3},{2,0},{3,1},{4,6},{5,7},{6,4},{7,5},{8,10},{9,11},{10,... | collective-permute-start | bytes 196616 | tf_op jit(solution)/shard_map/ppermute | solution.py:18
  86.8 6.0 %collective-permute-start.3 = (f32[8,8,256]{2,1,0:T(8,128)S(1)}, f32[8,8,256]{2,1,0:T(8,128)S(1)}, u32[]{:S(2)}, u32[]{:S(2)}) collective-permute-start(f32[8,8,256]{2,1,0:T(8,128)S(1)} %get-tuple-element.60), channel_id=1, source_target_pairs={{0,3},{1,0},{2,1},{3,2},{4,7},{5,4},{6,5},{7,6},{8,11},{9,8},{10,9... | collective-permute-start | bytes 196616 | tf_op jit(solution)/shard_map/ppermute | solution.py:18
  92.8 12.8 %copy-start.13 = (f32[8,8,256]{2,1,0:T(8,128)}, f32[8,8,256]{2,1,0:T(8,128)S(1)}, u32[]{:S(2)}) copy-start(f32[8,8,256]{2,1,0:T(8,128)S(1)} %add_add_fusion.2.squares.refs_11_) | copy-start | bytes 196612
  92.8 22.1 %collective-permute-start.9 = (bf16[2048,192]{0,1:T(8,128)(2,1)}, bf16[2048,192]{0,1:T(8,128)(2,1)}, u32[]{:S(2)}, u32[]{:S(2)}) collective-permute-start(bf16[2048,192]{0,1:T(8,128)(2,1)} %collective-permute-done.8), channel_id=1, source_target_pairs={{0,1},{1,2},{2,3},{3,0},{4,5},{5,6},{6,7},{7,4},{8,9},{9,10},{10,1... | collective-permute-start | bytes 2359304 | tf_op jit(solution)/shard_map/ppermute | solution.py:18
  109.3 23.1 %collective-permute-start.4 = (bf16[2048,192]{0,1:T(8,128)(2,1)}, bf16[2048,192]{0,1:T(8,128)(2,1)}, u32[]{:S(2)}, u32[]{:S(2)}) collective-permute-start(bf16[2048,192]{0,1:T(8,128)(2,1)} %bitcast.54), channel_id=1, source_target_pairs={{0,1},{1,2},{2,3},{3,0},{4,5},{5,6},{6,7},{7,4},{8,9},{9,10},{10,1... | collective-permute-start | bytes 2359304 | tf_op jit(solution)/shard_map/ppermute | solution.py:18
  119.4 12.4 %copy-start.51 = (pred[8]{0:T(512)(128)(4,1)S(1)}, pred[8]{0:T(512)(128)(4,1)}, u32[]{:S(2)}) copy-start(pred[8]{0:T(512)(128)(4,1)} %get-tuple-element.218) | copy-start | bytes 28
  128.0 7.1 %collective-permute-start.10 = (f32[8,8,256]{2,1,0:T(8,128)}, f32[8,8,256]{2,1,0:T(8,128)}, u32[]{:S(2)}, u32[]{:S(2)}) collective-permute-start(f32[8,8,256]{2,1,0:T(8,128)} %get-tuple-element.65), channel_id=1, source_target_pairs={{0,1},{1,2},{2,3},{3,0},{4,5},{5,6},{6,7},{7,4},{8,9},{9,10},{10,1... | collective-permute-start | bytes 196616 | tf_op jit(solution)/shard_map/ppermute | solution.py:18
  128.6 7.5 %collective-permute-start.11 = (f32[8,8,256]{2,1,0:T(8,128)}, f32[8,8,256]{2,1,0:T(8,128)}, u32[]{:S(2)}, u32[]{:S(2)}) collective-permute-start(f32[8,8,256]{2,1,0:T(8,128)} %get-tuple-element.65), channel_id=1, source_target_pairs={{0,2},{1,3},{2,0},{3,1},{4,6},{5,7},{6,4},{7,5},{8,10},{9,11},{10,... | collective-permute-start | bytes 196616 | tf_op jit(solution)/shard_map/ppermute | solution.py:18
  130.8 5.4 %collective-permute-start.12 = (f32[8,8,256]{2,1,0:T(8,128)}, f32[8,8,256]{2,1,0:T(8,128)}, u32[]{:S(2)}, u32[]{:S(2)}) collective-permute-start(f32[8,8,256]{2,1,0:T(8,128)} %get-tuple-element.65), channel_id=1, source_target_pairs={{0,3},{1,0},{2,1},{3,2},{4,7},{5,4},{6,5},{7,6},{8,11},{9,8},{10,9... | collective-permute-start | bytes 196616 | tf_op jit(solution)/shard_map/ppermute | solution.py:18
  182.9 28.7 %copy-start.32 = (f32[2048,192]{1,0:T(8,128)S(1)}, f32[2048,192]{1,0:T(8,128)}, u32[]{:S(2)}) copy-start(f32[2048,192]{1,0:T(8,128)} %copy.159) | copy-start | bytes 4718596
  210.4 7.5 %collective-permute-start.13 = (f32[8,640]{1,0:T(8,128)S(1)}, f32[8,640]{1,0:T(8,128)S(1)}, u32[]{:S(2)}, u32[]{:S(2)}) collective-permute-start(f32[8,640]{1,0:T(8,128)S(1)} %slice.74), channel_id=1, source_target_pairs={{4,0},{8,4},{12,8},{16,12},{20,16},{24,20},{28,24},{5,1},{9,5},{13... | collective-permute-start | bytes 61448 | tf_op jit(solution)/shard_map/ppermute | solution.py:23
  211.6 6.2 %copy-start.31 = (f32[2048,128]{1,0:T(8,128)S(1)}, f32[2048,128]{1,0:T(8,128)}, u32[]{:S(2)}) copy-start(f32[2048,128]{1,0:T(8,128)} %copy-done.30) | copy-start | bytes 3145732
  216.6 27.1 %collective-permute-start.5 = (bf16[2048,192]{0,1:T(8,128)(2,1)}, bf16[2048,192]{0,1:T(8,128)(2,1)}, u32[]{:S(2)}, u32[]{:S(2)}) collective-permute-start(bf16[2048,192]{0,1:T(8,128)(2,1)} %copy.160), channel_id=1, source_target_pairs={{0,1},{1,2},{2,3},{3,0},{4,5},{5,6},{6,7},{7,4},{8,9},{9,10},{10,1... | collective-permute-start | bytes 2359304 | tf_op jit(solution)/shard_map/ppermute | solution.py:18
  238.6 22.4 %collective-permute-start.14 = (bf16[512,768]{1,0:T(8,128)(2,1)}, bf16[512,768]{1,0:T(8,128)(2,1)S(1)}, u32[]{:S(2)}, u32[]{:S(2)}) collective-permute-start(bf16[512,768]{1,0:T(8,128)(2,1)} %constant_dynamic-slice_fusion), channel_id=1, source_target_pairs={{0,1},{1,2},{2,3},{3,0},{4,5},{5,6},{6,7},{7,4},{8,9},{9,10},{10,1... | collective-permute-start | bytes 2359304 | tf_op jit(solution)/shard_map/ppermute | solution.py:18
  249.8 28.1 %collective-permute-start.6 = (bf16[2048,192]{0,1:T(8,128)(2,1)}, bf16[2048,192]{0,1:T(8,128)(2,1)}, u32[]{:S(2)}, u32[]{:S(2)}) collective-permute-start(bf16[2048,192]{0,1:T(8,128)(2,1)} %copy.162), channel_id=1, source_target_pairs={{0,1},{1,2},{2,3},{3,0},{4,5},{5,6},{6,7},{7,4},{8,9},{9,10},{10,1... | collective-permute-start | bytes 2359304 | tf_op jit(solution)/shard_map/ppermute | solution.py:18
  263.2 31.5 %collective-permute-start.15 = (bf16[512,768]{1,0:T(8,128)(2,1)}, bf16[512,768]{1,0:T(8,128)(2,1)}, u32[]{:S(2)}, u32[]{:S(2)}) collective-permute-start(bf16[512,768]{1,0:T(8,128)(2,1)} %add_convert_fusion.1), channel_id=1, source_target_pairs={{0,1},{1,2},{2,3},{3,0},{4,5},{5,6},{6,7},{7,4},{8,9},{9,10},{10,1... | collective-permute-start | bytes 2359304 | tf_op jit(solution)/shard_map/ppermute | solution.py:18
  264.3 135.3 %all-reduce.8.cloned.1.call-start = ((), (), s32[]{:S(2)}) async-start(), calls=%async_computation | async-start | bytes 3932160 | tf_op jit(solution)/shard_map/psum | solution.py:623
  264.6 1.3 collective-permute-start.20
  266.5 12.9 %collective-permute-start.21 = (f32[72,128]{1,0:T(8,128)}, f32[72,128]{1,0:T(8,128)}, u32[]{:S(2)}, u32[]{:S(2)}) collective-permute-start(f32[72,128]{1,0:T(8,128)} %add.266), channel_id=1, source_target_pairs={{0,8},{4,12},{8,0},{12,4},{16,24},{20,28},{24,16},{28,20},{1,9},{5... | collective-permute-start | bytes 110600 | tf_op jit(solution)/shard_map/ppermute | solution.py:55
  280.2 22.7 %collective-permute-start.22 = (f32[72,128]{1,0:T(8,128)S(1)}, f32[72,128]{1,0:T(8,128)S(1)}, u32[]{:S(2)}, u32[]{:S(2)}) collective-permute-start(f32[72,128]{1,0:T(8,128)S(1)} %add.267), channel_id=1, source_target_pairs={{0,16},{4,20},{8,24},{12,28},{16,0},{20,4},{24,8},{28,12},{1,17},{... | collective-permute-start | bytes 110600 | tf_op jit(solution)/shard_map/ppermute | solution.py:55
  297.1 41.5 %collective-permute-start.16 = (bf16[512,768]{1,0:T(8,128)(2,1)}, bf16[512,768]{1,0:T(8,128)(2,1)}, u32[]{:S(2)}, u32[]{:S(2)}) collective-permute-start(bf16[512,768]{1,0:T(8,128)(2,1)} %add_convert_fusion), channel_id=1, source_target_pairs={{0,1},{1,2},{2,3},{3,0},{4,5},{5,6},{6,7},{7,4},{8,9},{9,10},{10,1... | collective-permute-start | bytes 2359304 | tf_op jit(solution)/shard_map/ppermute | solution.py:18
  302.9 30.4 %copy-start.41 = (f32[72,128]{1,0:T(8,128)}, f32[72,128]{1,0:T(8,128)S(1)}, u32[]{:S(2)}) copy-start(f32[72,128]{1,0:T(8,128)S(1)} %add.268) | copy-start | bytes 110596
  348.3 21.0 %collective-permute-start.17 = (bf16[512,768]{1,0:T(8,128)(2,1)}, bf16[512,768]{1,0:T(8,128)(2,1)S(1)}, u32[]{:S(2)}, u32[]{:S(2)}) collective-permute-start(bf16[512,768]{1,0:T(8,128)(2,1)} %get-tuple-element.207), channel_id=1, source_target_pairs={{0,1},{1,2},{2,3},{3,0},{4,5},{5,6},{6,7},{7,4},{8,9},{9,10},{10,1... | collective-permute-start | bytes 2359304 | tf_op jit(solution)/shard_map/ppermute | solution.py:18
  351.9 1.3 collective-permute-start.23
  353.2 52.7 %collective-permute-start.24 = (f32[22,128]{1,0:T(8,128)S(1)}, f32[22,128]{1,0:T(8,128)}, u32[]{:S(2)}, u32[]{:S(2)}) collective-permute-start(f32[22,128]{1,0:T(8,128)S(1)} %fusion.26), channel_id=1, source_target_pairs={{0,8},{4,12},{8,0},{12,4},{16,24},{20,28},{24,16},{28,20},{1,9},{5... | collective-permute-start | bytes 33800 | tf_op jit(solution)/shard_map/ppermute | solution.py:55
  369.4 88.0 %collective-permute-start.18 = (bf16[512,768]{1,0:T(8,128)(2,1)S(1)}, bf16[512,768]{1,0:T(8,128)(2,1)S(1)}, u32[]{:S(2)}, u32[]{:S(2)}) collective-permute-start(bf16[512,768]{1,0:T(8,128)(2,1)S(1)} %collective-permute-done.17), channel_id=1, source_target_pairs={{0,1},{1,2},{2,3},{3,0},{4,5},{5,6},{6,7},{7,4},{8,9},{9,10},{10,1... | collective-permute-start | bytes 2359304 | tf_op jit(solution)/shard_map/ppermute | solution.py:18
  400.5 41.4 %collective-permute-start.28 = (f32[96,256]{1,0:T(8,128)S(1)}, f32[96,256]{1,0:T(8,128)S(1)}, u32[]{:S(2)}, u32[]{:S(2)}) collective-permute-start(f32[96,256]{1,0:T(8,128)S(1)} %constant_dynamic-slice_fusion.2), channel_id=1, source_target_pairs={{0,1},{1,2},{2,3},{3,0},{4,5},{5,6},{6,7},{7,4},{8,9},{9,10},{10,1... | collective-permute-start | bytes 294920 | tf_op jit(solution)/shard_map/ppermute | solution.py:18
  402.0 39.9 %collective-permute-start.29 = (f32[96,256]{1,0:T(8,128)S(1)}, f32[96,256]{1,0:T(8,128)S(1)}, u32[]{:S(2)}, u32[]{:S(2)}) collective-permute-start(f32[96,256]{1,0:T(8,128)S(1)} %constant_dynamic-slice_fusion.2), channel_id=1, source_target_pairs={{0,2},{1,3},{2,0},{3,1},{4,6},{5,7},{6,4},{7,5},{8,10},{9,11},{10,... | collective-permute-start | bytes 294920 | tf_op jit(solution)/shard_map/ppermute | solution.py:18
  404.4 37.5 %collective-permute-start.30 = (f32[96,256]{1,0:T(8,128)S(1)}, f32[96,256]{1,0:T(8,128)S(1)}, u32[]{:S(2)}, u32[]{:S(2)}) collective-permute-start(f32[96,256]{1,0:T(8,128)S(1)} %constant_dynamic-slice_fusion.2), channel_id=1, source_target_pairs={{0,3},{1,0},{2,1},{3,2},{4,7},{5,4},{6,5},{7,6},{8,11},{9,8},{10,9... | collective-permute-start | bytes 294920 | tf_op jit(solution)/shard_map/ppermute | solution.py:18
  407.2 33.4 %collective-permute-start.25 = (f32[22,128]{1,0:T(8,128)}, f32[22,128]{1,0:T(8,128)S(1)}, u32[]{:S(2)}, u32[]{:S(2)}) collective-permute-start(f32[22,128]{1,0:T(8,128)} %add.270), channel_id=1, source_target_pairs={{0,16},{4,20},{8,24},{12,28},{16,0},{20,4},{24,8},{28,12},{1,17},{... | collective-permute-start | bytes 33800 | tf_op jit(solution)/shard_map/ppermute | solution.py:55
  441.3 3.8 collective-permute-start.26
  445.2 11.0 %collective-permute-start.27 = (f32[22,128]{1,0:T(8,128)S(1)}, f32[22,128]{1,0:T(8,128)S(1)}, u32[]{:S(2)}, u32[]{:S(2)}) collective-permute-start(f32[22,128]{1,0:T(8,128)S(1)} %add.272), channel_id=1, source_target_pairs={{0,2},{1,3},{2,0},{3,1},{4,6},{5,7},{6,4},{7,5},{8,10},{9,11},{10,... | collective-permute-start | bytes 33800 | tf_op jit(solution)/shard_map/ppermute | solution.py:55
  457.4 21.6 %collective-permute-start.19 = (bf16[512,768]{1,0:T(8,128)(2,1)S(1)}, bf16[512,768]{1,0:T(8,128)(2,1)S(1)}, u32[]{:S(2)}, u32[]{:S(2)}) collective-permute-start(bf16[512,768]{1,0:T(8,128)(2,1)S(1)} %collective-permute-done.18), channel_id=1, source_target_pairs={{0,1},{1,2},{2,3},{3,0},{4,5},{5,6},{6,7},{7,4},{8,9},{9,10},{10,1... | collective-permute-start | bytes 2359304 | tf_op jit(solution)/shard_map/ppermute | solution.py:18
  461.1 19.2 %copy-start.35 = (f32[768,384]{1,0:T(8,128)S(1)}, f32[768,384]{1,0:T(8,128)}, u32[]{:S(2)}) copy-start(f32[768,384]{1,0:T(8,128)} %get-tuple-element.239) | copy-start | bytes 3538948
  (41 other events, 102.4 us)
Sparse Core Ops, SparseCore 0:
  264.4 68.8 all-reduce.9
  338.7 60.8 all-reduce.7

commit v2 on v1

--- a/solution.py
+++ b/solution.py
@@ -1,6 +1,7 @@
 import functools
 import jax
 import jax.numpy as jnp
+import numpy as np
 from jax import lax
 from jax.experimental import pallas as pl
 from jax.experimental.pallas import tpu as pltpu
@@ -23,23 +24,91 @@
     return lax.ppermute(block, axis, [(i - distance, i) for i in devices if i - distance in devices])
 
 
-def ring_gather(block, axis):
-    pieces = [block]
-    for _ in range(lax.axis_size(axis) - 1):
-        pieces.append(turn(pieces[-1], axis, 1))
-    return pieces
+def tie(*values):
+    return lax.optimization_barrier(values)
 
 
 def ring_scatter(parts, axis):
     count, mine = lax.axis_size(axis), lax.axis_index(axis)
     total = parts((mine - 1) % count)
     for step in range(count - 1):
-        arrived = turn(total, axis, 1)
-        own = parts((mine - 2 - step) % count)
-        total = arrived.astype(F32) + own.astype(F32)
+        arrived = yield turn(total, axis, 1)
+        total = arrived.astype(F32) + parts((mine - 2 - step) % count).astype(F32)
         if step < count - 2:
             total = total.astype(BF16)
-    return total
+    yield total
+
+
+def halved(value, axis, reach):
+    count, mine = lax.axis_size(axis), lax.axis_index(axis)
+    pair = value.reshape(2, value.shape[0] // 2, value.shape[1])
+    bit = (mine // reach) % 2
+    sent = lax.dynamic_index_in_dim(pair, 1 - bit, 0, False)
+    kept = lax.dynamic_index_in_dim(pair, bit, 0, False)
+    return kept + lax.ppermute(sent, axis, [(i, i ^ reach) for i in range(count)])
+
+
+def doubled(value, axis, reach):
+    count, mine = lax.axis_size(axis), lax.axis_index(axis)
+    other = lax.ppermute(value, axis, [(i, i ^ reach) for i in range(count)])
+    second = (mine // reach) % 2 == 1
+    return jnp.where(second, jnp.concatenate([other, value], 0), jnp.concatenate([value, other], 0))
+
+
+def swapped_sum(value, axis, reach):
+    return value + lax.ppermute(value, axis, [(i, i ^ reach) for i in range(lax.axis_size(axis))])
+
+
+def reaches(axis):
+    reach, found = 1, []
+    while reach < lax.axis_size(axis):
+        found.append(reach)
+        reach *= 2
+    return found
+
+
+def weight_chores(gw_inner, gw_bc, sums, width):
+    for reach in reaches("seq"):
+        gw_inner, gw_bc, sums = yield (
+            halved(gw_inner, "seq", reach),
+            halved(gw_bc, "seq", reach),
+            swapped_sum(sums, "seq", reach),
+        )
+    share = gw_bc.shape[0]
+    mine = jnp.concatenate([gw_bc, sums[:8, width : width + gw_bc.shape[1]]], 0)
+    shared, gw_inner = yield small_sum(mine, "head"), gw_inner
+    gw_bc, bc_sums = shared[:share], shared[share:]
+    for reach in reaches("seq")[::-1]:
+        gw_inner, gw_bc = yield doubled(gw_inner, "seq", reach), doubled(gw_bc, "seq", reach)
+    yield gw_inner, gw_bc, sums, bc_sums
+
+
+def gain_chores(gain_part):
+    gain_part = yield (small_sum(gain_part[0], "head"),)
+    for reach in reaches("seq"):
+        gain_part = yield (swapped_sum(gain_part[0], "seq", reach),)
+
+
+class Chores:
+    def __init__(self, steps):
+        self.steps, self.state = steps, next(steps)
+
+    def beside(self, running):
+        if self.steps is not None:
+            running, *state = tie(running, *self.state)
+            self.advance(tuple(state))
+        return running
+
+    def advance(self, state):
+        try:
+            self.state = self.steps.send(state)
+        except StopIteration:
+            self.state, self.steps = state, None
+
+    def finish(self):
+        while self.steps is not None:
+            self.advance(self.state)
+        return self.state
 
 
 def small_sum(value, axis):
@@ -49,20 +118,13 @@
     return total
 
 
-def butterfly(value, axis):
-    count, reach = lax.axis_size(axis), 1
-    while reach < count:
-        value = value + lax.ppermute(value, axis, [(i, i ^ reach) for i in range(count)])
-        reach *= 2
-    return value
-
-
-def joined_states(payload, axis, width, heads, backward):
+def joined_states(pieces, axis, width, heads, backward, fine=None):
     count, mine = lax.axis_size(axis), lax.axis_index(axis)
-    pieces = [lax.all_gather(part, axis).astype(F32) for part in payload]
-    pieces = pieces[0] + pieces[1]
-    logs = pieces[:, width, :heads]
+    pieces = pieces.astype(F32)
+    logs = pieces[:, width, :heads] + pieces[:, width + 8, :heads]
     states = pieces[:, :width]
+    if fine is not None:
+        states = states + fine.astype(F32)
     place = jnp.arange(count)
     k, m = place[:, None], place[None, :]
     if backward:
@@ -140,8 +202,8 @@
 
 
 def forward_kernel(
-    x, halo, gain, w_gate, w_inner, w_bc, w_step, taps, bias, step_bias, decay_log, lower, spread,
-    normed_o, gate_o, pre_o, tot_o, raw_o, cum_o, cum_rows_o, local_o, payload_o,
+    x, halo, gain, w_gate, w_inner, w_bc, w_step, taps_a, taps_b, bias_a, bias_b, step_bias, decay_log, lower, spread,
+    normed_o, gate_o, pre_o, tot_o, raw_o, cum_o, cum_rows_o, local_o, payload_o, fine_o,
     before, state, passed,
 ):
     here, length, width = pl.program_id(0), x.shape[0], w_gate.shape[1]
@@ -163,18 +225,19 @@
     gate_o[...] = dot(normed, w_gate[...])
     pre = jnp.concatenate([dot(normed, w_inner[...]), dot(normed, w_bc[...])], 1)
     pre_o[...] = pre
-    raw = dot(normed, w_step[...])
+    raw = padded_row(dot(normed, w_step[...]))
     raw_o[...] = raw
     padded = jnp.concatenate([before[...], pre], 0)
+    taps = jnp.concatenate([taps_a[...], taps_b[...]], 1)
     kernel = taps.shape[0]
     first = 8 - (kernel - 1)
-    total = bias[...] + sum(taps[k : k + 1, :] * padded[first + k : first + k + length] for k in range(kernel))
+    total = jnp.concatenate([bias_a[...], bias_b[...]], 1) + sum(taps[k : k + 1, :] * padded[first + k : first + k + length] for k in range(kernel))
     before[...] = pre[length - 8 :]
     tot_o[...] = total
     inner = silu(total[:, :width])
     keys = silu(total[:, width : width + LANES]).astype(BF16)
-    _, step = steps(raw, step_bias[...])
-    rate = -jnp.exp(decay_log[...]) * step
+    _, step = steps(raw, padded_row(step_bias[...]))
+    rate = -jnp.exp(padded_row(decay_log[...])) * step
     cum = dot_right(lower[...], rate)
     cum_o[...] = cum
     cum_rows_o[0] = cum.T[:8]
@@ -184,20 +247,27 @@
     local_o[0] = local
     state[...] = state_decay(last, spread[...]) * state[...] + local
     passed[...] = passed[...] + last
-    write_payload(payload_o, state, passed)
-
-
-def write_payload(payload_o, state, passed):
+    write_payload(payload_o, state, passed, fine_o)
+
+
+def padded_row(row):
+    return jnp.concatenate([row, jnp.zeros((row.shape[0], LANES - row.shape[1]), F32)], 1)
+
+
+def skip_row(skip, spread):
+    return widen(jnp.broadcast_to(padded_row(skip[...]), (8, LANES)), spread[...])[0:1]
+
+
+def write_payload(payload_o, state, passed, fine_o=None):
     width = state.shape[0]
 
     @pl.when(pl.program_id(0) == pl.num_programs(0) - 1)
     def _():
-        coarse, fine = halves(state[...])
-        payload_o[0, :width] = coarse
-        payload_o[1, :width] = fine
-        coarse, fine = halves(passed[...])
-        payload_o[0, width:] = coarse
-        payload_o[1, width:] = fine
+        payload_o[:width] = state[...].astype(BF16)
+        coarse = passed[:8].astype(BF16).astype(F32)
+        payload_o[width : width + 16] = jnp.concatenate([coarse, passed[:8] - coarse], 0).astype(BF16)
+        if fine_o is not None:
+            fine_o[...] = halves(state[...])[1]
 
 
 def state_kernel(
@@ -214,7 +284,7 @@
     inner = silu(tot[:, :width])
     keys = silu(tot[:, width : width + LANES]).astype(BF16)
     queries = silu(tot[:, width + LANES :])
-    _, step = steps(raw[...], step_bias[...])
+    _, step = steps(raw[...], padded_row(step_bias[...]))
     cum = cum_in[...]
     start = state[...]
     start_o[0] = start
@@ -235,7 +305,7 @@
             part = dot((scores * decay).astype(BF16), pair)
             out = part if out is None else jnp.where(lane < half * head_dim, out, part)
         outs.append(out)
-    ssd = jnp.concatenate(outs, 1) + carried + skip[...] * inner
+    ssd = jnp.concatenate(outs, 1) + carried + skip_row(skip, spread) * inner
     ssd_o[...] = ssd
     mixed = ssd * silu(gate[...])
     squares_o[0] = as_rows(mixed * mixed)
@@ -258,12 +328,12 @@
     normed = (mixed * scale_of(squares[0], width, all_width) * gain[...]).astype(BF16)
     normed_o[...] = normed
     for piece in range(w_out.shape[0]):
-        part_o[piece] = dot(normed, w_out[piece]).astype(BF16)
+        part_o[piece] = dot(w_out[piece], normed, 1, 1).astype(BF16)
 
 
 def cross_kernel(pieces, *refs):
     grads, (w_out, ssd, gate, gain, dn_o, cross_o) = refs[:pieces], refs[pieces:]
-    dn = sum(dot(grads[p][...], w_out[p], 1, 1) for p in range(pieces))
+    dn = sum(dot(grads[p][...], w_out[p], 0, 0) for p in range(pieces))
     dn_o[...] = dn
     cross_o[0] = as_rows(dn * gain[...] * (ssd[...] * silu(gate[...])))
 
@@ -307,7 +377,7 @@
     state[...] = state_decay(cum[length - 1 :], spread[...]) * state[...] + local
     passed[...] = passed[...] + cum[length - 1 :]
     for p in range(pieces):
-        gw_out_o[p] = gw_out_o[p] + dot(normed_out[...], grads[p][...], 0, 0)
+        gw_out_o[p] = gw_out_o[p] + dot(grads[p][...], normed_out[...])
     gw_gate_o[...] = gw_gate_o[...] + dot(normed[...], dgate, 0, 0)
     write_payload(payload_o, state, passed)
 
@@ -327,8 +397,9 @@
     inner = silu(tot[:, :width])
     keys = silu(tot[:, width : width + LANES]).astype(BF16)
     queries = silu(tot[:, width + LANES :])
-    shifted_raw, step = steps(raw[...], step_bias[...])
-    rate = -jnp.exp(decay_log[...]) * step
+    shifted_raw, step = steps(raw[...], padded_row(step_bias[...]))
+    growth = jnp.exp(padded_row(decay_log[...]))
+    rate = -growth * step
     cum = cum_in[...]
     last = cum[length - 1 : length]
     ending = state[...]
@@ -383,12 +454,12 @@
     coarse, fine = halves(dscores)
     dqueries = dqueries + dot(coarse, keys) + dot(fine, keys)
     dkeys = dkeys + (dot_left(queries, coarse, 0, 0) + dot(queries.astype(BF16), fine, 0, 0)).T
-    dinner = (tail_w * taken + step_w * pulled) + skip[...] * dy
+    dinner = (tail_w * taken + step_w * pulled) + skip_row(skip, spread) * dy
     dstep = narrow(inner * pulled, spread[...]) + to_end
     given = to_end * step
     drate = dot_right(lower[...], crossing + from_start, 0, 0) + (dot_right(lower[...], given) - given)
     drate = drate + through
-    dstep = dstep - jnp.exp(decay_log[...]) * drate
+    dstep = dstep - growth * drate
     draw = dstep * jax.nn.sigmoid(shifted_raw)
     draw_o[...] = draw
     sums_o[0:1] = sums_o[0:1] + row_sum(draw)
@@ -399,19 +470,24 @@
 
 
 def project_kernel(
-    d, halo, pre, normed, dgate, draw, taps, w_gate, w_inner, w_bc, w_step,
-    part_o, gw_inner_o, gw_bc_o, gw_step_o, sums_o,
-    after,
+    earlier, d, halo, pre, normed, dgate, draw, gate_sums, rate_sums, taps_a, taps_b, w_gate, w_inner, w_bc, w_step, *refs
 ):
+    given, (part_o, *totals, after) = refs[:earlier], refs[earlier:]
+    gw_inner_o, gw_bc_o, sums_o = totals
     width, length = w_gate.shape[1], d.shape[0]
 
     @pl.when(pl.program_id(0) == 0)
     def _():
         after[...] = halo[...]
-        for out in (gw_inner_o, gw_bc_o, gw_step_o, sums_o):
-            out[...] = jnp.zeros_like(out)
-
-    kernel = taps.shape[0]
+        for at, out in enumerate(totals):
+            out[...] = given[at][...] if earlier else jnp.zeros_like(out)
+        if not earlier:
+            rows = jnp.concatenate([gate_sums[0:2], rate_sums[0:2], jnp.zeros((2, LANES), F32)], 1)
+            sums_o[taps_a.shape[0] + 1 : taps_a.shape[0] + 3, : rows.shape[1]] = rows
+
+    taps = jnp.concatenate([taps_a[...], taps_b[...]], 1)
+    kernel, heads, both = taps.shape[0], w_step.shape[1], taps.shape[1]
+    features = normed.shape[1]
     grads = d[...]
     padded = jnp.concatenate([grads, after[...]], 0)
     after[...] = grads[:8]
@@ -419,42 +495,118 @@
     for k in range(kernel):
         moved = padded[kernel - 1 - k : kernel - 1 - k + length]
         dpre = dpre + taps[k : k + 1, :] * moved
-        sums_o[k : k + 1] = sums_o[k : k + 1] + row_sum(pre[...] * moved)
-    sums_o[kernel : kernel + 1] = sums_o[kernel : kernel + 1] + row_sum(grads)
-    dinner, dbc, dstep = dpre[:, :width].astype(BF16), dpre[:, width:], draw[...].astype(BF16)
+        sums_o[k : k + 1, :both] = sums_o[k : k + 1, :both] + row_sum(pre[...] * moved)
+    sums_o[kernel : kernel + 1, :both] = sums_o[kernel : kernel + 1, :both] + row_sum(grads)
+    dinner, dbc, dstep = dpre[:, :width].astype(BF16), dpre[:, width:], draw[:, :heads].astype(BF16)
     part = dot(dgate[...], w_gate[...], 1, 1) + dot(dinner, w_inner[...], 1, 1)
     part = part + dot_left(dbc, w_bc[...], 1, 1) + dot(dstep, w_step[...], 1, 1)
     part_o[...] = part.astype(BF16)
     gw_inner_o[...] = gw_inner_o[...] + dot(normed[...], dinner, 0, 0)
     gw_bc_o[...] = gw_bc_o[...] + dot_right(normed[...], dbc, 0, 0)
-    gw_step_o[...] = gw_step_o[...] + dot(normed[...], dstep, 0, 0)
-
-
-def call(kernel, blocks, ins, outs, scratch=(), backward=False, flops=10**9):
-    def spec(shape, kind):
+    sums_o[8 : 8 + heads, :features] = sums_o[8 : 8 + heads, :features] + dot(dstep, normed[...], 0, 0)
+
+
+def input_kernel(place, dnormed, x, gain, *refs):
+    pieces = len(refs) - 3
+    grads, (block_o, sums_o, columns) = refs[:pieces], refs[pieces:]
+    for p in range(pieces):
+        columns[(place[0] - p + pieces) % pieces] = grads[p][...].astype(F32)
+    cotangent = jnp.concatenate([columns[q] for q in range(pieces)], 0).T
+    rows = x[...].astype(F32)
+    scale = lax.rsqrt(jnp.mean(rows * rows, -1, keepdims=True) + eps)
+    scaled = dnormed[...] * gain[...]
+    sums_o[...] = jnp.broadcast_to(row_sum(dnormed[...] * rows * scale), sums_o.shape)
+    along = rows * (scale * scale * scale * jnp.mean(scaled * rows, -1, keepdims=True))
+    block_o[...] = (scaled * scale - along + cotangent).astype(BF16)
+
+
+def input_call(mine, side, dnormed, layer_input, gain, cotangents):
+    rows, features = dnormed.shape
+    pieces = len(cotangents)
+    piece = cotangents[0].shape[0]
+    return pl.pallas_call(
+        input_kernel,
+        grid_spec=pltpu.PrefetchScalarGridSpec(
+            num_scalar_prefetch=1,
+            grid=(1,),
+            in_specs=[
+                pl.BlockSpec((rows, features), lambda i, place: (0, 0)),
+                pl.BlockSpec((rows, features), lambda i, place: (side * pieces + place[0], 0)),
+                pl.BlockSpec((1, features), lambda i, place: (0, 0)),
+            ]
+            + [pl.BlockSpec((piece, rows), lambda i, place: (0, side * pieces + place[0]))] * pieces,
+            out_specs=[
+                pl.BlockSpec((rows, features), lambda i, place: (0, 0)),
+                pl.BlockSpec((8, features), lambda i, place: (0, 0)),
+            ],
+            scratch_shapes=[pltpu.VMEM((pieces, piece, rows), F32)],
+        ),
+        out_shape=[jax.ShapeDtypeStruct((rows, features), BF16), jax.ShapeDtypeStruct((8, features), F32)],
+        compiler_params=pltpu.CompilerParams(
+            dimension_semantics=("arbitrary",), vmem_limit_bytes=60 * 1024 * 1024
+        ),
+        cost_estimate=pl.CostEstimate(flops=10**6, bytes_accessed=10**4, transcendentals=0),
+    )(mine[None].astype(jnp.int32), dnormed, layer_input, gain, *cotangents)
+
+
+def assemble_kernel(place, *refs):
+    blocks, out = refs[:-1], refs[-1]
+    pieces = len(blocks) // 2
+    here = pl.program_id(0)
+    wanted = here // pieces * pieces + (place[0] - here % pieces + pieces) % pieces
+    for at, block in enumerate(blocks):
+
+        @pl.when(wanted == at)
+        def _():
+            out[...] = block[...].astype(F32)
+
+
+def assemble_call(mine, blocks):
+    rows, features = blocks[0].shape
+    return pl.pallas_call(
+        assemble_kernel,
+        grid_spec=pltpu.PrefetchScalarGridSpec(
+            num_scalar_prefetch=1,
+            grid=(len(blocks),),
+            in_specs=[pl.BlockSpec((rows, features), lambda i, place: (0, 0))] * len(blocks),
+            out_specs=pl.BlockSpec((rows, features), lambda i, place: (i, 0)),
+        ),
+        out_shape=jax.ShapeDtypeStruct((rows * len(blocks), features), F32),
+        compiler_params=pltpu.CompilerParams(
+            dimension_semantics=("arbitrary",), vmem_limit_bytes=60 * 1024 * 1024
+        ),
+        cost_estimate=pl.CostEstimate(flops=10**6, bytes_accessed=10**4, transcendentals=0),
+    )(mine[None].astype(jnp.int32), *blocks)
+
+
+def call(kernel, blocks, ins, outs, scratch=(), backward=False, total=None, skipped=0):
+    steps_here = blocks
+
+    def spec(shape, kind, blocks=blocks, skipped=0):
         def at(i):
-            return blocks - 1 - i if backward else i
+            return skipped + (steps_here - 1 - i if backward else i)
 
         if kind == "rows":
             return pl.BlockSpec((shape[0] // blocks,) + shape[1:], lambda i: (at(i), 0))
         if kind == "stack":
             return pl.BlockSpec((1,) + shape[1:], lambda i: (at(i), 0, 0))
-        if kind == "mid":
-            return pl.BlockSpec((shape[0], shape[1] // blocks, shape[2]), lambda i: (0, at(i), 0))
+        if kind == "columns":
+            return pl.BlockSpec((shape[0], shape[1] // blocks), lambda i: (0, at(i)))
+        if kind == "last":
+            return pl.BlockSpec((shape[0], shape[1], shape[2] // blocks), lambda i: (0, 0, at(i)))
         return pl.BlockSpec(shape, lambda i: (0,) * len(shape))
 
-    moved = sum(a.size * a.dtype.itemsize for a, _ in ins)
     return pl.pallas_call(
         kernel,
         grid=(blocks,),
-        in_specs=[spec(a.shape, kind) for a, kind in ins],
+        in_specs=[spec(a.shape, kind, total or blocks, skipped) for a, kind in ins],
         out_specs=[spec(shape, kind) for shape, _, kind in outs],
         out_shape=[jax.ShapeDtypeStruct(shape, dtype) for shape, dtype, _ in outs],
         scratch_shapes=[pltpu.VMEM(shape, F32) for shape in scratch],
         compiler_params=pltpu.CompilerParams(
-            dimension_semantics=("arbitrary",), vmem_limit_bytes=48 * 1024 * 1024
+            dimension_semantics=("arbitrary",), vmem_limit_bytes=60 * 1024 * 1024
         ),
-        cost_estimate=pl.CostEstimate(flops=flops, bytes_accessed=moved, transcendentals=0),
+        cost_estimate=pl.CostEstimate(flops=10**6, bytes_accessed=10**4, transcendentals=0),
     )(*[a for a, _ in ins])
 
 
@@ -472,33 +624,29 @@
     all_width = width * pieces
     piece = output_grad.shape[1]
     rows = count // pieces
-    heads_pad = ((0, 0), (0, LANES - heads))
-
-    place = jnp.arange(BLOCK)
+
+    place = np.arange(BLOCK)
     keep = place[:, None] >= place[None, :]
-    lower = keep.astype(BF16)
-    hide = jnp.where(keep, 0.0, -1e30).astype(F32)
-    spread = (jnp.arange(LANES)[:, None] == (jnp.arange(width) // (width // heads))[None, :]).astype(BF16)
-    w_step_pad = jnp.pad(w_step, heads_pad)
-    step_bias_pad = jnp.pad(step_bias[None], heads_pad)
-    decay_pad = jnp.pad(decay_log[None], heads_pad)
-    taps = jnp.concatenate([conv_inner, conv_bc], 1)
-    bias = jnp.concatenate([conv_inner_bias, conv_bc_bias], 0)[None]
-    skip = jnp.repeat(skip_gain, width // heads)[None]
+    lower = jnp.asarray(keep, BF16)
+    hide = jnp.asarray(np.where(keep, 0.0, -1e30), F32)
+    spread = jnp.asarray(np.arange(LANES)[:, None] == (np.arange(width) // (width // heads))[None, :], BF16)
+    bias_row, decay_row, skip = step_bias[None], decay_log[None], skip_gain[None]
     gain_out_row = gain_out[None]
-    w_out_pieces = w_out.reshape(width, pieces, piece).transpose(1, 0, 2)
+    w_out_pieces = w_out.T.reshape(pieces, piece, width)
     owners = (mine - jnp.arange(pieces)) % pieces
     w_out_ring = jnp.take(w_out_pieces, owners, axis=0)
 
     halo = shifted(layer_input[count - EDGE :], "seq", 1)
-    cotangents = ring_gather(output_grad, "head")
+    halo, grad_columns = tie(halo, output_grad.T)
+    cotangents = [grad_columns, turn(grad_columns, "head", 1)]
 
     whole = lambda *arrays: [(a, "whole") for a in arrays]
-    normed, gate, pre, tot, raw, cum, cum_rows, local, payload = call(
+    normed, gate, pre, tot, raw, cum, cum_rows, local, payload, fine = call(
         forward_kernel,
         blocks,
         [(layer_input, "rows")]
-        + whole(halo, gain_in[None], w_gate, w_inner, w_bc, w_step_pad, taps, bias, step_bias_pad, decay_pad, lower, spread),
+        + whole(halo, gain_in[None], w_gate, w_inner, w_bc, w_step, conv_inner, conv_bc)
+        + whole(conv_inner_bias[None], conv_bc_bias[None], bias_row, decay_row, lower, spread),
         [
             ((count, features), BF16, "rows"),
             ((count, width), F32, "rows"),
@@ -508,52 +656,57 @@
             ((count, LANES), F32, "rows"),
             ((blocks, 8, BLOCK), F32, "stack"),
             ((blocks, width, states), F32, "stack"),
-            ((2, width + 16, states), BF16, "whole"),
+            ((width + 16, states), BF16, "whole"),
+            ((width, states), BF16, "whole"),
         ],
         [(8, both), (width, states), (16, LANES)],
-        flops=4 * 10**9,
-    )
-    incoming = joined_states(payload, "seq", width, heads, False)
+    )
+    payload, cotangents[1] = tie(payload, cotangents[1])
+    cotangents.append(turn(cotangents[1], "head", 1))
+    gathered = lax.all_gather(payload, "seq")
+    gathered, fine, cotangents[2] = tie(gathered, fine, cotangents[2])
+    incoming = joined_states(gathered, "seq", width, heads, False, lax.all_gather(fine, "seq"))
+    for _ in range(pieces - 3):
+        cotangents.append(turn(cotangents[-1], "head", 1))
     ssd, starts, squares = call(
         state_kernel,
         blocks,
         [(tot, "rows"), (raw, "rows"), (cum, "rows"), (cum_rows, "stack"), (gate, "rows"), (local, "stack")]
-        + whole(incoming, step_bias_pad, skip, hide, spread),
+        + whole(incoming, bias_row, skip, hide, spread),
         [
             ((count, width), F32, "rows"),
             ((blocks, width, states), F32, "stack"),
             ((blocks, 8, BLOCK), F32, "stack"),
         ],
         [(width, states)],
-        flops=3 * 10**9,
-    )
+    )
+    squares, cotangents[-1] = tie(squares, cotangents[-1])
     squares = small_sum(squares, "head")
-    normed_out, mixed_parts = call(
-        functools.partial(out_kernel, all_width),
-        blocks,
-        [(ssd, "rows"), (gate, "rows"), (squares, "stack")] + whole(gain_out_row, w_out_pieces),
-        [((count, width), BF16, "rows"), ((pieces, count, piece), BF16, "mid")],
-        flops=2 * 10**9,
-    )
     dn, cross = call(
         functools.partial(cross_kernel, pieces),
         blocks,
-        [(c, "rows") for c in cotangents]
+        [(c, "columns") for c in cotangents]
         + whole(w_out_ring)
         + [(ssd, "rows"), (gate, "rows")]
         + whole(gain_out_row),
         [((count, width), F32, "rows"), ((blocks, 8, BLOCK), F32, "stack")],
-        flops=2 * 10**9,
     )
     cross = small_sum(cross, "head")
-    summed = ring_scatter(lambda q: lax.dynamic_index_in_dim(mixed_parts, q, 0, False), "head")
-    residual = lax.dynamic_slice_in_dim(layer_input, mine * piece, piece, 1).astype(F32)
-    mixed = (residual + summed).astype(BF16)
+    squares_out, dn = tie(squares, dn)
+    normed_out, mixed_parts = call(
+        functools.partial(out_kernel, all_width),
+        blocks,
+        [(ssd, "rows"), (gate, "rows"), (squares_out, "stack")] + whole(gain_out_row, w_out_pieces),
+        [((count, width), BF16, "rows"), ((pieces, piece, count), BF16, "last")],
+    )
+    mixed_parts, cross = tie(mixed_parts, cross)
+    mixed_ring = ring_scatter(lambda q: lax.dynamic_index_in_dim(mixed_parts, q, 0, False), "head")
+    arrived = next(mixed_ring)
 
     dssd, dgate, local_back, payload_back, gw_out, gw_gate, gate_sums = call(
         functools.partial(gate_kernel, pieces, all_width),
         blocks,
-        [(c, "rows") for c in cotangents]
+        [(c, "columns") for c in cotangents]
         + [(a, "rows") for a in (ssd, gate, dn, tot, cum, normed, normed_out)]
         + [(squares, "stack"), (cross, "stack")]
         + whole(gain_out_row, spread),
@@ -561,80 +714,98 @@
             ((count, width), F32, "rows"),
             ((count, width), BF16, "rows"),
             ((blocks, width, states), F32, "stack"),
-            ((2, width + 16, states), BF16, "whole"),
-            ((pieces, width, piece), F32, "whole"),
+            ((width + 16, states), BF16, "whole"),
+            ((pieces, piece, width), F32, "whole"),
             ((features, width), F32, "whole"),
             ((8, width), F32, "whole"),
         ],
         [(width, states), (16, LANES)],
         backward=True,
-        flops=4 * 10**9,
-    )
-    gw_out, gw_gate = lax.psum((gw_out, gw_gate), "seq")
-    outgoing = joined_states(payload_back, "seq", width, heads, True)
+    )
+    payload_back, arrived = tie(payload_back, arrived)
+    for _ in range(pieces - 3):
+        arrived = mixed_ring.send(arrived)
+    outgoing = joined_states(lax.all_gather(payload_back, "seq"), "seq", width, heads, True)
     d, draw, rate_sums = call(
         pull_kernel,
         blocks,
         [(tot, "rows"), (raw, "rows"), (cum, "rows"), (cum_rows, "stack"), (dssd, "rows"), (starts, "stack"), (local_back, "stack")]
-        + whole(outgoing, step_bias_pad, decay_pad, skip, lower, hide, spread),
+        + whole(outgoing, bias_row, decay_row, skip, lower, hide, spread),
         [((count, both), F32, "rows"), ((count, LANES), F32, "rows"), ((8, LANES), F32, "whole")],
         [(width, states)],
         backward=True,
-        flops=8 * 10**9,
-    )
-    d_halo = shifted(d[:8], "seq", -1)
-    part, gw_inner, gw_bc, gw_step, conv_sums = call(
-        project_kernel,
-        blocks,
-        [(d, "rows")]
-        + whole(d_halo)
-        + [(pre, "rows"), (normed, "rows"), (dgate, "rows"), (draw, "rows")]
-        + whole(taps, w_gate, w_inner, w_bc, w_step_pad),
-        [
-            ((count, features), BF16, "rows"),
-            ((features, width), F32, "whole"),
-            ((features, 2 * states), F32, "whole"),
-            ((features, LANES), F32, "whole"),
-            ((8, both), F32, "whole"),
-        ],
-        [(8, both)],
-        backward=True,
-        flops=8 * 10**9,
-    )
-    dnormed = ring_scatter(lambda q: lax.dynamic_slice_in_dim(part, q * rows, rows, 0), "head")
-
-    layer_x = lax.dynamic_slice_in_dim(layer_input, mine * rows, rows, 0).astype(F32)
-    own = [lax.dynamic_slice_in_dim(c, mine * rows, rows, 0) for c in cotangents]
-    cotangent = jnp.take(jnp.stack(own), owners, axis=0).transpose(1, 0, 2).reshape(rows, features).astype(F32)
-    scale_in = lax.rsqrt(jnp.mean(layer_x * layer_x, -1, keepdims=True) + eps)
-    scaled_in = dnormed * gain_in
-    gain_part = jnp.sum(dnormed * layer_x * scale_in, 0)
-    own_input = scaled_in * scale_in - layer_x * scale_in**3 * jnp.mean(scaled_in * layer_x, -1, keepdims=True)
-    own_input = (own_input + cotangent).astype(BF16)
-    grad_input = jnp.zeros((count, features), F32)
-    for step, block in enumerate(ring_gather(own_input, "head")):
-        owner = (mine - step) % pieces
-        grad_input = lax.dynamic_update_slice_in_dim(grad_input, block.astype(F32), owner * rows, 0)
-
-    gw_out = jnp.take(gw_out, owners, axis=0).transpose(1, 0, 2).reshape(width, features)
-    (gw_inner, gw_bc, gw_step), gw_gate, gw_out = lax.optimization_barrier(
-        ((gw_inner, gw_bc, gw_step), gw_gate, gw_out)
-    )
-    gw_inner, gw_bc, gw_step = lax.psum((gw_inner, gw_bc, gw_step[:, :heads]), "seq")
-    seq_count, seq_mine = lax.axis_size("seq"), lax.axis_index("seq")
-    share = features // seq_count
-    bc_share = lax.dynamic_slice_in_dim(gw_bc, seq_mine * share, share, 0)
-    gw_bc = lax.all_gather(small_sum(bc_share, "head"), "seq", axis=0, tiled=True)
-    small = [conv_sums, gate_sums, rate_sums]
-    packed = butterfly(jnp.concatenate([v.reshape(-1, LANES) for v in small], 0), "seq")
-    split, at = [], 0
-    for v in small:
-        split.append(packed[at : at + v.size // LANES].reshape(v.shape))
-        at += v.size // LANES
-    conv_sums, gate_sums, rate_sums = split
-    shared = jnp.concatenate([v.reshape(-1, LANES) for v in (conv_sums[:, width:] / seq_count, gain_part)], 0)
-    shared = butterfly(butterfly(shared, "seq"), "head")
-    bc_sums, grad_gain_in = shared[: 4 * states // LANES * 4].reshape(8, 2 * states), shared[16 * states // LANES :].reshape(-1)
+    )
+    d, arrived = tie(d, arrived)
+    arrived = mixed_ring.send(arrived)
+
+    half, half_rows = count // 2, rows // 2
+    halo_d = shifted(d[:8], "seq", -1)
+    shares, totals = [None, None], []
+    for side in (1, 0):
+        part, *totals = call(
+            functools.partial(project_kernel, len(totals)),
+            blocks // 2,
+            [(d, "rows")]
+            + whole(halo_d)
+            + [(pre, "rows"), (normed, "rows"), (dgate, "rows"), (draw, "rows")]
+            + whole(gate_sums, rate_sums, conv_inner, conv_bc, w_gate, w_inner, w_bc, w_step, *totals),
+            [
+                ((half, features), BF16, "rows"),
+                ((features, width), F32, "whole"),
+                ((features, 2 * states), F32, "whole"),
+                ((16, max(features, both)), F32, "whole"),
+            ],
+            [(8, both)],
+            backward=True,
+            total=blocks,
+            skipped=side * (blocks // 2),
+        )
+        halo_d = d[half : half + 8]
+        if side:
+            d, arrived = tie(d, arrived)
+        shares[side] = ring_scatter(
+            lambda q, part=part: lax.dynamic_slice_in_dim(part, q * half_rows, half_rows, 0), "head"
+        )
+        running = next(shares[side])
+        if side:
+            first = running
+        else:
+            first, part = tie(first, part)
+    gw_inner, gw_bc, conv_sums = totals
+    gw_out, gw_gate = lax.psum((gw_out, gw_gate), "seq")
+
+    gain_row = gain_in[None]
+    runs, blocks_of, sums = {1: first, 0: running}, {}, {}
+    for step in range(pieces - 1):
+        for side in (1, 0):
+            runs[side] = shares[side].send(runs[side])
+    runs[1], gw_inner, gw_bc, conv_sums, arrived, layer_late = tie(
+        runs[1], gw_inner, gw_bc, conv_sums, arrived, layer_input
+    )
+    chores = Chores(weight_chores(gw_inner, gw_bc, conv_sums, width))
+    for side in (1, 0):
+        blocks_of[side], sums[side] = input_call(mine, side, runs[side], layer_input, gain_row, cotangents)
+    summed = mixed_ring.send(arrived)
+    residual = lax.dynamic_slice_in_dim(layer_late, mine * piece, piece, 1).astype(F32)
+    mixed = (residual.T + summed).astype(BF16).T
+
+    arrivals = {side: [blocks_of[side]] for side in (0, 1)}
+    for step in range(1, pieces):
+        for side in (1, 0):
+            blocks_of[side] = turn(blocks_of[side], "head", 1)
+            blocks_of[side] = chores.beside(blocks_of[side])
+            if step == 1 and side:
+                blocks_of[1], gain_part = tie(blocks_of[1], (sums[0] + sums[1])[0].reshape(-1, LANES))
+                gains = Chores(gain_chores((gain_part,)))
+            else:
+                blocks_of[side] = gains.beside(blocks_of[side])
+            arrivals[side].append(blocks_of[side])
+            if step == pieces - 2 and not side:
+                blocks_of[0], gw_out = tie(blocks_of[0], gw_out)
+    grad_input = assemble_call(mine, arrivals[0] + arrivals[1])
+    gw_inner, gw_bc, sums, bc_sums = chores.finish()
+    grad_gain_in = gains.finish()[0].reshape(-1)
+    gw_out = jnp.take(gw_out, owners, axis=0).reshape(features, width).T
     head_dim = width // heads
     return (
         mixed,
@@ -643,15 +814,15 @@
         gw_gate,
         gw_inner,
         gw_bc,
-        gw_step,
-        conv_sums[:kernel, :width],
-        conv_sums[kernel, :width],
+        sums[8 : 8 + heads, :features].T,
+        sums[:kernel, :width],
+        sums[kernel, :width],
         bc_sums[:kernel],
         bc_sums[kernel],
-        rate_sums[0, :heads],
-        rate_sums[1, :heads],
-        gate_sums[1].reshape(heads, head_dim).sum(1),
-        gate_sums[0],
+        sums[kernel + 1, width : width + heads],
+        sums[kernel + 2, width : width + heads],
+        sums[kernel + 2, :width].reshape(heads, head_dim).sum(1),
+        sums[kernel + 1, :width],
         gw_out,
     )
 

time: 494 us -> 375 us (0.76)
  local copies, waits for them, and re-layouts: 76.9 us -> 27.8 us
  waiting for transfers between devices: 130 us -> 83.1 us
  blocking collectives: 78.9 us -> 35.5 us
  Pallas kernels: 108 us -> 132 us
  other arithmetic: 44.2 us -> 32.3 us
  starting transfers between devices: 38 us -> 47.4 us
    psum x1 -> x0, waiting for transfers between devices: 30.2 us -> none  [per_device(): lax.psum((gw_inner, gw_bc, gw_step[:, :heads]), 'seq')]
    psum x1, waiting for transfers between devices: 29.8 us -> 0.01 us  [per_device(): gw_out, gw_gate = lax.psum((gw_out, gw_gate), 'seq')]
    psum x1 -> x0, blocking collectives: 26.8 us -> none  [per_device(): lax.psum((gw_inner, gw_bc, gw_step[:, :heads]), 'seq')]
    ppermute x8 -> x18, waiting for transfers between devices: 2.76 us -> 28.6 us  [the longest x6 15.8 us: halved(): lax.ppermute(sent, axis, [(i, i ^ reach) for i in range(count)])]
    pallas_call x7 -> x11, Pallas kernels: 108 us -> 132 us  [the longest x8 121 us: call(): pl.pallas_call(kernel, grid=(blocks,), in_specs=[spec(a.shape, kind, tota...]
    unnamed x124 -> x60, local copies, waits for them, and re-layouts: 28 us -> 4.51 us
    all_gather x5 -> x3, blocking collectives: 52 us -> 35.5 us  [the longest x1 14.2 us: per_device(): gathered = lax.all_gather(payload, 'seq')]
    ppermute x21 -> x30, waiting for transfers between devices: 66.8 us -> 51.9 us  [turn(): lax.ppermute(block, axis, [(i, (i + distance) % count) for i in range(cou...]
  transfers between devices with their start and end apart: 33 -> 51, of which waited for: 13 -> 21; matrix products, arithmetic and copies ran while one was open for 19% -> 13% of each run, Pallas kernels for 13% -> 35%
where the time goes in v2:
time: 375 us; the launch traced here: 373 us
  Pallas kernels  132 us (35%)
  waiting for transfers between devices  83.1 us (22%)
  starting transfers between devices  47.4 us (13%)
  blocking collectives  35.5 us (9%)
  other arithmetic  32.3 us (9%)
  local copies, waits for them, and re-layouts  27.8 us (7%)
  between operations  14.7 us (4%)
    pallas_call x8, Pallas kernels, call(): pl.pallas_call(kernel, grid=(blocks,), in_specs=[spec(a.shape, kind, tota...  121 us
    ppermute x30, waiting for transfers between devices, turn(): lax.ppermute(block, axis, [(i, (i + distance) % count) for i in range(cou...  51.9 us
    ppermute x30, starting transfers between devices, turn(): lax.ppermute(block, axis, [(i, (i + distance) % count) for i in range(cou...  28.5 us
    ppermute x6, waiting for transfers between devices, halved(): lax.ppermute(sent, axis, [(i, i ^ reach) for i in range(count)])  15.8 us
    all_gather x1, blocking collectives, per_device(): gathered = lax.all_gather(payload, 'seq')  14.2 us
    ppermute x6, waiting for transfers between devices, doubled(): other = lax.ppermute(value, axis, [(i, i ^ reach) for i in range(count)])  11.8 us
    all_gather x1, blocking collectives, per_device(): lax.all_gather(fine, 'seq')  11.6 us
    all_gather x1, blocking collectives, per_device(): lax.all_gather(payload_back, 'seq')  9.75 us
  transfers between devices with their start and end apart: 51, of which 21 were waited for; matrix products, arithmetic and copies ran while one was open for 13% of the time, Pallas kernels for 35%

profile of v2, /device:TPU:0, one launch (start us, length us, event | category | flops | bytes accessed | tf_op | source)
XLA Modules:
  0.0 373.1 jit_solution(3644542385763559039)
XLA Ops:
  8.0 2.3 collective-permute-start
  11.2 2.4 collective-permute-start.1
  17.6 19.2 %shard_map.306 = (bf16[2048,768]{1,0:T(8,128)(2,1)}, f32[2048,384]{1,0:T(8,128)}, f32[2048,640]{1,0:T(8,128)}, f32[2048,640]{1,0:T(8,128)}, f32[2048,128]{1,0:T(...) custom-call(bf16[2048,768]{1,0:T(8,128)(2,1)} %x.5, ...), custom_call_target="tpu_custom_call" | custom-call | flops 1000000 | bytes 10000 | tf_op jit(solution)/shard_map/pallas_call | solution.py:599
  40.4 14.2 %all-gather = bf16[3200,128]{1,0:T(8,128)(2,1)S(1)} all-gather(bf16[400,128]{1,0:T(8,128)(2,1)S(1)} %copy-done.17), channel_id=2, replica_groups=mesh['seq'=8,'head'=4] {'seq'}, dimensions={0}, use_global_device_ids=true | all-gather | bytes 921600 | tf_op jit(solution)/shard_map/all_gather | solution.py:666
  54.6 4.0 %collective-permute-done.2.refs_2_ = bf16[192,2048]{1,0:T(8,128)(2,1)S(1)} collective-permute-done((bf16[192,2048]{1,0:T(8,128)(2,1)S(1)}, bf16[192,2048]{1,0:T(8,128)(2,1)S(1)}, u32[]{:S(2)}, u32[]{:S(2)}) %collective-permute-start.2) | collective-permute-done | bytes 786464 | tf_op jit(solution)/shard_map/ppermute | solution.py:19
  58.9 11.6 %all-gather.1 = bf16[3072,128]{1,0:T(8,128)(2,1)S(1)} all-gather(bf16[384,128]{1,0:T(8,128)(2,1)S(1)} %copy-done.19), channel_id=3, replica_groups=mesh['seq'=8,'head'=4] {'seq'}, dimensions={0}, use_global_device_ids=true | all-gather | bytes 884736 | tf_op jit(solution)/shard_map/all_gather | solution.py:668
  70.7 2.0 fusion.2.incoming
  72.7 14.0 %shard_map.307 = (f32[2048,384]{1,0:T(8,128)}, f32[8,384,128]{2,1,0:T(8,128)}, f32[8,8,256]{2,1,0:T(8,128)}) custom-call(f32[2048,640]{1,0:T(8,128)} %get-tuple-element.115.tot.refs_7_, f32[2048,128]{1,0:T(8,128)} %get-tuple-element.116.raw, f32[2048,128]{1,0:T(8,128)} %get-tuple-element.117.cum_in.refs_8_, f32[8,8,256]{2,1,0:T(8,128)} %get-tuple-element.118.cum_rows, ...), custom_call_target="tpu_custom_call" | custom-call | flops 1000000 | bytes 10000 | tf_op jit(solution)/shard_map/pallas_call | solution.py:599
  88.1 3.0 collective-permute-start.5
  92.7 10.0 %shard_map.308 = (f32[2048,384]{1,0:T(8,128)}, f32[8,8,256]{2,1,0:T(8,128)}) custom-call(bf16[192,2048]{1,0:T(8,128)(2,1)} %bitcast.82, bf16[192,2048]{1,0:T(8,128)(2,1)} %copy-done.1, bf16[192,2048]{1,0:T(8,128)(2,1)} %copy-done.2, bf16[192,2048]{1,0:T(8,128)(2,1)} %copy-done.3, bf16[4,192,384]{2,1,0:T(8,128)(2,1)} %broadcast_select_fusion.refs_4_, ...), custom_call_target="tpu_custom_call" | custom-call | flops 1000000 | bytes 10000 | tf_op jit(solution)/shard_map/pallas_call | solution.py:599
  102.7 2.0 collective-permute-start.7
  104.7 2.4 collective-permute-start.9
  107.8 9.8 %shard_map.309 = (bf16[2048,384]{1,0:T(8,128)(2,1)}, bf16[4,192,2048]{2,1,0:T(8,128)(2,1)}) custom-call(f32[2048,384]{1,0:T(8,128)} %get-tuple-element.131.refs_5_.ssd.refs_4_, f32[2048,384]{1,0:T(8,128)} %get-tuple-element.125.gate.refs_6_.refs_5_, f32[8,8,256]{2,1,0:T(8,128)} %add_add_fusion.2.squares.refs_11_, ...), custom_call_target="tpu_custom_call" | custom-call | flops 1000000 | bytes 10000 | tf_op jit(solution)/shard_map/pallas_call | solution.py:599
  119.6 17.6 %shard_map.310 = (f32[2048,384]{1,0:T(8,128)}, bf16[2048,384]{1,0:T(8,128)(2,1)}, f32[8,384,128]{2,1,0:T(8,128)}, bf16[400,128]{1,0:T(8,128)(2,1)}, f32[4,192,38...) custom-call(bf16[192,2048]{1,0:T(8,128)(2,1)} %bitcast.83, bf16[192,2048]{1,0:T(8,128)(2,1)} %copy-done.1, ...), custom_call_target="tpu_custom_call" | custom-call | flops 1000000 | bytes 10000 | tf_op jit(solution)/shard_map/pallas_call | solution.py:599
  137.2 2.5 collective-permute-done.10
  141.2 9.8 %all-gather.2 = bf16[3200,128]{1,0:T(8,128)(2,1)S(1)} all-gather(bf16[400,128]{1,0:T(8,128)(2,1)S(1)} %copy-done.18), channel_id=4, replica_groups=mesh['seq'=8,'head'=4] {'seq'}, dimensions={0}, use_global_device_ids=true | all-gather | bytes 921600 | tf_op jit(solution)/shard_map/all_gather | solution.py:728
  152.6 27.1 %shard_map.311 = (f32[2048,640]{1,0:T(8,128)}, f32[2048,128]{1,0:T(8,128)}, f32[8,128]{1,0:T(8,128)}) custom-call(f32[2048,640]{1,0:T(8,128)} %get-tuple-element.115.tot.refs_7_, f32[2048,128]{1,0:T(8,128)} %get-tuple-element.116.raw, f32[2048,128]{1,0:T(8,128)} %get-tuple-element.117.cum_in.refs_8_, f32[8,8,256]{2,1,0:T(8,128)} %get-tuple-element.118.cum_rows, ...), custom_call_target="tpu_custom_call" | custom-call | flops 1000000 | bytes 10000 | tf_op jit(solution)/shard_map/pallas_call | solution.py:599
  186.8 11.2 %shard_map.312 = (bf16[1024,768]{1,0:T(8,128)(2,1)}, f32[768,384]{1,0:T(8,128)}, f32[768,256]{1,0:T(8,128)}, f32[16,768]{1,0:T(8,128)}) custom-call(f32[2048,640]{1,0:T(8,128)} %get-tuple-element.157.d, f32[8,640]{1,0:T(8,128)} %copy-done.24, f32[2048,640]{1,0:T(8,128)} %get-tuple-element.150.pre, bf16[2048,768]{1,0:T(8,128)(2,1)} %get-tuple-element.135.refs_9_.normed, ...), custom_call_target="tpu_custom_call" | custom-call | flops 1000000 | bytes 10000 | tf_op jit(solution)/shard_map/pallas_call | solution.py:599
  199.8 1.9 collective-permute-start.13
  204.0 12.0 %shard_map.313 = (bf16[1024,768]{1,0:T(8,128)(2,1)}, f32[768,384]{1,0:T(8,128)}, f32[768,256]{1,0:T(8,128)}, f32[16,768]{1,0:T(8,128)}) custom-call(f32[2048,640]{1,0:T(8,128)} %get-tuple-element.157.d, f32[8,640]{1,0:T(8,128)} %get-tuple-element.217.halo, f32[2048,640]{1,0:T(8,128)} %get-tuple-element.150.pre, ...), custom_call_target="tpu_custom_call" | custom-call | flops 1000000 | bytes 10000 | tf_op jit(solution)/shard_map/pallas_call | solution.py:599
  216.0 1.9 constant_dynamic-slice_fusion
  219.8 12.1 %collective-permute-done.17 = bf16[256,768]{1,0:T(8,128)(2,1)} collective-permute-done((bf16[256,768]{1,0:T(8,128)(2,1)}, bf16[256,768]{1,0:T(8,128)(2,1)}, u32[]{:S(2)}, u32[]{:S(2)}) %collective-permute-start.17) | collective-permute-done | bytes 393248 | tf_op jit(solution)/shard_map/ppermute | solution.py:19
  231.9 1.8 add_convert_fusion.1
  233.8 6.5 %collective-permute-done.15 = bf16[256,768]{1,0:T(8,128)(2,1)S(1)} collective-permute-done((bf16[256,768]{1,0:T(8,128)(2,1)}, bf16[256,768]{1,0:T(8,128)(2,1)S(1)}, u32[]{:S(2)}, u32[]{:S(2)}) %collective-permute-start.15) | collective-permute-done | bytes 393248 | tf_op jit(solution)/shard_map/ppermute | solution.py:19
  241.1 7.7 %collective-permute-done.18 = bf16[256,768]{1,0:T(8,128)(2,1)} collective-permute-done((bf16[256,768]{1,0:T(8,128)(2,1)}, bf16[256,768]{1,0:T(8,128)(2,1)}, u32[]{:S(2)}, u32[]{:S(2)}) %collective-permute-start.18) | collective-permute-done | bytes 393248 | tf_op jit(solution)/shard_map/ppermute | solution.py:19
  250.6 6.5 %collective-permute-done.16 = bf16[256,768]{1,0:T(8,128)(2,1)S(1)} collective-permute-done((bf16[256,768]{1,0:T(8,128)(2,1)}, bf16[256,768]{1,0:T(8,128)(2,1)S(1)}, u32[]{:S(2)}, u32[]{:S(2)}) %collective-permute-start.16) | collective-permute-done | bytes 393248 | tf_op jit(solution)/shard_map/ppermute | solution.py:19
  259.6 2.8 shard_map.315
  263.1 2.2 collective-permute-done.19
  265.3 2.0 convert_add_fusion.3.dnormed
  267.3 2.8 shard_map.314
  273.1 3.3 collective-permute-done.21.refs_5_
  277.6 2.7 collective-permute-start.30
  280.3 2.0 collective-permute-start.27
  282.4 2.3 collective-permute-done.28
  287.3 5.2 %collective-permute-done.26 = f32[192,256]{1,0:T(8,128)S(1)} collective-permute-done((f32[192,256]{1,0:T(8,128)S(1)}, f32[192,256]{1,0:T(8,128)S(1)}, u32[]{:S(2)}, u32[]{:S(2)}) %collective-permute-start.26) | collective-permute-done | bytes 196640 | tf_op jit(solution)/shard_map/ppermute | solution.py:48
  292.5 5.2 %collective-permute-done.25 = f32[192,384]{1,0:T(8,128)S(1)} collective-permute-done((f32[192,384]{1,0:T(8,128)S(1)}, f32[192,384]{1,0:T(8,128)S(1)}, u32[]{:S(2)}, u32[]{:S(2)}) %collective-permute-start.25) | collective-permute-done | bytes 294944 | tf_op jit(solution)/shard_map/ppermute | solution.py:48
  303.4 3.0 collective-permute-done.34
  306.4 2.5 collective-permute-done.33
  310.5 1.9 collective-permute-start.37
  316.7 2.9 copy.68
  325.2 2.9 fusion.7
  329.0 2.0 collective-permute-done.43
  331.0 3.2 collective-permute-done.42.refs_7_
  336.8 5.2 %collective-permute-done.46 = f32[192,256]{1,0:T(8,128)S(1)} collective-permute-done((f32[192,256]{1,0:T(8,128)S(1)}, f32[192,256]{1,0:T(8,128)S(1)}, u32[]{:S(2)}, u32[]{:S(2)}) %collective-permute-start.46) | collective-permute-done | bytes 196640 | tf_op jit(solution)/shard_map/ppermute | solution.py:53
  342.0 4.6 %collective-permute-done.45 = f32[192,384]{1,0:T(8,128)S(1)} collective-permute-done((f32[192,384]{1,0:T(8,128)S(1)}, f32[192,384]{1,0:T(8,128)S(1)}, u32[]{:S(2)}, u32[]{:S(2)}) %collective-permute-start.45) | collective-permute-done | bytes 294944 | tf_op jit(solution)/shard_map/ppermute | solution.py:53
  354.9 5.9 %shard_map.316 = f32[2048,768]{1,0:T(8,128)} custom-call(s32[1]{0:T(128)} %bitcast.21.place, bf16[256,768]{1,0:T(8,128)(2,1)} %get-tuple-element.169.refs_0_, bf16[256,768]{1,0:T(8,128)(2,1)} %collective-permute-done.20.refs_1_, bf16[256,768]{1,0:T(8,128)(2,1)} %collective-permute-done.31.refs_2_, bf16[256,768]{1,0:T(8,128)(2,1)} %copy-done.16, ...), custom_call_target="tpu_custom_call" | custom-call | flops 1000000 | bytes 10000 | tf_op jit(solution)/shard_map/pallas_call | solution.py:566
  360.7 2.1 maximum_select_fusion.1
  362.8 2.5 maximum_select_fusion
  (219 shorter events, 73.9 us)
Async XLA Ops:
  7.2 320.9 %all-reduce.3.cloned.1.call-start = ((), (), s32[]{:S(2)}) async-start(), calls=%async_computation | async-start | bytes 4718592 | tf_op jit(solution)/shard_map/psum | solution.py:775
  11.2 25.7 %collective-permute-start.1 = (bf16[192,2048]{1,0:T(8,128)(2,1)}, bf16[192,2048]{1,0:T(8,128)(2,1)S(1)}, u32[]{:S(2)}, u32[]{:S(2)}) collective-permute-start(bf16[192,2048]{1,0:T(8,128)(2,1)} %bitcast.81), channel_id=1, source_target_pairs={{0,1},{1,2},{2,3},{3,0},{4,5},{5,6},{6,7},{7,4},{8,9},{9,10},{10,1... | collective-permute-start | bytes 2359304 | tf_op jit(solution)/shard_map/ppermute | solution.py:19
  36.9 21.7 %collective-permute-start.2 = (bf16[192,2048]{1,0:T(8,128)(2,1)S(1)}, bf16[192,2048]{1,0:T(8,128)(2,1)S(1)}, u32[]{:S(2)}, u32[]{:S(2)}) collective-permute-start(bf16[192,2048]{1,0:T(8,128)(2,1)S(1)} %collective-permute-done.1.refs_1_), channel_id=1, source_target_pairs={{0,1},{1,2},{2,3},{3,0},{4,5},{5,6},{6,7},{7,4},{8,9},{9,10},{10,1... | collective-permute-start | bytes 2359304 | tf_op jit(solution)/shard_map/ppermute | solution.py:19
  58.8 27.9 %collective-permute-start.3 = (bf16[192,2048]{1,0:T(8,128)(2,1)S(1)}, bf16[192,2048]{1,0:T(8,128)(2,1)S(1)}, u32[]{:S(2)}, u32[]{:S(2)}) collective-permute-start(bf16[192,2048]{1,0:T(8,128)(2,1)S(1)} %collective-permute-done.2.refs_2_), channel_id=1, source_target_pairs={{0,1},{1,2},{2,3},{3,0},{4,5},{5,6},{6,7},{7,4},{8,9},{9,10},{10,1... | collective-permute-start | bytes 2359304 | tf_op jit(solution)/shard_map/ppermute | solution.py:19
  86.7 18.0 %collective-permute-start.4 = (f32[8,8,256]{2,1,0:T(8,128)}, f32[8,8,256]{2,1,0:T(8,128)S(1)}, u32[]{:S(2)}, u32[]{:S(2)}) collective-permute-start(f32[8,8,256]{2,1,0:T(8,128)} %get-tuple-element.132), channel_id=1, source_target_pairs={{0,1},{1,2},{2,3},{3,0},{4,5},{5,6},{6,7},{7,4},{8,9},{9,10},{10,1... | collective-permute-start | bytes 196616 | tf_op jit(solution)/shard_map/ppermute | solution.py:19
  88.1 19.1 %collective-permute-start.5 = (f32[8,8,256]{2,1,0:T(8,128)}, f32[8,8,256]{2,1,0:T(8,128)S(1)}, u32[]{:S(2)}, u32[]{:S(2)}) collective-permute-start(f32[8,8,256]{2,1,0:T(8,128)} %get-tuple-element.132), channel_id=1, source_target_pairs={{0,2},{1,3},{2,0},{3,1},{4,6},{5,7},{6,4},{7,5},{8,10},{9,11},{10,... | collective-permute-start | bytes 196616 | tf_op jit(solution)/shard_map/ppermute | solution.py:19
  91.1 16.0 %collective-permute-start.6 = (f32[8,8,256]{2,1,0:T(8,128)}, f32[8,8,256]{2,1,0:T(8,128)S(1)}, u32[]{:S(2)}, u32[]{:S(2)}) collective-permute-start(f32[8,8,256]{2,1,0:T(8,128)} %get-tuple-element.132), channel_id=1, source_target_pairs={{0,3},{1,0},{2,1},{3,2},{4,7},{5,4},{6,5},{7,6},{8,11},{9,8},{10,9... | collective-permute-start | bytes 196616 | tf_op jit(solution)/shard_map/ppermute | solution.py:19
  102.7 14.9 %collective-permute-start.7 = (f32[8,8,256]{2,1,0:T(8,128)}, f32[8,8,256]{2,1,0:T(8,128)S(1)}, u32[]{:S(2)}, u32[]{:S(2)}) collective-permute-start(f32[8,8,256]{2,1,0:T(8,128)} %get-tuple-element.139), channel_id=1, source_target_pairs={{0,1},{1,2},{2,3},{3,0},{4,5},{5,6},{6,7},{7,4},{8,9},{9,10},{10,1... | collective-permute-start | bytes 196616 | tf_op jit(solution)/shard_map/ppermute | solution.py:19
  104.7 12.9 %collective-permute-start.8 = (f32[8,8,256]{2,1,0:T(8,128)}, f32[8,8,256]{2,1,0:T(8,128)S(1)}, u32[]{:S(2)}, u32[]{:S(2)}) collective-permute-start(f32[8,8,256]{2,1,0:T(8,128)} %get-tuple-element.139), channel_id=1, source_target_pairs={{0,2},{1,3},{2,0},{3,1},{4,6},{5,7},{6,4},{7,5},{8,10},{9,11},{10,... | collective-permute-start | bytes 196616 | tf_op jit(solution)/shard_map/ppermute | solution.py:19
  104.7 12.9 %collective-permute-start.9 = (f32[8,8,256]{2,1,0:T(8,128)}, f32[8,8,256]{2,1,0:T(8,128)S(1)}, u32[]{:S(2)}, u32[]{:S(2)}) collective-permute-start(f32[8,8,256]{2,1,0:T(8,128)} %get-tuple-element.139), channel_id=1, source_target_pairs={{0,3},{1,0},{2,1},{3,2},{4,7},{5,4},{6,5},{7,6},{8,11},{9,8},{10,9... | collective-permute-start | bytes 196616 | tf_op jit(solution)/shard_map/ppermute | solution.py:19
  119.4 20.2 %collective-permute-start.10 = (bf16[192,2048]{1,0:T(8,128)(2,1)S(1)}, bf16[192,2048]{1,0:T(8,128)(2,1)S(1)}, u32[]{:S(2)}, u32[]{:S(2)}) collective-permute-start(bf16[192,2048]{1,0:T(8,128)(2,1)S(1)} %dynamic-slice_bitcast_fusion), channel_id=1, source_target_pairs={{0,1},{1,2},{2,3},{3,0},{4,5},{5,6},{6,7},{7,4},{8,9},{9,10},{10,1... | collective-permute-start | bytes 2359304 | tf_op jit(solution)/shard_map/ppermute | solution.py:19
  141.1 38.7 %collective-permute-start.11 = (bf16[192,2048]{1,0:T(8,128)(2,1)S(1)}, bf16[192,2048]{1,0:T(8,128)(2,1)S(1)}, u32[]{:S(2)}, u32[]{:S(2)}) collective-permute-start(bf16[192,2048]{1,0:T(8,128)(2,1)S(1)} %fusion.6), channel_id=1, source_target_pairs={{0,1},{1,2},{2,3},{3,0},{4,5},{5,6},{6,7},{7,4},{8,9},{9,10},{10,1... | collective-permute-start | bytes 2359304 | tf_op jit(solution)/shard_map/ppermute | solution.py:19
  181.2 21.9 %collective-permute-start.14 = (bf16[192,2048]{1,0:T(8,128)(2,1)S(1)}, bf16[192,2048]{1,0:T(8,128)(2,1)S(1)}, u32[]{:S(2)}, u32[]{:S(2)}) collective-permute-start(bf16[192,2048]{1,0:T(8,128)(2,1)S(1)} %fusion.5), channel_id=1, source_target_pairs={{0,1},{1,2},{2,3},{3,0},{4,5},{5,6},{6,7},{7,4},{8,9},{9,10},{10,1... | collective-permute-start | bytes 2359304 | tf_op jit(solution)/shard_map/ppermute | solution.py:19
  199.8 19.2 %collective-permute-start.13 = (bf16[256,768]{1,0:T(8,128)(2,1)}, bf16[256,768]{1,0:T(8,128)(2,1)S(1)}, u32[]{:S(2)}, u32[]{:S(2)}) collective-permute-start(bf16[256,768]{1,0:T(8,128)(2,1)} %constant_dynamic-slice_fusion.1), channel_id=1, source_target_pairs={{0,1},{1,2},{2,3},{3,0},{4,5},{5,6},{6,7},{7,4},{8,9},{9,10},{10,1... | collective-permute-start | bytes 1179656 | tf_op jit(solution)/shard_map/ppermute | solution.py:19
  217.8 14.1 %collective-permute-start.17 = (bf16[256,768]{1,0:T(8,128)(2,1)}, bf16[256,768]{1,0:T(8,128)(2,1)}, u32[]{:S(2)}, u32[]{:S(2)}) collective-permute-start(bf16[256,768]{1,0:T(8,128)(2,1)} %constant_dynamic-slice_fusion), channel_id=1, source_target_pairs={{0,1},{1,2},{2,3},{3,0},{4,5},{5,6},{6,7},{7,4},{8,9},{9,10},{10,1... | collective-permute-start | bytes 1179656 | tf_op jit(solution)/shard_map/ppermute | solution.py:19
  219.8 20.5 %collective-permute-start.15 = (bf16[256,768]{1,0:T(8,128)(2,1)}, bf16[256,768]{1,0:T(8,128)(2,1)S(1)}, u32[]{:S(2)}, u32[]{:S(2)}) collective-permute-start(bf16[256,768]{1,0:T(8,128)(2,1)} %add_convert_fusion.3), channel_id=1, source_target_pairs={{0,1},{1,2},{2,3},{3,0},{4,5},{5,6},{6,7},{7,4},{8,9},{9,10},{10,1... | collective-permute-start | bytes 1179656 | tf_op jit(solution)/shard_map/ppermute | solution.py:19
  233.8 15.0 %collective-permute-start.18 = (bf16[256,768]{1,0:T(8,128)(2,1)}, bf16[256,768]{1,0:T(8,128)(2,1)}, u32[]{:S(2)}, u32[]{:S(2)}) collective-permute-start(bf16[256,768]{1,0:T(8,128)(2,1)} %add_convert_fusion.1), channel_id=1, source_target_pairs={{0,1},{1,2},{2,3},{3,0},{4,5},{5,6},{6,7},{7,4},{8,9},{9,10},{10,1... | collective-permute-start | bytes 1179656 | tf_op jit(solution)/shard_map/ppermute | solution.py:19
  241.1 16.0 %collective-permute-start.16 = (bf16[256,768]{1,0:T(8,128)(2,1)}, bf16[256,768]{1,0:T(8,128)(2,1)S(1)}, u32[]{:S(2)}, u32[]{:S(2)}) collective-permute-start(bf16[256,768]{1,0:T(8,128)(2,1)} %add_convert_fusion.2), channel_id=1, source_target_pairs={{0,1},{1,2},{2,3},{3,0},{4,5},{5,6},{6,7},{7,4},{8,9},{9,10},{10,1... | collective-permute-start | bytes 1179656 | tf_op jit(solution)/shard_map/ppermute | solution.py:19
  250.6 14.7 %collective-permute-start.19 = (bf16[256,768]{1,0:T(8,128)(2,1)}, bf16[256,768]{1,0:T(8,128)(2,1)}, u32[]{:S(2)}, u32[]{:S(2)}) collective-permute-start(bf16[256,768]{1,0:T(8,128)(2,1)} %add_convert_fusion), channel_id=1, source_target_pairs={{0,1},{1,2},{2,3},{3,0},{4,5},{5,6},{6,7},{7,4},{8,9},{9,10},{10,1... | collective-permute-start | bytes 1179656 | tf_op jit(solution)/shard_map/ppermute | solution.py:19
  258.9 11.3 %collective-permute-start.23 = (f32[384,256]{1,0:T(8,128)}, f32[384,256]{1,0:T(8,128)}, u32[]{:S(2)}, u32[]{:S(2)}) collective-permute-start(f32[384,256]{1,0:T(8,128)} %dynamic-slice_bitcast_fusion.2), channel_id=1, source_target_pairs={{0,4},{4,0},{8,12},{12,8},{16,20},{20,16},{24,28},{28,24},{1,5},{5... | collective-permute-start | bytes 1179656 | tf_op jit(solution)/shard_map/ppermute | solution.py:48
  259.6 12.4 %collective-permute-start.22 = (f32[384,384]{1,0:T(8,128)S(1)}, f32[384,384]{1,0:T(8,128)}, u32[]{:S(2)}, u32[]{:S(2)}) collective-permute-start(f32[384,384]{1,0:T(8,128)S(1)} %dynamic-slice_bitcast_fusion.1), channel_id=1, source_target_pairs={{0,4},{4,0},{8,12},{12,8},{16,20},{20,16},{24,28},{28,24},{1,5},{5... | collective-permute-start | bytes 1769480 | tf_op jit(solution)/shard_map/ppermute | solution.py:48
  262.4 14.0 %collective-permute-start.21 = (bf16[256,768]{1,0:T(8,128)(2,1)}, bf16[256,768]{1,0:T(8,128)(2,1)}, u32[]{:S(2)}, u32[]{:S(2)}) collective-permute-start(bf16[256,768]{1,0:T(8,128)(2,1)} %get-tuple-element.171.refs_4_), channel_id=1, source_target_pairs={{0,1},{1,2},{2,3},{3,0},{4,5},{5,6},{6,7},{7,4},{8,9},{9,10},{10,1... | collective-permute-start | bytes 1179656 | tf_op jit(solution)/shard_map/ppermute | solution.py:19
  270.1 27.6 %collective-permute-start.20 = (bf16[256,768]{1,0:T(8,128)(2,1)}, bf16[256,768]{1,0:T(8,128)(2,1)}, u32[]{:S(2)}, u32[]{:S(2)}) collective-permute-start(bf16[256,768]{1,0:T(8,128)(2,1)} %get-tuple-element.169.refs_0_), channel_id=1, source_target_pairs={{0,1},{1,2},{2,3},{3,0},{4,5},{5,6},{6,7},{7,4},{8,9},{9,10},{10,1... | collective-permute-start | bytes 1179656 | tf_op jit(solution)/shard_map/ppermute | solution.py:19
  276.4 8.3 %collective-permute-start.28 = (f32[6,128]{1,0:T(8,128)S(1)}, f32[6,128]{1,0:T(8,128)S(1)}, u32[]{:S(2)}, u32[]{:S(2)}) collective-permute-start(f32[6,128]{1,0:T(8,128)S(1)} %bitcast.107), channel_id=1, source_target_pairs={{0,1},{1,2},{2,3},{3,0},{4,5},{5,6},{6,7},{7,4},{8,9},{9,10},{10,1... | collective-permute-start | bytes 9224 | tf_op jit(solution)/shard_map/ppermute | solution.py:19
  276.4 9.7 %collective-permute-start.29 = (f32[6,128]{1,0:T(8,128)S(1)}, f32[6,128]{1,0:T(8,128)S(1)}, u32[]{:S(2)}, u32[]{:S(2)}) collective-permute-start(f32[6,128]{1,0:T(8,128)S(1)} %bitcast.108), channel_id=1, source_target_pairs={{0,2},{1,3},{2,0},{3,1},{4,6},{5,7},{6,4},{7,5},{8,10},{9,11},{10,... | collective-permute-start | bytes 9224 | tf_op jit(solution)/shard_map/ppermute | solution.py:19
  277.6 9.2 %collective-permute-start.30 = (f32[6,128]{1,0:T(8,128)S(1)}, f32[6,128]{1,0:T(8,128)S(1)}, u32[]{:S(2)}, u32[]{:S(2)}) collective-permute-start(f32[6,128]{1,0:T(8,128)S(1)} %bitcast.109), channel_id=1, source_target_pairs={{0,3},{1,0},{2,1},{3,2},{4,7},{5,4},{6,5},{7,6},{8,11},{9,8},{10,9... | collective-permute-start | bytes 9224 | tf_op jit(solution)/shard_map/ppermute | solution.py:19
  280.3 7.1 %collective-permute-start.27 = (f32[16,768]{1,0:T(8,128)S(1)}, f32[16,768]{1,0:T(8,128)S(1)}, u32[]{:S(2)}, u32[]{:S(2)}) collective-permute-start(f32[16,768]{1,0:T(8,128)S(1)} %add.324), channel_id=1, source_target_pairs={{0,8},{4,12},{8,0},{12,4},{16,24},{20,28},{24,16},{28,20},{1,9},{5... | collective-permute-start | bytes 147464 | tf_op jit(solution)/shard_map/ppermute | solution.py:59
  284.7 7.8 %collective-permute-start.26 = (f32[192,256]{1,0:T(8,128)S(1)}, f32[192,256]{1,0:T(8,128)S(1)}, u32[]{:S(2)}, u32[]{:S(2)}) collective-permute-start(f32[192,256]{1,0:T(8,128)S(1)} %dynamic-slice_bitcast_fusion.4), channel_id=1, source_target_pairs={{0,8},{4,12},{8,0},{12,4},{16,24},{20,28},{24,16},{28,20},{1,9},{5... | collective-permute-start | bytes 589832 | tf_op jit(solution)/shard_map/ppermute | solution.py:48
  286.2 11.6 %collective-permute-start.25 = (f32[192,384]{1,0:T(8,128)S(1)}, f32[192,384]{1,0:T(8,128)S(1)}, u32[]{:S(2)}, u32[]{:S(2)}) collective-permute-start(f32[192,384]{1,0:T(8,128)S(1)} %dynamic-slice_bitcast_fusion.3), channel_id=1, source_target_pairs={{0,8},{4,12},{8,0},{12,4},{16,24},{20,28},{24,16},{28,20},{1,9},{5... | collective-permute-start | bytes 884744 | tf_op jit(solution)/shard_map/ppermute | solution.py:48
  286.7 22.2 %collective-permute-start.32 = (bf16[256,768]{1,0:T(8,128)(2,1)}, bf16[256,768]{1,0:T(8,128)(2,1)}, u32[]{:S(2)}, u32[]{:S(2)}) collective-permute-start(bf16[256,768]{1,0:T(8,128)(2,1)} %collective-permute-done.21.refs_5_), channel_id=1, source_target_pairs={{0,1},{1,2},{2,3},{3,0},{4,5},{5,6},{6,7},{7,4},{8,9},{9,10},{10,1... | collective-permute-start | bytes 1179656 | tf_op jit(solution)/shard_map/ppermute | solution.py:19
  297.8 5.6 %collective-permute-start.35 = (f32[16,768]{1,0:T(8,128)S(1)}, f32[16,768]{1,0:T(8,128)S(1)}, u32[]{:S(2)}, u32[]{:S(2)}) collective-permute-start(f32[16,768]{1,0:T(8,128)S(1)} %add.330), channel_id=1, source_target_pairs={{0,16},{4,20},{8,24},{12,28},{16,0},{20,4},{24,8},{28,12},{1,17},{... | collective-permute-start | bytes 147464 | tf_op jit(solution)/shard_map/ppermute | solution.py:59
  299.3 7.1 %collective-permute-start.34 = (f32[96,256]{1,0:T(8,128)S(1)}, f32[96,256]{1,0:T(8,128)S(1)}, u32[]{:S(2)}, u32[]{:S(2)}) collective-permute-start(f32[96,256]{1,0:T(8,128)S(1)} %dynamic-slice_bitcast_fusion.6), channel_id=1, source_target_pairs={{0,16},{4,20},{8,24},{12,28},{16,0},{20,4},{24,8},{28,12},{1,17},{... | collective-permute-start | bytes 294920 | tf_op jit(solution)/shard_map/ppermute | solution.py:48
  299.9 9.0 %collective-permute-start.33 = (f32[96,384]{1,0:T(8,128)S(1)}, f32[96,384]{1,0:T(8,128)S(1)}, u32[]{:S(2)}, u32[]{:S(2)}) collective-permute-start(f32[96,384]{1,0:T(8,128)S(1)} %dynamic-slice_bitcast_fusion.5), channel_id=1, source_target_pairs={{0,16},{4,20},{8,24},{12,28},{16,0},{20,4},{24,8},{28,12},{1,17},{... | collective-permute-start | bytes 442376 | tf_op jit(solution)/shard_map/ppermute | solution.py:48
  301.5 21.6 %collective-permute-start.31 = (bf16[256,768]{1,0:T(8,128)(2,1)}, bf16[256,768]{1,0:T(8,128)(2,1)}, u32[]{:S(2)}, u32[]{:S(2)}) collective-permute-start(bf16[256,768]{1,0:T(8,128)(2,1)} %collective-permute-done.20.refs_1_), channel_id=1, source_target_pairs={{0,1},{1,2},{2,3},{3,0},{4,5},{5,6},{6,7},{7,4},{8,9},{9,10},{10,1... | collective-permute-start | bytes 1179656 | tf_op jit(solution)/shard_map/ppermute | solution.py:19
  309.0 11.7 %collective-permute-start.36 = (f32[104,256]{1,0:T(8,128)S(1)}, f32[104,256]{1,0:T(8,128)}, u32[]{:S(2)}, u32[]{:S(2)}) collective-permute-start(f32[104,256]{1,0:T(8,128)S(1)} %pad_maximum_fusion), channel_id=1, source_target_pairs={{0,1},{1,2},{2,3},{3,0},{4,5},{5,6},{6,7},{7,4},{8,9},{9,10},{10,1... | collective-permute-start | bytes 319496 | tf_op jit(solution)/shard_map/ppermute | solution.py:19
  310.5 11.5 %collective-permute-start.37 = (f32[104,256]{1,0:T(8,128)S(1)}, f32[104,256]{1,0:T(8,128)}, u32[]{:S(2)}, u32[]{:S(2)}) collective-permute-start(f32[104,256]{1,0:T(8,128)S(1)} %pad_maximum_fusion), channel_id=1, source_target_pairs={{0,2},{1,3},{2,0},{3,1},{4,6},{5,7},{6,4},{7,5},{8,10},{9,11},{10,... | collective-permute-start | bytes 319496 | tf_op jit(solution)/shard_map/ppermute | solution.py:19
  312.5 9.5 %collective-permute-start.38 = (f32[104,256]{1,0:T(8,128)S(1)}, f32[104,256]{1,0:T(8,128)}, u32[]{:S(2)}, u32[]{:S(2)}) collective-permute-start(f32[104,256]{1,0:T(8,128)S(1)} %pad_maximum_fusion), channel_id=1, source_target_pairs={{0,3},{1,0},{2,1},{3,2},{4,7},{5,4},{6,5},{7,6},{8,11},{9,8},{10,9... | collective-permute-start | bytes 319496 | tf_op jit(solution)/shard_map/ppermute | solution.py:19
  314.0 5.5 %collective-permute-start.39 = (f32[6,128]{1,0:T(8,128)}, f32[6,128]{1,0:T(8,128)}, u32[]{:S(2)}, u32[]{:S(2)}) collective-permute-start(f32[6,128]{1,0:T(8,128)} %add_add_fusion.3), channel_id=1, source_target_pairs={{0,4},{4,0},{8,12},{12,8},{16,20},{20,16},{24,28},{28,24},{1,5},{5... | collective-permute-start | bytes 9224 | tf_op jit(solution)/shard_map/ppermute | solution.py:59
  320.2 13.9 %collective-permute-start.42 = (bf16[256,768]{1,0:T(8,128)(2,1)}, bf16[256,768]{1,0:T(8,128)(2,1)S(1)}, u32[]{:S(2)}, u32[]{:S(2)}) collective-permute-start(bf16[256,768]{1,0:T(8,128)(2,1)} %collective-permute-done.32.refs_6_), channel_id=1, source_target_pairs={{0,1},{1,2},{2,3},{3,0},{4,5},{5,6},{6,7},{7,4},{8,9},{9,10},{10,1... | collective-permute-start | bytes 1179656 | tf_op jit(solution)/shard_map/ppermute | solution.py:19
  320.7 7.4 %collective-permute-start.40 = (f32[6,128]{1,0:T(8,128)S(1)}, f32[6,128]{1,0:T(8,128)S(1)}, u32[]{:S(2)}, u32[]{:S(2)}) collective-permute-start(f32[6,128]{1,0:T(8,128)S(1)} %add.344), channel_id=1, source_target_pairs={{0,8},{4,12},{8,0},{12,4},{16,24},{20,28},{24,16},{28,20},{1,9},{5... | collective-permute-start | bytes 9224 | tf_op jit(solution)/shard_map/ppermute | solution.py:59
  323.1 5.9 %collective-permute-start.44 = (f32[96,256]{1,0:T(8,128)S(1)}, f32[96,256]{1,0:T(8,128)S(1)}, u32[]{:S(2)}, u32[]{:S(2)}) collective-permute-start(f32[96,256]{1,0:T(8,128)S(1)} %slice.77), channel_id=1, source_target_pairs={{0,16},{4,20},{8,24},{12,28},{16,0},{20,4},{24,8},{28,12},{1,17},{... | collective-permute-start | bytes 294920 | tf_op jit(solution)/shard_map/ppermute | solution.py:53
  323.8 7.1 %collective-permute-start.43 = (f32[96,384]{1,0:T(8,128)S(1)}, f32[96,384]{1,0:T(8,128)S(1)}, u32[]{:S(2)}, u32[]{:S(2)}) collective-permute-start(f32[96,384]{1,0:T(8,128)S(1)} %bitcast_add_fusion.4), channel_id=1, source_target_pairs={{0,16},{4,20},{8,24},{12,28},{16,0},{20,4},{24,8},{28,12},{1,17},{... | collective-permute-start | bytes 442376 | tf_op jit(solution)/shard_map/ppermute | solution.py:53
  328.1 18.6 %collective-permute-start.41 = (bf16[256,768]{1,0:T(8,128)(2,1)}, bf16[256,768]{1,0:T(8,128)(2,1)S(1)}, u32[]{:S(2)}, u32[]{:S(2)}) collective-permute-start(bf16[256,768]{1,0:T(8,128)(2,1)} %collective-permute-done.31.refs_2_), channel_id=1, source_target_pairs={{0,1},{1,2},{2,3},{3,0},{4,5},{5,6},{6,7},{7,4},{8,9},{9,10},{10,1... | collective-permute-start | bytes 1179656 | tf_op jit(solution)/shard_map/ppermute | solution.py:19
  334.1 7.8 %collective-permute-start.46 = (f32[192,256]{1,0:T(8,128)S(1)}, f32[192,256]{1,0:T(8,128)S(1)}, u32[]{:S(2)}, u32[]{:S(2)}) collective-permute-start(f32[192,256]{1,0:T(8,128)S(1)} %maximum_select_fusion.5), channel_id=1, source_target_pairs={{0,8},{4,12},{8,0},{12,4},{16,24},{20,28},{24,16},{28,20},{1,9},{5... | collective-permute-start | bytes 589832 | tf_op jit(solution)/shard_map/ppermute | solution.py:53
  335.4 11.2 %collective-permute-start.45 = (f32[192,384]{1,0:T(8,128)S(1)}, f32[192,384]{1,0:T(8,128)S(1)}, u32[]{:S(2)}, u32[]{:S(2)}) collective-permute-start(f32[192,384]{1,0:T(8,128)S(1)} %maximum_select_fusion.4), channel_id=1, source_target_pairs={{0,8},{4,12},{8,0},{12,4},{16,24},{20,28},{24,16},{28,20},{1,9},{5... | collective-permute-start | bytes 884744 | tf_op jit(solution)/shard_map/ppermute | solution.py:53
  346.7 16.2 %collective-permute-start.48 = (f32[384,384]{1,0:T(8,128)S(1)}, f32[384,384]{1,0:T(8,128)}, u32[]{:S(2)}, u32[]{:S(2)}) collective-permute-start(f32[384,384]{1,0:T(8,128)S(1)} %maximum_select_fusion.2), channel_id=1, source_target_pairs={{0,4},{4,0},{8,12},{12,8},{16,20},{20,16},{24,28},{28,24},{1,5},{5... | collective-permute-start | bytes 1769480 | tf_op jit(solution)/shard_map/ppermute | solution.py:53
  347.9 12.9 %collective-permute-start.49 = (f32[384,256]{1,0:T(8,128)S(1)}, f32[384,256]{1,0:T(8,128)}, u32[]{:S(2)}, u32[]{:S(2)}) collective-permute-start(f32[384,256]{1,0:T(8,128)S(1)} %maximum_select_fusion.3), channel_id=1, source_target_pairs={{0,4},{4,0},{8,12},{12,8},{16,20},{20,16},{24,28},{28,24},{1,5},{5... | collective-permute-start | bytes 1179656 | tf_op jit(solution)/shard_map/ppermute | solution.py:53
  349.7 4.6 %collective-permute-start.47 = (f32[6,128]{1,0:T(8,128)S(1)}, f32[6,128]{1,0:T(8,128)S(1)}, u32[]{:S(2)}, u32[]{:S(2)}) collective-permute-start(f32[6,128]{1,0:T(8,128)S(1)} %add.345), channel_id=1, source_target_pairs={{0,16},{4,20},{8,24},{12,28},{16,0},{20,4},{24,8},{28,12},{1,17},{... | collective-permute-start | bytes 9224 | tf_op jit(solution)/shard_map/ppermute | solution.py:59
  (32 other events, 372.2 us)
Sparse Core Ops, SparseCore 0:
  259.0 67.0 all-reduce.2

commit v3 on v2

--- a/solution.py
+++ b/solution.py
@@ -342,7 +342,7 @@
     grads = refs[:pieces]
     (
         ssd, gate, dn, tot, cum_in, normed, normed_out, squares, cross, gain, spread,
-        dssd_o, dgate_o, local_o, payload_o, gw_out_o, gw_gate_o, sums_o,
+        dssd_o, dgate_o, local_o, payload_o, fine_o, gw_out_o, gw_gate_o, sums_o,
         state, passed,
     ) = refs[pieces:]
     width, length = ssd.shape[1], ssd.shape[0]
@@ -379,7 +379,7 @@
     for p in range(pieces):
         gw_out_o[p] = gw_out_o[p] + dot(grads[p][...], normed_out[...])
     gw_gate_o[...] = gw_gate_o[...] + dot(normed[...], dgate, 0, 0)
-    write_payload(payload_o, state, passed)
+    write_payload(payload_o, state, passed, fine_o)
 
 
 def pull_kernel(
@@ -549,11 +549,9 @@
     )(mine[None].astype(jnp.int32), dnormed, layer_input, gain, *cotangents)
 
 
-def assemble_kernel(place, *refs):
-    blocks, out = refs[:-1], refs[-1]
-    pieces = len(blocks) // 2
-    here = pl.program_id(0)
-    wanted = here // pieces * pieces + (place[0] - here % pieces + pieces) % pieces
+def assemble_kernel(given, place, *refs):
+    blocks, out = refs[given:-1], refs[-1]
+    wanted = (place[0] - pl.program_id(0) + len(blocks)) % len(blocks)
     for at, block in enumerate(blocks):
 
         @pl.when(wanted == at)
@@ -561,22 +559,25 @@
             out[...] = block[...].astype(F32)
 
 
-def assemble_call(mine, blocks):
+def assemble_call(mine, side, blocks, total, given=()):
     rows, features = blocks[0].shape
+    pieces = len(blocks)
     return pl.pallas_call(
-        assemble_kernel,
+        functools.partial(assemble_kernel, len(given)),
         grid_spec=pltpu.PrefetchScalarGridSpec(
             num_scalar_prefetch=1,
-            grid=(len(blocks),),
-            in_specs=[pl.BlockSpec((rows, features), lambda i, place: (0, 0))] * len(blocks),
-            out_specs=pl.BlockSpec((rows, features), lambda i, place: (i, 0)),
+            grid=(pieces,),
+            in_specs=[pl.BlockSpec(memory_space=pl.ANY)] * len(given)
+            + [pl.BlockSpec((rows, features), lambda i, place: (0, 0))] * pieces,
+            out_specs=pl.BlockSpec((rows, features), lambda i, place: (side * pieces + i, 0)),
         ),
-        out_shape=jax.ShapeDtypeStruct((rows * len(blocks), features), F32),
+        out_shape=jax.ShapeDtypeStruct((total, features), F32),
+        input_output_aliases={1: 0} if given else {},
         compiler_params=pltpu.CompilerParams(
             dimension_semantics=("arbitrary",), vmem_limit_bytes=60 * 1024 * 1024
         ),
         cost_estimate=pl.CostEstimate(flops=10**6, bytes_accessed=10**4, transcendentals=0),
-    )(mine[None].astype(jnp.int32), *blocks)
+    )(mine[None].astype(jnp.int32), *given, *blocks)
 
 
 def call(kernel, blocks, ins, outs, scratch=(), backward=False, total=None, skipped=0):
@@ -703,7 +704,7 @@
     mixed_ring = ring_scatter(lambda q: lax.dynamic_index_in_dim(mixed_parts, q, 0, False), "head")
     arrived = next(mixed_ring)
 
-    dssd, dgate, local_back, payload_back, gw_out, gw_gate, gate_sums = call(
+    dssd, dgate, local_back, payload_back, fine_back, gw_out, gw_gate, gate_sums = call(
         functools.partial(gate_kernel, pieces, all_width),
         blocks,
         [(c, "columns") for c in cotangents]
@@ -715,6 +716,7 @@
             ((count, width), BF16, "rows"),
             ((blocks, width, states), F32, "stack"),
             ((width + 16, states), BF16, "whole"),
+            ((width, states), BF16, "whole"),
             ((pieces, piece, width), F32, "whole"),
             ((features, width), F32, "whole"),
             ((8, width), F32, "whole"),
@@ -723,9 +725,10 @@
         backward=True,
     )
     payload_back, arrived = tie(payload_back, arrived)
+    gathered_back = lax.all_gather(payload_back, "seq")
     for _ in range(pieces - 3):
         arrived = mixed_ring.send(arrived)
-    outgoing = joined_states(lax.all_gather(payload_back, "seq"), "seq", width, heads, True)
+    outgoing = joined_states(gathered_back, "seq", width, heads, True, lax.all_gather(fine_back, "seq"))
     d, draw, rate_sums = call(
         pull_kernel,
         blocks,
@@ -762,7 +765,7 @@
         )
         halo_d = d[half : half + 8]
         if side:
-            d, arrived = tie(d, arrived)
+            d, arrived, gw_out, gw_gate = tie(d, arrived, *lax.psum((gw_out, gw_gate), "seq"))
         shares[side] = ring_scatter(
             lambda q, part=part: lax.dynamic_slice_in_dim(part, q * half_rows, half_rows, 0), "head"
         )
@@ -772,17 +775,17 @@
         else:
             first, part = tie(first, part)
     gw_inner, gw_bc, conv_sums = totals
-    gw_out, gw_gate = lax.psum((gw_out, gw_gate), "seq")
 
     gain_row = gain_in[None]
     runs, blocks_of, sums = {1: first, 0: running}, {}, {}
+    runs[1], gw_inner, gw_bc, conv_sums = tie(runs[1], gw_inner, gw_bc, conv_sums)
+    chores = Chores(weight_chores(gw_inner, gw_bc, conv_sums, width))
     for step in range(pieces - 1):
         for side in (1, 0):
             runs[side] = shares[side].send(runs[side])
-    runs[1], gw_inner, gw_bc, conv_sums, arrived, layer_late = tie(
-        runs[1], gw_inner, gw_bc, conv_sums, arrived, layer_input
-    )
-    chores = Chores(weight_chores(gw_inner, gw_bc, conv_sums, width))
+            if side and step < pieces - 2:
+                runs[1] = chores.beside(runs[1])
+    runs[0], arrived, layer_late = tie(runs[0], arrived, layer_input)
     for side in (1, 0):
         blocks_of[side], sums[side] = input_call(mine, side, runs[side], layer_input, gain_row, cotangents)
     summed = mixed_ring.send(arrived)
@@ -793,16 +796,18 @@
     for step in range(1, pieces):
         for side in (1, 0):
             blocks_of[side] = turn(blocks_of[side], "head", 1)
-            blocks_of[side] = chores.beside(blocks_of[side])
+            if step > 1 or side:
+                blocks_of[side] = chores.beside(blocks_of[side])
             if step == 1 and side:
                 blocks_of[1], gain_part = tie(blocks_of[1], (sums[0] + sums[1])[0].reshape(-1, LANES))
                 gains = Chores(gain_chores((gain_part,)))
-            else:
+            elif step > 1:
                 blocks_of[side] = gains.beside(blocks_of[side])
             arrivals[side].append(blocks_of[side])
-            if step == pieces - 2 and not side:
+            if step == 1 and not side:
                 blocks_of[0], gw_out = tie(blocks_of[0], gw_out)
-    grad_input = assemble_call(mine, arrivals[0] + arrivals[1])
+    grad_input = assemble_call(mine, 1, arrivals[1], count)
+    grad_input = assemble_call(mine, 0, arrivals[0], count, (grad_input,))
     gw_inner, gw_bc, sums, bc_sums = chores.finish()
     grad_gain_in = gains.finish()[0].reshape(-1)
     gw_out = jnp.take(gw_out, owners, axis=0).reshape(features, width).T

time: 375 us -> 373 us (level)
  waiting for transfers between devices: 83.1 us -> 63.9 us
  starting transfers between devices: 47.4 us -> 63.2 us
  blocking collectives: 35.5 us -> 47.6 us
  other arithmetic: 32.3 us -> 22.2 us
    ppermute x30, starting transfers between devices: 28.5 us -> 44.3 us  [turn(): lax.ppermute(block, axis, [(i, (i + distance) % count) for i in range(cou...]
    all_gather x1 -> x2, blocking collectives: 9.75 us -> 21.9 us  [the longest x1 11.4 us: per_device(): lax.all_gather(fine_back, 'seq')]
    ppermute x30, waiting for transfers between devices: 51.9 us -> 42.8 us  [turn(): lax.ppermute(block, axis, [(i, (i + distance) % count) for i in range(cou...]
    ppermute x6, waiting for transfers between devices: 11.8 us -> 6.16 us  [doubled(): other = lax.ppermute(value, axis, [(i, i ^ reach) for i in range(count)])]
    convert_element_type x6, other arithmetic: 8.14 us -> 3.47 us  [ring_scatter(): total = total.astype(BF16)]
    ppermute x6, waiting for transfers between devices: 15.8 us -> 11.2 us  [halved(): lax.ppermute(sent, axis, [(i, i ^ reach) for i in range(count)])]
  transfers between devices with their start and end apart: 51 -> 51, of which waited for: 21 -> 18; matrix products, arithmetic and copies ran while one was open for 13% -> 11% of each run, Pallas kernels for 35% -> 35%
where the time goes in v3:
time: 373 us; the launch traced here: 371 us
  Pallas kernels  134 us (36%)
  waiting for transfers between devices  63.9 us (17%)
  starting transfers between devices  63.2 us (17%)
  blocking collectives  47.6 us (13%)
  local copies, waits for them, and re-layouts  25.7 us (7%)
  other arithmetic  22.2 us (6%)
  between operations  14.8 us (4%)
    pallas_call x8, Pallas kernels, call(): pl.pallas_call(kernel, grid=(blocks,), in_specs=[spec(a.shape, kind, tota...  121 us
    ppermute x30, starting transfers between devices, turn(): lax.ppermute(block, axis, [(i, (i + distance) % count) for i in range(cou...  44.3 us
    ppermute x30, waiting for transfers between devices, turn(): lax.ppermute(block, axis, [(i, (i + distance) % count) for i in range(cou...  42.8 us
    all_gather x1, blocking collectives, per_device(): gathered = lax.all_gather(payload, 'seq')  14.1 us
    all_gather x1, blocking collectives, per_device(): lax.all_gather(fine, 'seq')  11.6 us
    all_gather x1, blocking collectives, per_device(): lax.all_gather(fine_back, 'seq')  11.4 us
    ppermute x6, waiting for transfers between devices, halved(): lax.ppermute(sent, axis, [(i, i ^ reach) for i in range(count)])  11.2 us
    all_gather x1, blocking collectives, per_device(): gathered_back = lax.all_gather(payload_back, 'seq')  10.4 us
  transfers between devices with their start and end apart: 51, of which 18 were waited for; matrix products, arithmetic and copies ran while one was open for 11% of the time, Pallas kernels for 35%

profile of v3, /device:TPU:0, one launch (start us, length us, event | category | flops | bytes accessed | tf_op | source)
XLA Modules:
  0.0 371.0 jit_solution(6308486826153350317)
XLA Ops:
  8.0 2.3 collective-permute-start
  11.2 2.4 collective-permute-start.1
  17.6 19.2 %shard_map.306 = (bf16[2048,768]{1,0:T(8,128)(2,1)}, f32[2048,384]{1,0:T(8,128)}, f32[2048,640]{1,0:T(8,128)}, f32[2048,640]{1,0:T(8,128)}, f32[2048,128]{1,0:T(...) custom-call(bf16[2048,768]{1,0:T(8,128)(2,1)} %x.5, ...), custom_call_target="tpu_custom_call" | custom-call | flops 1000000 | bytes 10000 | tf_op jit(solution)/shard_map/pallas_call | solution.py:600
  36.9 1.6 collective-permute-start.2
  40.4 14.1 %all-gather = bf16[3200,128]{1,0:T(8,128)(2,1)S(1)} all-gather(bf16[400,128]{1,0:T(8,128)(2,1)S(1)} %copy-done.19), channel_id=2, replica_groups=mesh['seq'=8,'head'=4] {'seq'}, dimensions={0}, use_global_device_ids=true | all-gather | bytes 921600 | tf_op jit(solution)/shard_map/all_gather | solution.py:667
  54.5 4.0 %collective-permute-done.2.refs_2_ = bf16[192,2048]{1,0:T(8,128)(2,1)S(1)} collective-permute-done((bf16[192,2048]{1,0:T(8,128)(2,1)S(1)}, bf16[192,2048]{1,0:T(8,128)(2,1)S(1)}, u32[]{:S(2)}, u32[]{:S(2)}) %collective-permute-start.2) | collective-permute-done | bytes 786464 | tf_op jit(solution)/shard_map/ppermute | solution.py:19
  58.9 11.6 %all-gather.1 = bf16[3072,128]{1,0:T(8,128)(2,1)S(1)} all-gather(bf16[384,128]{1,0:T(8,128)(2,1)S(1)} %copy-done.20), channel_id=3, replica_groups=mesh['seq'=8,'head'=4] {'seq'}, dimensions={0}, use_global_device_ids=true | all-gather | bytes 884736 | tf_op jit(solution)/shard_map/all_gather | solution.py:669
  70.7 2.0 fusion.3.incoming
  72.7 14.0 %shard_map.307 = (f32[2048,384]{1,0:T(8,128)}, f32[8,384,128]{2,1,0:T(8,128)}, f32[8,8,256]{2,1,0:T(8,128)}) custom-call(f32[2048,640]{1,0:T(8,128)} %get-tuple-element.122.tot.refs_7_, f32[2048,128]{1,0:T(8,128)} %get-tuple-element.123.raw, f32[2048,128]{1,0:T(8,128)} %get-tuple-element.124.cum_in.refs_8_, f32[8,8,256]{2,1,0:T(8,128)} %get-tuple-element.125.cum_rows, ...), custom_call_target="tpu_custom_call" | custom-call | flops 1000000 | bytes 10000 | tf_op jit(solution)/shard_map/pallas_call | solution.py:600
  88.1 3.0 collective-permute-start.5
  92.6 10.0 %shard_map.308 = (f32[2048,384]{1,0:T(8,128)}, f32[8,8,256]{2,1,0:T(8,128)}) custom-call(bf16[192,2048]{1,0:T(8,128)(2,1)} %bitcast.84, bf16[192,2048]{1,0:T(8,128)(2,1)} %copy-done.1, bf16[192,2048]{1,0:T(8,128)(2,1)} %copy-done.2, bf16[192,2048]{1,0:T(8,128)(2,1)} %copy-done.3, bf16[4,192,384]{2,1,0:T(8,128)(2,1)} %broadcast_select_fusion.refs_4_, ...), custom_call_target="tpu_custom_call" | custom-call | flops 1000000 | bytes 10000 | tf_op jit(solution)/shard_map/pallas_call | solution.py:600
  102.6 2.0 collective-permute-start.7
  104.7 2.4 collective-permute-start.9
  107.8 9.8 %shard_map.309 = (bf16[2048,384]{1,0:T(8,128)(2,1)}, bf16[4,192,2048]{2,1,0:T(8,128)(2,1)}) custom-call(f32[2048,384]{1,0:T(8,128)} %get-tuple-element.138.refs_5_.ssd.refs_4_, f32[2048,384]{1,0:T(8,128)} %get-tuple-element.132.gate.refs_6_.refs_5_, f32[8,8,256]{2,1,0:T(8,128)} %add_add_fusion.2.squares.refs_11_, ...), custom_call_target="tpu_custom_call" | custom-call | flops 1000000 | bytes 10000 | tf_op jit(solution)/shard_map/pallas_call | solution.py:600
  119.5 17.6 %shard_map.310 = (f32[2048,384]{1,0:T(8,128)}, bf16[2048,384]{1,0:T(8,128)(2,1)}, f32[8,384,128]{2,1,0:T(8,128)}, bf16[400,128]{1,0:T(8,128)(2,1)}, bf16[384,128...) custom-call(bf16[192,2048]{1,0:T(8,128)(2,1)} %bitcast.85, ...), custom_call_target="tpu_custom_call" | custom-call | flops 1000000 | bytes 10000 | tf_op jit(solution)/shard_map/pallas_call | solution.py:600
  138.0 11.4 %all-gather.3 = bf16[3072,128]{1,0:T(8,128)(2,1)S(1)} all-gather(bf16[384,128]{1,0:T(8,128)(2,1)S(1)} %copy-done.21), channel_id=5, replica_groups=mesh['seq'=8,'head'=4] {'seq'}, dimensions={0}, use_global_device_ids=true | all-gather | bytes 884736 | tf_op jit(solution)/shard_map/all_gather | solution.py:731
  150.9 2.2 collective-permute-start.11
  153.1 10.4 %all-gather.2 = bf16[3200,128]{1,0:T(8,128)(2,1)S(1)} all-gather(bf16[400,128]{1,0:T(8,128)(2,1)S(1)} %copy-done.18), channel_id=4, replica_groups=mesh['seq'=8,'head'=4] {'seq'}, dimensions={0}, use_global_device_ids=true | all-gather | bytes 921600 | tf_op jit(solution)/shard_map/all_gather | solution.py:728
  165.3 27.2 %shard_map.311 = (f32[2048,640]{1,0:T(8,128)}, f32[2048,128]{1,0:T(8,128)}, f32[8,128]{1,0:T(8,128)}) custom-call(f32[2048,640]{1,0:T(8,128)} %get-tuple-element.122.tot.refs_7_, f32[2048,128]{1,0:T(8,128)} %get-tuple-element.123.raw, f32[2048,128]{1,0:T(8,128)} %get-tuple-element.124.cum_in.refs_8_, f32[8,8,256]{2,1,0:T(8,128)} %get-tuple-element.125.cum_rows, ...), custom_call_target="tpu_custom_call" | custom-call | flops 1000000 | bytes 10000 | tf_op jit(solution)/shard_map/pallas_call | solution.py:600
  192.5 1.6 fusion.6
  197.9 1.8 collective-permute-done.13.halo
  200.3 11.2 %shard_map.312 = (bf16[1024,768]{1,0:T(8,128)(2,1)}, f32[768,384]{1,0:T(8,128)}, f32[768,256]{1,0:T(8,128)}, f32[16,768]{1,0:T(8,128)}) custom-call(f32[2048,640]{1,0:T(8,128)} %get-tuple-element.161.d, f32[8,640]{1,0:T(8,128)} %copy-done.26, f32[2048,640]{1,0:T(8,128)} %get-tuple-element.162.pre, bf16[2048,768]{1,0:T(8,128)(2,1)} %get-tuple-element.142.refs_9_.normed, ...), custom_call_target="tpu_custom_call" | custom-call | flops 1000000 | bytes 10000 | tf_op jit(solution)/shard_map/pallas_call | solution.py:600
  212.5 2.0 collective-permute-start.17
  215.9 12.1 %shard_map.313 = (bf16[1024,768]{1,0:T(8,128)(2,1)}, f32[768,384]{1,0:T(8,128)}, f32[768,256]{1,0:T(8,128)}, f32[16,768]{1,0:T(8,128)}) custom-call(f32[2048,640]{1,0:T(8,128)} %get-tuple-element.161.d, f32[8,640]{1,0:T(8,128)} %get-tuple-element.232.halo, f32[2048,640]{1,0:T(8,128)} %get-tuple-element.162.pre, ...), custom_call_target="tpu_custom_call" | custom-call | flops 1000000 | bytes 10000 | tf_op jit(solution)/shard_map/pallas_call | solution.py:600
  235.2 7.6 %collective-permute-done.14 = bf16[256,768]{1,0:T(8,128)(2,1)S(1)} collective-permute-done((bf16[256,768]{1,0:T(8,128)(2,1)S(1)}, bf16[256,768]{1,0:T(8,128)(2,1)S(1)}, u32[]{:S(2)}, u32[]{:S(2)}) %collective-permute-start.14) | collective-permute-done | bytes 393248 | tf_op jit(solution)/shard_map/ppermute | solution.py:19
  243.2 8.1 %collective-permute-done.18 = bf16[256,768]{1,0:T(8,128)(2,1)S(1)} collective-permute-done((bf16[256,768]{1,0:T(8,128)(2,1)S(1)}, bf16[256,768]{1,0:T(8,128)(2,1)S(1)}, u32[]{:S(2)}, u32[]{:S(2)}) %collective-permute-start.18) | collective-permute-done | bytes 393248 | tf_op jit(solution)/shard_map/ppermute | solution.py:19
  255.7 4.2 %collective-permute-done.24 = f32[192,256]{1,0:T(8,128)S(1)} collective-permute-done((f32[192,256]{1,0:T(8,128)S(1)}, f32[192,256]{1,0:T(8,128)S(1)}, u32[]{:S(2)}, u32[]{:S(2)}) %collective-permute-start.24) | collective-permute-done | bytes 196640 | tf_op jit(solution)/shard_map/ppermute | solution.py:48
  260.1 5.7 %collective-permute-done.23 = f32[192,384]{1,0:T(8,128)S(1)} collective-permute-done((f32[192,384]{1,0:T(8,128)S(1)}, f32[192,384]{1,0:T(8,128)S(1)}, u32[]{:S(2)}, u32[]{:S(2)}) %collective-permute-start.23) | collective-permute-done | bytes 294944 | tf_op jit(solution)/shard_map/ppermute | solution.py:48
  265.9 2.5 collective-permute-done.22
  273.1 2.7 shard_map.314
  278.0 2.9 shard_map.315
  280.9 2.9 copy.69
  284.6 3.5 collective-permute-done.26.refs_1_
  289.0 2.9 collective-permute-start.33
  292.5 2.9 fusion.8
  295.4 3.4 collective-permute-done.31
  298.8 11.7 %collective-permute-done.32 = f32[104,256]{1,0:T(8,128)S(1)} collective-permute-done((f32[104,256]{1,0:T(8,128)S(1)}, f32[104,256]{1,0:T(8,128)S(1)}, u32[]{:S(2)}, u32[]{:S(2)}) %collective-permute-start.32) | collective-permute-done | bytes 106528 | tf_op jit(solution)/shard_map/ppermute | solution.py:19
  310.6 2.8 collective-permute-start.39
  313.4 1.8 collective-permute-start.41
  315.6 16.6 %collective-permute-start.37 = (bf16[256,768]{1,0:T(8,128)(2,1)S(1)}, bf16[256,768]{1,0:T(8,128)(2,1)S(1)}, u32[]{:S(2)}, u32[]{:S(2)}) collective-permute-start(bf16[256,768]{1,0:T(8,128)(2,1)S(1)} %collective-permute-done.30.refs_2_), channel_id=1, source_target_pairs={{0,1},{1,2},{2,3},{3,0},{4,5},{5,6},{6,7},{7,4},{8,9},{9,10},{10,1... | collective-permute-start | bytes 1179656 | tf_op jit(solution)/shard_map/ppermute | solution.py:19
  332.7 1.6 collective-permute-start.42
  334.9 3.0 collective-permute-done.43
  338.0 3.1 collective-permute-done.42
  345.6 1.8 collective-permute-start.49
  349.6 3.5 shard_map.316.refs_0_
  353.7 2.1 maximum_select_fusion.1
  355.7 2.4 maximum_select_fusion
  359.6 3.5 shard_map.317
  (219 shorter events, 57.0 us)
Async XLA Ops:
  7.2 207.5 %all-reduce.3.cloned.1.call-start = ((), (), s32[]{:S(2)}) async-start(), calls=%async_computation | async-start | bytes 4718592 | tf_op jit(solution)/shard_map/psum | solution.py:768
  11.2 25.7 %collective-permute-start.1 = (bf16[192,2048]{1,0:T(8,128)(2,1)}, bf16[192,2048]{1,0:T(8,128)(2,1)S(1)}, u32[]{:S(2)}, u32[]{:S(2)}) collective-permute-start(bf16[192,2048]{1,0:T(8,128)(2,1)} %bitcast.83), channel_id=1, source_target_pairs={{0,1},{1,2},{2,3},{3,0},{4,5},{5,6},{6,7},{7,4},{8,9},{9,10},{10,1... | collective-permute-start | bytes 2359304 | tf_op jit(solution)/shard_map/ppermute | solution.py:19
  36.9 21.7 %collective-permute-start.2 = (bf16[192,2048]{1,0:T(8,128)(2,1)S(1)}, bf16[192,2048]{1,0:T(8,128)(2,1)S(1)}, u32[]{:S(2)}, u32[]{:S(2)}) collective-permute-start(bf16[192,2048]{1,0:T(8,128)(2,1)S(1)} %collective-permute-done.1.refs_1_), channel_id=1, source_target_pairs={{0,1},{1,2},{2,3},{3,0},{4,5},{5,6},{6,7},{7,4},{8,9},{9,10},{10,1... | collective-permute-start | bytes 2359304 | tf_op jit(solution)/shard_map/ppermute | solution.py:19
  58.7 27.9 %collective-permute-start.3 = (bf16[192,2048]{1,0:T(8,128)(2,1)S(1)}, bf16[192,2048]{1,0:T(8,128)(2,1)S(1)}, u32[]{:S(2)}, u32[]{:S(2)}) collective-permute-start(bf16[192,2048]{1,0:T(8,128)(2,1)S(1)} %collective-permute-done.2.refs_2_), channel_id=1, source_target_pairs={{0,1},{1,2},{2,3},{3,0},{4,5},{5,6},{6,7},{7,4},{8,9},{9,10},{10,1... | collective-permute-start | bytes 2359304 | tf_op jit(solution)/shard_map/ppermute | solution.py:19
  86.7 18.0 %collective-permute-start.4 = (f32[8,8,256]{2,1,0:T(8,128)}, f32[8,8,256]{2,1,0:T(8,128)S(1)}, u32[]{:S(2)}, u32[]{:S(2)}) collective-permute-start(f32[8,8,256]{2,1,0:T(8,128)} %get-tuple-element.139), channel_id=1, source_target_pairs={{0,1},{1,2},{2,3},{3,0},{4,5},{5,6},{6,7},{7,4},{8,9},{9,10},{10,1... | collective-permute-start | bytes 196616 | tf_op jit(solution)/shard_map/ppermute | solution.py:19
  88.1 19.0 %collective-permute-start.5 = (f32[8,8,256]{2,1,0:T(8,128)}, f32[8,8,256]{2,1,0:T(8,128)S(1)}, u32[]{:S(2)}, u32[]{:S(2)}) collective-permute-start(f32[8,8,256]{2,1,0:T(8,128)} %get-tuple-element.139), channel_id=1, source_target_pairs={{0,2},{1,3},{2,0},{3,1},{4,6},{5,7},{6,4},{7,5},{8,10},{9,11},{10,... | collective-permute-start | bytes 196616 | tf_op jit(solution)/shard_map/ppermute | solution.py:19
  91.1 16.0 %collective-permute-start.6 = (f32[8,8,256]{2,1,0:T(8,128)}, f32[8,8,256]{2,1,0:T(8,128)S(1)}, u32[]{:S(2)}, u32[]{:S(2)}) collective-permute-start(f32[8,8,256]{2,1,0:T(8,128)} %get-tuple-element.139), channel_id=1, source_target_pairs={{0,3},{1,0},{2,1},{3,2},{4,7},{5,4},{6,5},{7,6},{8,11},{9,8},{10,9... | collective-permute-start | bytes 196616 | tf_op jit(solution)/shard_map/ppermute | solution.py:19
  102.6 14.9 %collective-permute-start.7 = (f32[8,8,256]{2,1,0:T(8,128)}, f32[8,8,256]{2,1,0:T(8,128)S(1)}, u32[]{:S(2)}, u32[]{:S(2)}) collective-permute-start(f32[8,8,256]{2,1,0:T(8,128)} %get-tuple-element.146), channel_id=1, source_target_pairs={{0,1},{1,2},{2,3},{3,0},{4,5},{5,6},{6,7},{7,4},{8,9},{9,10},{10,1... | collective-permute-start | bytes 196616 | tf_op jit(solution)/shard_map/ppermute | solution.py:19
  104.7 12.9 %collective-permute-start.8 = (f32[8,8,256]{2,1,0:T(8,128)}, f32[8,8,256]{2,1,0:T(8,128)S(1)}, u32[]{:S(2)}, u32[]{:S(2)}) collective-permute-start(f32[8,8,256]{2,1,0:T(8,128)} %get-tuple-element.146), channel_id=1, source_target_pairs={{0,2},{1,3},{2,0},{3,1},{4,6},{5,7},{6,4},{7,5},{8,10},{9,11},{10,... | collective-permute-start | bytes 196616 | tf_op jit(solution)/shard_map/ppermute | solution.py:19
  104.7 12.9 %collective-permute-start.9 = (f32[8,8,256]{2,1,0:T(8,128)}, f32[8,8,256]{2,1,0:T(8,128)S(1)}, u32[]{:S(2)}, u32[]{:S(2)}) collective-permute-start(f32[8,8,256]{2,1,0:T(8,128)} %get-tuple-element.146), channel_id=1, source_target_pairs={{0,3},{1,0},{2,1},{3,2},{4,7},{5,4},{6,5},{7,6},{8,11},{9,8},{10,9... | collective-permute-start | bytes 196616 | tf_op jit(solution)/shard_map/ppermute | solution.py:19
  119.4 30.1 %collective-permute-start.10 = (bf16[192,2048]{1,0:T(8,128)(2,1)S(1)}, bf16[192,2048]{1,0:T(8,128)(2,1)S(1)}, u32[]{:S(2)}, u32[]{:S(2)}) collective-permute-start(bf16[192,2048]{1,0:T(8,128)(2,1)S(1)} %dynamic-slice_bitcast_fusion), channel_id=1, source_target_pairs={{0,1},{1,2},{2,3},{3,0},{4,5},{5,6},{6,7},{7,4},{8,9},{9,10},{10,1... | collective-permute-start | bytes 2359304 | tf_op jit(solution)/shard_map/ppermute | solution.py:19
  150.9 41.6 %collective-permute-start.11 = (bf16[192,2048]{1,0:T(8,128)(2,1)S(1)}, bf16[192,2048]{1,0:T(8,128)(2,1)}, u32[]{:S(2)}, u32[]{:S(2)}) collective-permute-start(bf16[192,2048]{1,0:T(8,128)(2,1)S(1)} %fusion.7), channel_id=1, source_target_pairs={{0,1},{1,2},{2,3},{3,0},{4,5},{5,6},{6,7},{7,4},{8,9},{9,10},{10,1... | collective-permute-start | bytes 2359304 | tf_op jit(solution)/shard_map/ppermute | solution.py:19
  194.1 21.7 %collective-permute-start.12 = (bf16[192,2048]{1,0:T(8,128)(2,1)S(1)}, bf16[192,2048]{1,0:T(8,128)(2,1)S(1)}, u32[]{:S(2)}, u32[]{:S(2)}) collective-permute-start(bf16[192,2048]{1,0:T(8,128)(2,1)S(1)} %fusion.6), channel_id=1, source_target_pairs={{0,1},{1,2},{2,3},{3,0},{4,5},{5,6},{6,7},{7,4},{8,9},{9,10},{10,1... | collective-permute-start | bytes 2359304 | tf_op jit(solution)/shard_map/ppermute | solution.py:19
  212.5 16.6 %collective-permute-start.17 = (bf16[256,768]{1,0:T(8,128)(2,1)S(1)}, bf16[256,768]{1,0:T(8,128)(2,1)S(1)}, u32[]{:S(2)}, u32[]{:S(2)}) collective-permute-start(bf16[256,768]{1,0:T(8,128)(2,1)S(1)} %constant_dynamic-slice_fusion), channel_id=1, source_target_pairs={{0,1},{1,2},{2,3},{3,0},{4,5},{5,6},{6,7},{7,4},{8,9},{9,10},{10,1... | collective-permute-start | bytes 1179656 | tf_op jit(solution)/shard_map/ppermute | solution.py:19
  229.1 13.8 %collective-permute-start.14 = (bf16[256,768]{1,0:T(8,128)(2,1)S(1)}, bf16[256,768]{1,0:T(8,128)(2,1)S(1)}, u32[]{:S(2)}, u32[]{:S(2)}) collective-permute-start(bf16[256,768]{1,0:T(8,128)(2,1)S(1)} %constant_dynamic-slice_fusion.1), channel_id=1, source_target_pairs={{0,1},{1,2},{2,3},{3,0},{4,5},{5,6},{6,7},{7,4},{8,9},{9,10},{10,1... | collective-permute-start | bytes 1179656 | tf_op jit(solution)/shard_map/ppermute | solution.py:19
  229.2 6.1 %collective-permute-start.21 = (f32[16,768]{1,0:T(8,128)}, f32[16,768]{1,0:T(8,128)S(1)}, u32[]{:S(2)}, u32[]{:S(2)}) collective-permute-start(f32[16,768]{1,0:T(8,128)} %get-tuple-element.182), channel_id=1, source_target_pairs={{0,4},{4,0},{8,12},{12,8},{16,20},{20,16},{24,28},{28,24},{1,5},{5... | collective-permute-start | bytes 147464 | tf_op jit(solution)/shard_map/ppermute | solution.py:59
  231.8 11.2 %collective-permute-start.20 = (f32[384,256]{1,0:T(8,128)S(1)}, f32[384,256]{1,0:T(8,128)S(1)}, u32[]{:S(2)}, u32[]{:S(2)}) collective-permute-start(f32[384,256]{1,0:T(8,128)S(1)} %dynamic-slice_bitcast_fusion.2), channel_id=1, source_target_pairs={{0,4},{4,0},{8,12},{12,8},{16,20},{20,16},{24,28},{28,24},{1,5},{5... | collective-permute-start | bytes 1179656 | tf_op jit(solution)/shard_map/ppermute | solution.py:48
  233.1 10.0 %collective-permute-start.19 = (f32[384,384]{1,0:T(8,128)S(1)}, f32[384,384]{1,0:T(8,128)S(1)}, u32[]{:S(2)}, u32[]{:S(2)}) collective-permute-start(f32[384,384]{1,0:T(8,128)S(1)} %dynamic-slice_bitcast_fusion.1), channel_id=1, source_target_pairs={{0,4},{4,0},{8,12},{12,8},{16,20},{20,16},{24,28},{28,24},{1,5},{5... | collective-permute-start | bytes 1769480 | tf_op jit(solution)/shard_map/ppermute | solution.py:48
  233.7 17.5 %collective-permute-start.18 = (bf16[256,768]{1,0:T(8,128)(2,1)S(1)}, bf16[256,768]{1,0:T(8,128)(2,1)S(1)}, u32[]{:S(2)}, u32[]{:S(2)}) collective-permute-start(bf16[256,768]{1,0:T(8,128)(2,1)S(1)} %add_convert_fusion.1), channel_id=1, source_target_pairs={{0,1},{1,2},{2,3},{3,0},{4,5},{5,6},{6,7},{7,4},{8,9},{9,10},{10,1... | collective-permute-start | bytes 1179656 | tf_op jit(solution)/shard_map/ppermute | solution.py:19
  243.0 17.0 %collective-permute-start.15 = (bf16[256,768]{1,0:T(8,128)(2,1)S(1)}, bf16[256,768]{1,0:T(8,128)(2,1)S(1)}, u32[]{:S(2)}, u32[]{:S(2)}) collective-permute-start(bf16[256,768]{1,0:T(8,128)(2,1)S(1)} %add_convert_fusion.3), channel_id=1, source_target_pairs={{0,1},{1,2},{2,3},{3,0},{4,5},{5,6},{6,7},{7,4},{8,9},{9,10},{10,1... | collective-permute-start | bytes 1179656 | tf_op jit(solution)/shard_map/ppermute | solution.py:19
  251.3 4.4 %collective-permute-start.25 = (f32[16,768]{1,0:T(8,128)S(1)}, f32[16,768]{1,0:T(8,128)S(1)}, u32[]{:S(2)}, u32[]{:S(2)}) collective-permute-start(f32[16,768]{1,0:T(8,128)S(1)} %add.326), channel_id=1, source_target_pairs={{0,8},{4,12},{8,0},{12,4},{16,24},{20,28},{24,16},{28,20},{1,9},{5... | collective-permute-start | bytes 147464 | tf_op jit(solution)/shard_map/ppermute | solution.py:59
  252.0 8.0 %collective-permute-start.24 = (f32[192,256]{1,0:T(8,128)S(1)}, f32[192,256]{1,0:T(8,128)S(1)}, u32[]{:S(2)}, u32[]{:S(2)}) collective-permute-start(f32[192,256]{1,0:T(8,128)S(1)} %dynamic-slice_bitcast_fusion.4), channel_id=1, source_target_pairs={{0,8},{4,12},{8,0},{12,4},{16,24},{20,28},{24,16},{28,20},{1,9},{5... | collective-permute-start | bytes 589832 | tf_op jit(solution)/shard_map/ppermute | solution.py:48
  253.4 12.5 %collective-permute-start.23 = (f32[192,384]{1,0:T(8,128)S(1)}, f32[192,384]{1,0:T(8,128)S(1)}, u32[]{:S(2)}, u32[]{:S(2)}) collective-permute-start(f32[192,384]{1,0:T(8,128)S(1)} %dynamic-slice_bitcast_fusion.3), channel_id=1, source_target_pairs={{0,8},{4,12},{8,0},{12,4},{16,24},{20,28},{24,16},{28,20},{1,9},{5... | collective-permute-start | bytes 884744 | tf_op jit(solution)/shard_map/ppermute | solution.py:48
  254.3 14.1 %collective-permute-start.22 = (bf16[256,768]{1,0:T(8,128)(2,1)S(1)}, bf16[256,768]{1,0:T(8,128)(2,1)S(1)}, u32[]{:S(2)}, u32[]{:S(2)}) collective-permute-start(bf16[256,768]{1,0:T(8,128)(2,1)S(1)} %add_convert_fusion), channel_id=1, source_target_pairs={{0,1},{1,2},{2,3},{3,0},{4,5},{5,6},{6,7},{7,4},{8,9},{9,10},{10,1... | collective-permute-start | bytes 1179656 | tf_op jit(solution)/shard_map/ppermute | solution.py:19
  260.1 17.0 %collective-permute-start.16 = (bf16[256,768]{1,0:T(8,128)(2,1)S(1)}, bf16[256,768]{1,0:T(8,128)(2,1)S(1)}, u32[]{:S(2)}, u32[]{:S(2)}) collective-permute-start(bf16[256,768]{1,0:T(8,128)(2,1)S(1)} %add_convert_fusion.2), channel_id=1, source_target_pairs={{0,1},{1,2},{2,3},{3,0},{4,5},{5,6},{6,7},{7,4},{8,9},{9,10},{10,1... | collective-permute-start | bytes 1179656 | tf_op jit(solution)/shard_map/ppermute | solution.py:19
  268.4 7.4 %collective-permute-start.29 = (f32[16,768]{1,0:T(8,128)S(1)}, f32[16,768]{1,0:T(8,128)S(1)}, u32[]{:S(2)}, u32[]{:S(2)}) collective-permute-start(f32[16,768]{1,0:T(8,128)S(1)} %add.333), channel_id=1, source_target_pairs={{0,16},{4,20},{8,24},{12,28},{16,0},{20,4},{24,8},{28,12},{1,17},{... | collective-permute-start | bytes 147464 | tf_op jit(solution)/shard_map/ppermute | solution.py:59
  269.9 5.9 %collective-permute-start.28 = (f32[96,256]{1,0:T(8,128)S(1)}, f32[96,256]{1,0:T(8,128)S(1)}, u32[]{:S(2)}, u32[]{:S(2)}) collective-permute-start(f32[96,256]{1,0:T(8,128)S(1)} %dynamic-slice_bitcast_fusion.6), channel_id=1, source_target_pairs={{0,16},{4,20},{8,24},{12,28},{16,0},{20,4},{24,8},{28,12},{1,17},{... | collective-permute-start | bytes 294920 | tf_op jit(solution)/shard_map/ppermute | solution.py:48
  270.5 6.5 %collective-permute-start.27 = (f32[96,384]{1,0:T(8,128)S(1)}, f32[96,384]{1,0:T(8,128)S(1)}, u32[]{:S(2)}, u32[]{:S(2)}) collective-permute-start(f32[96,384]{1,0:T(8,128)S(1)} %dynamic-slice_bitcast_fusion.5), channel_id=1, source_target_pairs={{0,16},{4,20},{8,24},{12,28},{16,0},{20,4},{24,8},{28,12},{1,17},{... | collective-permute-start | bytes 442376 | tf_op jit(solution)/shard_map/ppermute | solution.py:48
  275.8 12.2 %collective-permute-start.26 = (bf16[256,768]{1,0:T(8,128)(2,1)}, bf16[256,768]{1,0:T(8,128)(2,1)}, u32[]{:S(2)}, u32[]{:S(2)}) collective-permute-start(bf16[256,768]{1,0:T(8,128)(2,1)} %get-tuple-element.188.refs_0_), channel_id=1, source_target_pairs={{0,1},{1,2},{2,3},{3,0},{4,5},{5,6},{6,7},{7,4},{8,9},{9,10},{10,1... | collective-permute-start | bytes 1179656 | tf_op jit(solution)/shard_map/ppermute | solution.py:19
  280.9 29.6 %collective-permute-start.38 = (bf16[256,768]{1,0:T(8,128)(2,1)}, bf16[256,768]{1,0:T(8,128)(2,1)}, u32[]{:S(2)}, u32[]{:S(2)}) collective-permute-start(bf16[256,768]{1,0:T(8,128)(2,1)} %get-tuple-element.203.refs_1_), channel_id=1, source_target_pairs={{0,1},{1,2},{2,3},{3,0},{4,5},{5,6},{6,7},{7,4},{8,9},{9,10},{10,1... | collective-permute-start | bytes 1179656 | tf_op jit(solution)/shard_map/ppermute | solution.py:19
  288.0 10.7 %collective-permute-start.31 = (f32[104,256]{1,0:T(8,128)S(1)}, f32[104,256]{1,0:T(8,128)S(1)}, u32[]{:S(2)}, u32[]{:S(2)}) collective-permute-start(f32[104,256]{1,0:T(8,128)S(1)} %pad_maximum_fusion), channel_id=1, source_target_pairs={{0,1},{1,2},{2,3},{3,0},{4,5},{5,6},{6,7},{7,4},{8,9},{9,10},{10,1... | collective-permute-start | bytes 319496 | tf_op jit(solution)/shard_map/ppermute | solution.py:19
  288.1 22.4 %collective-permute-start.32 = (f32[104,256]{1,0:T(8,128)S(1)}, f32[104,256]{1,0:T(8,128)S(1)}, u32[]{:S(2)}, u32[]{:S(2)}) collective-permute-start(f32[104,256]{1,0:T(8,128)S(1)} %pad_maximum_fusion), channel_id=1, source_target_pairs={{0,2},{1,3},{2,0},{3,1},{4,6},{5,7},{6,4},{7,5},{8,10},{9,11},{10,... | collective-permute-start | bytes 319496 | tf_op jit(solution)/shard_map/ppermute | solution.py:19
  289.0 21.5 %collective-permute-start.33 = (f32[104,256]{1,0:T(8,128)S(1)}, f32[104,256]{1,0:T(8,128)S(1)}, u32[]{:S(2)}, u32[]{:S(2)}) collective-permute-start(f32[104,256]{1,0:T(8,128)S(1)} %pad_maximum_fusion), channel_id=1, source_target_pairs={{0,3},{1,0},{2,1},{3,2},{4,7},{5,4},{6,5},{7,6},{8,11},{9,8},{10,9... | collective-permute-start | bytes 319496 | tf_op jit(solution)/shard_map/ppermute | solution.py:19
  291.9 21.5 %collective-permute-start.30 = (bf16[256,768]{1,0:T(8,128)(2,1)}, bf16[256,768]{1,0:T(8,128)(2,1)S(1)}, u32[]{:S(2)}, u32[]{:S(2)}) collective-permute-start(bf16[256,768]{1,0:T(8,128)(2,1)} %collective-permute-done.26.refs_1_), channel_id=1, source_target_pairs={{0,1},{1,2},{2,3},{3,0},{4,5},{5,6},{6,7},{7,4},{8,9},{9,10},{10,1... | collective-permute-start | bytes 1179656 | tf_op jit(solution)/shard_map/ppermute | solution.py:19
  298.8 16.5 %collective-permute-start.34 = (f32[6,128]{1,0:T(8,128)S(1)}, f32[6,128]{1,0:T(8,128)S(1)}, u32[]{:S(2)}, u32[]{:S(2)}) collective-permute-start(f32[6,128]{1,0:T(8,128)S(1)} %bitcast.110), channel_id=1, source_target_pairs={{0,1},{1,2},{2,3},{3,0},{4,5},{5,6},{6,7},{7,4},{8,9},{9,10},{10,1... | collective-permute-start | bytes 9224 | tf_op jit(solution)/shard_map/ppermute | solution.py:19
  310.5 5.1 %collective-permute-start.35 = (f32[6,128]{1,0:T(8,128)S(1)}, f32[6,128]{1,0:T(8,128)S(1)}, u32[]{:S(2)}, u32[]{:S(2)}) collective-permute-start(f32[6,128]{1,0:T(8,128)S(1)} %bitcast.111), channel_id=1, source_target_pairs={{0,2},{1,3},{2,0},{3,1},{4,6},{5,7},{6,4},{7,5},{8,10},{9,11},{10,... | collective-permute-start | bytes 9224 | tf_op jit(solution)/shard_map/ppermute | solution.py:19
  310.5 5.1 %collective-permute-start.36 = (f32[6,128]{1,0:T(8,128)S(1)}, f32[6,128]{1,0:T(8,128)S(1)}, u32[]{:S(2)}, u32[]{:S(2)}) collective-permute-start(f32[6,128]{1,0:T(8,128)S(1)} %bitcast.112), channel_id=1, source_target_pairs={{0,3},{1,0},{2,1},{3,2},{4,7},{5,4},{6,5},{7,6},{8,11},{9,8},{10,9... | collective-permute-start | bytes 9224 | tf_op jit(solution)/shard_map/ppermute | solution.py:19
  310.6 21.7 %collective-permute-start.39 = (bf16[256,768]{1,0:T(8,128)(2,1)}, bf16[256,768]{1,0:T(8,128)(2,1)S(1)}, u32[]{:S(2)}, u32[]{:S(2)}) collective-permute-start(bf16[256,768]{1,0:T(8,128)(2,1)} %collective-permute-done.38.refs_2_), channel_id=1, source_target_pairs={{0,1},{1,2},{2,3},{3,0},{4,5},{5,6},{6,7},{7,4},{8,9},{9,10},{10,1... | collective-permute-start | bytes 1179656 | tf_op jit(solution)/shard_map/ppermute | solution.py:19
  313.4 18.7 %collective-permute-start.41 = (f32[96,256]{1,0:T(8,128)S(1)}, f32[96,256]{1,0:T(8,128)S(1)}, u32[]{:S(2)}, u32[]{:S(2)}) collective-permute-start(f32[96,256]{1,0:T(8,128)S(1)} %slice.77), channel_id=1, source_target_pairs={{0,16},{4,20},{8,24},{12,28},{16,0},{20,4},{24,8},{28,12},{1,17},{... | collective-permute-start | bytes 294920 | tf_op jit(solution)/shard_map/ppermute | solution.py:53
  315.2 17.0 %collective-permute-start.40 = (f32[96,384]{1,0:T(8,128)S(1)}, f32[96,384]{1,0:T(8,128)S(1)}, u32[]{:S(2)}, u32[]{:S(2)}) collective-permute-start(f32[96,384]{1,0:T(8,128)S(1)} %bitcast_add_fusion.4), channel_id=1, source_target_pairs={{0,16},{4,20},{8,24},{12,28},{16,0},{20,4},{24,8},{28,12},{1,17},{... | collective-permute-start | bytes 442376 | tf_op jit(solution)/shard_map/ppermute | solution.py:53
  315.6 25.6 %collective-permute-start.37 = (bf16[256,768]{1,0:T(8,128)(2,1)S(1)}, bf16[256,768]{1,0:T(8,128)(2,1)S(1)}, u32[]{:S(2)}, u32[]{:S(2)}) collective-permute-start(bf16[256,768]{1,0:T(8,128)(2,1)S(1)} %collective-permute-done.30.refs_2_), channel_id=1, source_target_pairs={{0,1},{1,2},{2,3},{3,0},{4,5},{5,6},{6,7},{7,4},{8,9},{9,10},{10,1... | collective-permute-start | bytes 1179656 | tf_op jit(solution)/shard_map/ppermute | solution.py:19
  332.2 5.7 %collective-permute-start.43 = (f32[192,256]{1,0:T(8,128)S(1)}, f32[192,256]{1,0:T(8,128)S(1)}, u32[]{:S(2)}, u32[]{:S(2)}) collective-permute-start(f32[192,256]{1,0:T(8,128)S(1)} %maximum_select_fusion.5), channel_id=1, source_target_pairs={{0,8},{4,12},{8,0},{12,4},{16,24},{20,28},{24,16},{28,20},{1,9},{5... | collective-permute-start | bytes 589832 | tf_op jit(solution)/shard_map/ppermute | solution.py:53
  332.7 8.4 %collective-permute-start.42 = (f32[192,384]{1,0:T(8,128)S(1)}, f32[192,384]{1,0:T(8,128)S(1)}, u32[]{:S(2)}, u32[]{:S(2)}) collective-permute-start(f32[192,384]{1,0:T(8,128)S(1)} %maximum_select_fusion.4), channel_id=1, source_target_pairs={{0,8},{4,12},{8,0},{12,4},{16,24},{20,28},{24,16},{28,20},{1,9},{5... | collective-permute-start | bytes 884744 | tf_op jit(solution)/shard_map/ppermute | solution.py:53
  334.9 6.9 %collective-permute-start.44 = (f32[6,128]{1,0:T(8,128)S(1)}, f32[6,128]{1,0:T(8,128)S(1)}, u32[]{:S(2)}, u32[]{:S(2)}) collective-permute-start(f32[6,128]{1,0:T(8,128)S(1)} %add_add_fusion.3), channel_id=1, source_target_pairs={{0,4},{4,0},{8,12},{12,8},{16,20},{20,16},{24,28},{28,24},{1,5},{5... | collective-permute-start | bytes 9224 | tf_op jit(solution)/shard_map/ppermute | solution.py:59
  341.2 14.5 %collective-permute-start.47 = (f32[384,384]{1,0:T(8,128)S(1)}, f32[384,384]{1,0:T(8,128)}, u32[]{:S(2)}, u32[]{:S(2)}) collective-permute-start(f32[384,384]{1,0:T(8,128)S(1)} %maximum_select_fusion.2), channel_id=1, source_target_pairs={{0,4},{4,0},{8,12},{12,8},{16,20},{20,16},{24,28},{28,24},{1,5},{5... | collective-permute-start | bytes 1769480 | tf_op jit(solution)/shard_map/ppermute | solution.py:53
  342.4 11.3 %collective-permute-start.48 = (f32[384,256]{1,0:T(8,128)S(1)}, f32[384,256]{1,0:T(8,128)}, u32[]{:S(2)}, u32[]{:S(2)}) collective-permute-start(f32[384,256]{1,0:T(8,128)S(1)} %maximum_select_fusion.3), channel_id=1, source_target_pairs={{0,4},{4,0},{8,12},{12,8},{16,20},{20,16},{24,28},{28,24},{1,5},{5... | collective-permute-start | bytes 1179656 | tf_op jit(solution)/shard_map/ppermute | solution.py:53
  345.4 13.4 %collective-permute-start.46 = (bf16[256,768]{1,0:T(8,128)(2,1)}, bf16[256,768]{1,0:T(8,128)(2,1)S(1)}, u32[]{:S(2)}, u32[]{:S(2)}) collective-permute-start(bf16[256,768]{1,0:T(8,128)(2,1)} %copy-done.15), channel_id=1, source_target_pairs={{0,1},{1,2},{2,3},{3,0},{4,5},{5,6},{6,7},{7,4},{8,9},{9,10},{10,1... | collective-permute-start | bytes 1179656 | tf_op jit(solution)/shard_map/ppermute | solution.py:19
  345.6 7.5 %collective-permute-start.49 = (f32[6,128]{1,0:T(8,128)S(1)}, f32[6,128]{1,0:T(8,128)S(1)}, u32[]{:S(2)}, u32[]{:S(2)}) collective-permute-start(f32[6,128]{1,0:T(8,128)S(1)} %add.349), channel_id=1, source_target_pairs={{0,16},{4,20},{8,24},{12,28},{16,0},{20,4},{24,8},{28,12},{1,17},{... | collective-permute-start | bytes 9224 | tf_op jit(solution)/shard_map/ppermute | solution.py:59
  (31 other events, 322.9 us)
Sparse Core Ops, SparseCore 0:
  137.3 65.4 all-reduce.2

commit v4 on v3

--- a/solution.py
+++ b/solution.py
@@ -415,29 +415,28 @@
     read = dot(queries.astype(BF16), beginning.astype(BF16), 1, 1)
     dqueries = dot_both(ecum_w * dy, beginning)
     taken = dot(keys, ending.astype(BF16), 1, 1)
-    dkeys = dot_both(tail_w * inner, ending)
+    dkeys = dot_right((tail_w * inner).astype(BF16), ending)
     from_start = ecum * narrow(dy * read, spread[...])
     to_end = tail * narrow(inner * taken, spread[...])
     both = as_rows(ending * beginning)
     through = jnp.exp(last) * narrow(both, spread[...])[0:1]
     scores = dot_left(queries, keys, 1, 1)
-    fed, fed_fine = halves(inner * step_w)
+    fed = (inner * step_w).astype(BF16)
     dscores = jnp.zeros_like(scores)
     crossing = jnp.zeros((length, LANES), F32)
     pulls, downs = [], []
     lanes_all = lax.broadcasted_iota(jnp.int32, (length, LANES), 1)
     for begin in range(0, width, LANES):
         size = min(LANES, width - begin)
-        fed_pair, fed_low, dy_pair, dy_low = (v[:, begin : begin + size] for v in (fed, fed_fine, dy16, dy_fine))
+        fed_pair, dy_pair, dy_low = (v[:, begin : begin + size] for v in (fed, dy16, dy_fine))
         lane = lax.broadcasted_iota(jnp.int32, (1, size), 1)
         rows = []
         for half in range(size // HEAD_DIM):
             h = begin // HEAD_DIM + half
             inside = (lane >= half * HEAD_DIM) & (lane < (half + 1) * HEAD_DIM)
             fed_head = jnp.where(inside, fed_pair, jnp.zeros_like(fed_pair))
-            low_head = jnp.where(inside, fed_low, jnp.zeros_like(fed_low))
             decay = jnp.exp(cum[:, h : h + 1] - cum_rows[0, h : h + 1, :] + hide[...])
-            dweight = dot(dy_pair, fed_head, 1, 1) + dot(dy_low, fed_head, 1, 1) + dot(dy_pair, low_head, 1, 1)
+            dweight = dot(dy_pair, fed_head, 1, 1) + dot(dy_low, fed_head, 1, 1)
             dweight = dweight * decay
             dscores = dscores + dweight
             weight = (scores * decay).astype(BF16)

time: 373 us -> 371 us (level)
  no operation moved by 1% of the time
where the time goes in v4:
time: 371 us; the launch traced here: 369 us
  Pallas kernels  131 us (35%)
  waiting for transfers between devices  64.3 us (17%)
  starting transfers between devices  63.1 us (17%)
  blocking collectives  47.6 us (13%)
  local copies, waits for them, and re-layouts  25.7 us (7%)
  other arithmetic  22.3 us (6%)
  between operations  14.8 us (4%)
    pallas_call x8, Pallas kernels, call(): pl.pallas_call(kernel, grid=(blocks,), in_specs=[spec(a.shape, kind, tota...  119 us
    ppermute x30, starting transfers between devices, turn(): lax.ppermute(block, axis, [(i, (i + distance) % count) for i in range(cou...  44.3 us
    ppermute x30, waiting for transfers between devices, turn(): lax.ppermute(block, axis, [(i, (i + distance) % count) for i in range(cou...  41.9 us
    all_gather x1, blocking collectives, per_device(): gathered = lax.all_gather(payload, 'seq')  14.1 us
    ppermute x6, waiting for transfers between devices, halved(): lax.ppermute(sent, axis, [(i, i ^ reach) for i in range(count)])  12 us
    all_gather x1, blocking collectives, per_device(): lax.all_gather(fine, 'seq')  11.6 us
    all_gather x1, blocking collectives, per_device(): lax.all_gather(fine_back, 'seq')  11.4 us
    all_gather x1, blocking collectives, per_device(): gathered_back = lax.all_gather(payload_back, 'seq')  10.4 us
  transfers between devices with their start and end apart: 51, of which 18 were waited for; matrix products, arithmetic and copies ran while one was open for 11% of the time, Pallas kernels for 35%

profile of v4, /device:TPU:0, one launch (start us, length us, event | category | flops | bytes accessed | tf_op | source)
XLA Modules:
  0.0 369.2 jit_solution(435720771504063838)
XLA Ops:
  8.0 2.3 collective-permute-start
  11.2 2.4 collective-permute-start.1
  17.6 19.2 %shard_map.306 = (bf16[2048,768]{1,0:T(8,128)(2,1)}, f32[2048,384]{1,0:T(8,128)}, f32[2048,640]{1,0:T(8,128)}, f32[2048,640]{1,0:T(8,128)}, f32[2048,128]{1,0:T(...) custom-call(bf16[2048,768]{1,0:T(8,128)(2,1)} %x.5, ...), custom_call_target="tpu_custom_call" | custom-call | flops 1000000 | bytes 10000 | tf_op jit(solution)/shard_map/pallas_call | solution.py:599
  40.4 14.1 %all-gather = bf16[3200,128]{1,0:T(8,128)(2,1)S(1)} all-gather(bf16[400,128]{1,0:T(8,128)(2,1)S(1)} %copy-done.19), channel_id=2, replica_groups=mesh['seq'=8,'head'=4] {'seq'}, dimensions={0}, use_global_device_ids=true | all-gather | bytes 921600 | tf_op jit(solution)/shard_map/all_gather | solution.py:666
  54.5 4.0 %collective-permute-done.2.refs_2_ = bf16[192,2048]{1,0:T(8,128)(2,1)S(1)} collective-permute-done((bf16[192,2048]{1,0:T(8,128)(2,1)S(1)}, bf16[192,2048]{1,0:T(8,128)(2,1)S(1)}, u32[]{:S(2)}, u32[]{:S(2)}) %collective-permute-start.2) | collective-permute-done | bytes 786464 | tf_op jit(solution)/shard_map/ppermute | solution.py:19
  58.9 11.6 %all-gather.1 = bf16[3072,128]{1,0:T(8,128)(2,1)S(1)} all-gather(bf16[384,128]{1,0:T(8,128)(2,1)S(1)} %copy-done.20), channel_id=3, replica_groups=mesh['seq'=8,'head'=4] {'seq'}, dimensions={0}, use_global_device_ids=true | all-gather | bytes 884736 | tf_op jit(solution)/shard_map/all_gather | solution.py:668
  70.7 2.0 fusion.3.incoming
  72.7 14.0 %shard_map.307 = (f32[2048,384]{1,0:T(8,128)}, f32[8,384,128]{2,1,0:T(8,128)}, f32[8,8,256]{2,1,0:T(8,128)}) custom-call(f32[2048,640]{1,0:T(8,128)} %get-tuple-element.122.tot.refs_7_, f32[2048,128]{1,0:T(8,128)} %get-tuple-element.123.raw, f32[2048,128]{1,0:T(8,128)} %get-tuple-element.124.cum_in.refs_8_, f32[8,8,256]{2,1,0:T(8,128)} %get-tuple-element.125.cum_rows, ...), custom_call_target="tpu_custom_call" | custom-call | flops 1000000 | bytes 10000 | tf_op jit(solution)/shard_map/pallas_call | solution.py:599
  88.1 3.0 collective-permute-start.5
  92.6 10.0 %shard_map.308 = (f32[2048,384]{1,0:T(8,128)}, f32[8,8,256]{2,1,0:T(8,128)}) custom-call(bf16[192,2048]{1,0:T(8,128)(2,1)} %bitcast.84, bf16[192,2048]{1,0:T(8,128)(2,1)} %copy-done.1, bf16[192,2048]{1,0:T(8,128)(2,1)} %copy-done.2, bf16[192,2048]{1,0:T(8,128)(2,1)} %copy-done.3, bf16[4,192,384]{2,1,0:T(8,128)(2,1)} %broadcast_select_fusion.refs_4_, ...), custom_call_target="tpu_custom_call" | custom-call | flops 1000000 | bytes 10000 | tf_op jit(solution)/shard_map/pallas_call | solution.py:599
  102.6 2.0 collective-permute-start.7
  104.7 2.4 collective-permute-start.9
  107.8 9.8 %shard_map.309 = (bf16[2048,384]{1,0:T(8,128)(2,1)}, bf16[4,192,2048]{2,1,0:T(8,128)(2,1)}) custom-call(f32[2048,384]{1,0:T(8,128)} %get-tuple-element.138.refs_5_.ssd.refs_4_, f32[2048,384]{1,0:T(8,128)} %get-tuple-element.132.gate.refs_6_.refs_5_, f32[8,8,256]{2,1,0:T(8,128)} %add_add_fusion.2.squares.refs_11_, ...), custom_call_target="tpu_custom_call" | custom-call | flops 1000000 | bytes 10000 | tf_op jit(solution)/shard_map/pallas_call | solution.py:599
  119.5 17.6 %shard_map.310 = (f32[2048,384]{1,0:T(8,128)}, bf16[2048,384]{1,0:T(8,128)(2,1)}, f32[8,384,128]{2,1,0:T(8,128)}, bf16[400,128]{1,0:T(8,128)(2,1)}, bf16[384,128...) custom-call(bf16[192,2048]{1,0:T(8,128)(2,1)} %bitcast.85, ...), custom_call_target="tpu_custom_call" | custom-call | flops 1000000 | bytes 10000 | tf_op jit(solution)/shard_map/pallas_call | solution.py:599
  138.0 11.4 %all-gather.3 = bf16[3072,128]{1,0:T(8,128)(2,1)S(1)} all-gather(bf16[384,128]{1,0:T(8,128)(2,1)S(1)} %copy-done.21), channel_id=5, replica_groups=mesh['seq'=8,'head'=4] {'seq'}, dimensions={0}, use_global_device_ids=true | all-gather | bytes 884736 | tf_op jit(solution)/shard_map/all_gather | solution.py:730
  150.9 2.2 collective-permute-start.11
  153.1 10.4 %all-gather.2 = bf16[3200,128]{1,0:T(8,128)(2,1)S(1)} all-gather(bf16[400,128]{1,0:T(8,128)(2,1)S(1)} %copy-done.18), channel_id=4, replica_groups=mesh['seq'=8,'head'=4] {'seq'}, dimensions={0}, use_global_device_ids=true | all-gather | bytes 921600 | tf_op jit(solution)/shard_map/all_gather | solution.py:727
  165.3 24.9 %shard_map.311 = (f32[2048,640]{1,0:T(8,128)}, f32[2048,128]{1,0:T(8,128)}, f32[8,128]{1,0:T(8,128)}) custom-call(f32[2048,640]{1,0:T(8,128)} %get-tuple-element.122.tot.refs_7_, f32[2048,128]{1,0:T(8,128)} %get-tuple-element.123.raw, f32[2048,128]{1,0:T(8,128)} %get-tuple-element.124.cum_in.refs_8_, f32[8,8,256]{2,1,0:T(8,128)} %get-tuple-element.125.cum_rows, ...), custom_call_target="tpu_custom_call" | custom-call | flops 1000000 | bytes 10000 | tf_op jit(solution)/shard_map/pallas_call | solution.py:599
  190.2 1.7 fusion.6
  195.8 1.8 collective-permute-done.13.halo
  198.2 11.2 %shard_map.312 = (bf16[1024,768]{1,0:T(8,128)(2,1)}, f32[768,384]{1,0:T(8,128)}, f32[768,256]{1,0:T(8,128)}, f32[16,768]{1,0:T(8,128)}) custom-call(f32[2048,640]{1,0:T(8,128)} %get-tuple-element.161.d, f32[8,640]{1,0:T(8,128)} %copy-done.26, f32[2048,640]{1,0:T(8,128)} %get-tuple-element.162.pre, bf16[2048,768]{1,0:T(8,128)(2,1)} %get-tuple-element.142.refs_9_.normed, ...), custom_call_target="tpu_custom_call" | custom-call | flops 1000000 | bytes 10000 | tf_op jit(solution)/shard_map/pallas_call | solution.py:599
  210.5 1.9 collective-permute-start.17
  213.6 12.1 %shard_map.313 = (bf16[1024,768]{1,0:T(8,128)(2,1)}, f32[768,384]{1,0:T(8,128)}, f32[768,256]{1,0:T(8,128)}, f32[16,768]{1,0:T(8,128)}) custom-call(f32[2048,640]{1,0:T(8,128)} %get-tuple-element.161.d, f32[8,640]{1,0:T(8,128)} %get-tuple-element.232.halo, f32[2048,640]{1,0:T(8,128)} %get-tuple-element.162.pre, ...), custom_call_target="tpu_custom_call" | custom-call | flops 1000000 | bytes 10000 | tf_op jit(solution)/shard_map/pallas_call | solution.py:599
  233.1 7.2 %collective-permute-done.14 = bf16[256,768]{1,0:T(8,128)(2,1)S(1)} collective-permute-done((bf16[256,768]{1,0:T(8,128)(2,1)S(1)}, bf16[256,768]{1,0:T(8,128)(2,1)S(1)}, u32[]{:S(2)}, u32[]{:S(2)}) %collective-permute-start.14) | collective-permute-done | bytes 393248 | tf_op jit(solution)/shard_map/ppermute | solution.py:19
  240.7 8.1 %collective-permute-done.18 = bf16[256,768]{1,0:T(8,128)(2,1)S(1)} collective-permute-done((bf16[256,768]{1,0:T(8,128)(2,1)S(1)}, bf16[256,768]{1,0:T(8,128)(2,1)S(1)}, u32[]{:S(2)}, u32[]{:S(2)}) %collective-permute-start.18) | collective-permute-done | bytes 393248 | tf_op jit(solution)/shard_map/ppermute | solution.py:19
  253.2 4.1 %collective-permute-done.24 = f32[192,256]{1,0:T(8,128)S(1)} collective-permute-done((f32[192,256]{1,0:T(8,128)S(1)}, f32[192,256]{1,0:T(8,128)S(1)}, u32[]{:S(2)}, u32[]{:S(2)}) %collective-permute-start.24) | collective-permute-done | bytes 196640 | tf_op jit(solution)/shard_map/ppermute | solution.py:48
  257.7 5.9 %collective-permute-done.23 = f32[192,384]{1,0:T(8,128)S(1)} collective-permute-done((f32[192,384]{1,0:T(8,128)S(1)}, f32[192,384]{1,0:T(8,128)S(1)}, u32[]{:S(2)}, u32[]{:S(2)}) %collective-permute-start.23) | collective-permute-done | bytes 294944 | tf_op jit(solution)/shard_map/ppermute | solution.py:48
  263.6 2.0 collective-permute-done.22
  265.6 1.8 collective-permute-start.29
  267.8 1.8 collective-permute-start.27
  270.6 2.7 shard_map.314
  273.3 1.9 collective-permute-done.27
  276.3 2.9 shard_map.315
  279.2 2.9 copy.69
  282.8 3.9 %collective-permute-done.26.refs_1_ = bf16[256,768]{1,0:T(8,128)(2,1)} collective-permute-done((bf16[256,768]{1,0:T(8,128)(2,1)}, bf16[256,768]{1,0:T(8,128)(2,1)}, u32[]{:S(2)}, u32[]{:S(2)}) %collective-permute-start.26) | collective-permute-done | bytes 393248 | tf_op jit(solution)/shard_map/ppermute | solution.py:19
  287.3 3.3 collective-permute-start.33
  291.2 2.9 fusion.8
  294.1 3.4 collective-permute-done.31
  297.5 11.3 %collective-permute-done.32 = f32[104,256]{1,0:T(8,128)S(1)} collective-permute-done((f32[104,256]{1,0:T(8,128)S(1)}, f32[104,256]{1,0:T(8,128)S(1)}, u32[]{:S(2)}, u32[]{:S(2)}) %collective-permute-start.32) | collective-permute-done | bytes 106528 | tf_op jit(solution)/shard_map/ppermute | solution.py:19
  308.8 2.8 collective-permute-start.39
  311.7 1.8 collective-permute-start.41
  313.8 16.6 %collective-permute-start.37 = (bf16[256,768]{1,0:T(8,128)(2,1)S(1)}, bf16[256,768]{1,0:T(8,128)(2,1)S(1)}, u32[]{:S(2)}, u32[]{:S(2)}) collective-permute-start(bf16[256,768]{1,0:T(8,128)(2,1)S(1)} %collective-permute-done.30.refs_2_), channel_id=1, source_target_pairs={{0,1},{1,2},{2,3},{3,0},{4,5},{5,6},{6,7},{7,4},{8,9},{9,10},{10,1... | collective-permute-start | bytes 1179656 | tf_op jit(solution)/shard_map/ppermute | solution.py:19
  333.2 3.0 collective-permute-done.43
  336.3 3.1 collective-permute-done.42
  347.8 3.5 shard_map.316.refs_0_
  351.9 2.1 maximum_select_fusion.1
  353.9 2.4 maximum_select_fusion
  357.8 3.5 shard_map.317
  (219 shorter events, 57.1 us)
Async XLA Ops:
  7.2 205.4 %all-reduce.3.cloned.1.call-start = ((), (), s32[]{:S(2)}) async-start(), calls=%async_computation | async-start | bytes 4718592 | tf_op jit(solution)/shard_map/psum | solution.py:767
  11.2 25.7 %collective-permute-start.1 = (bf16[192,2048]{1,0:T(8,128)(2,1)}, bf16[192,2048]{1,0:T(8,128)(2,1)S(1)}, u32[]{:S(2)}, u32[]{:S(2)}) collective-permute-start(bf16[192,2048]{1,0:T(8,128)(2,1)} %bitcast.83), channel_id=1, source_target_pairs={{0,1},{1,2},{2,3},{3,0},{4,5},{5,6},{6,7},{7,4},{8,9},{9,10},{10,1... | collective-permute-start | bytes 2359304 | tf_op jit(solution)/shard_map/ppermute | solution.py:19
  36.9 21.7 %collective-permute-start.2 = (bf16[192,2048]{1,0:T(8,128)(2,1)S(1)}, bf16[192,2048]{1,0:T(8,128)(2,1)S(1)}, u32[]{:S(2)}, u32[]{:S(2)}) collective-permute-start(bf16[192,2048]{1,0:T(8,128)(2,1)S(1)} %collective-permute-done.1.refs_1_), channel_id=1, source_target_pairs={{0,1},{1,2},{2,3},{3,0},{4,5},{5,6},{6,7},{7,4},{8,9},{9,10},{10,1... | collective-permute-start | bytes 2359304 | tf_op jit(solution)/shard_map/ppermute | solution.py:19
  58.7 27.9 %collective-permute-start.3 = (bf16[192,2048]{1,0:T(8,128)(2,1)S(1)}, bf16[192,2048]{1,0:T(8,128)(2,1)S(1)}, u32[]{:S(2)}, u32[]{:S(2)}) collective-permute-start(bf16[192,2048]{1,0:T(8,128)(2,1)S(1)} %collective-permute-done.2.refs_2_), channel_id=1, source_target_pairs={{0,1},{1,2},{2,3},{3,0},{4,5},{5,6},{6,7},{7,4},{8,9},{9,10},{10,1... | collective-permute-start | bytes 2359304 | tf_op jit(solution)/shard_map/ppermute | solution.py:19
  86.7 18.0 %collective-permute-start.4 = (f32[8,8,256]{2,1,0:T(8,128)}, f32[8,8,256]{2,1,0:T(8,128)S(1)}, u32[]{:S(2)}, u32[]{:S(2)}) collective-permute-start(f32[8,8,256]{2,1,0:T(8,128)} %get-tuple-element.139), channel_id=1, source_target_pairs={{0,1},{1,2},{2,3},{3,0},{4,5},{5,6},{6,7},{7,4},{8,9},{9,10},{10,1... | collective-permute-start | bytes 196616 | tf_op jit(solution)/shard_map/ppermute | solution.py:19
  88.1 19.0 %collective-permute-start.5 = (f32[8,8,256]{2,1,0:T(8,128)}, f32[8,8,256]{2,1,0:T(8,128)S(1)}, u32[]{:S(2)}, u32[]{:S(2)}) collective-permute-start(f32[8,8,256]{2,1,0:T(8,128)} %get-tuple-element.139), channel_id=1, source_target_pairs={{0,2},{1,3},{2,0},{3,1},{4,6},{5,7},{6,4},{7,5},{8,10},{9,11},{10,... | collective-permute-start | bytes 196616 | tf_op jit(solution)/shard_map/ppermute | solution.py:19
  91.1 16.0 %collective-permute-start.6 = (f32[8,8,256]{2,1,0:T(8,128)}, f32[8,8,256]{2,1,0:T(8,128)S(1)}, u32[]{:S(2)}, u32[]{:S(2)}) collective-permute-start(f32[8,8,256]{2,1,0:T(8,128)} %get-tuple-element.139), channel_id=1, source_target_pairs={{0,3},{1,0},{2,1},{3,2},{4,7},{5,4},{6,5},{7,6},{8,11},{9,8},{10,9... | collective-permute-start | bytes 196616 | tf_op jit(solution)/shard_map/ppermute | solution.py:19
  102.6 14.9 %collective-permute-start.7 = (f32[8,8,256]{2,1,0:T(8,128)}, f32[8,8,256]{2,1,0:T(8,128)S(1)}, u32[]{:S(2)}, u32[]{:S(2)}) collective-permute-start(f32[8,8,256]{2,1,0:T(8,128)} %get-tuple-element.146), channel_id=1, source_target_pairs={{0,1},{1,2},{2,3},{3,0},{4,5},{5,6},{6,7},{7,4},{8,9},{9,10},{10,1... | collective-permute-start | bytes 196616 | tf_op jit(solution)/shard_map/ppermute | solution.py:19
  104.7 12.9 %collective-permute-start.8 = (f32[8,8,256]{2,1,0:T(8,128)}, f32[8,8,256]{2,1,0:T(8,128)S(1)}, u32[]{:S(2)}, u32[]{:S(2)}) collective-permute-start(f32[8,8,256]{2,1,0:T(8,128)} %get-tuple-element.146), channel_id=1, source_target_pairs={{0,2},{1,3},{2,0},{3,1},{4,6},{5,7},{6,4},{7,5},{8,10},{9,11},{10,... | collective-permute-start | bytes 196616 | tf_op jit(solution)/shard_map/ppermute | solution.py:19
  104.7 12.9 %collective-permute-start.9 = (f32[8,8,256]{2,1,0:T(8,128)}, f32[8,8,256]{2,1,0:T(8,128)S(1)}, u32[]{:S(2)}, u32[]{:S(2)}) collective-permute-start(f32[8,8,256]{2,1,0:T(8,128)} %get-tuple-element.146), channel_id=1, source_target_pairs={{0,3},{1,0},{2,1},{3,2},{4,7},{5,4},{6,5},{7,6},{8,11},{9,8},{10,9... | collective-permute-start | bytes 196616 | tf_op jit(solution)/shard_map/ppermute | solution.py:19
  119.4 30.1 %collective-permute-start.10 = (bf16[192,2048]{1,0:T(8,128)(2,1)S(1)}, bf16[192,2048]{1,0:T(8,128)(2,1)S(1)}, u32[]{:S(2)}, u32[]{:S(2)}) collective-permute-start(bf16[192,2048]{1,0:T(8,128)(2,1)S(1)} %dynamic-slice_bitcast_fusion), channel_id=1, source_target_pairs={{0,1},{1,2},{2,3},{3,0},{4,5},{5,6},{6,7},{7,4},{8,9},{9,10},{10,1... | collective-permute-start | bytes 2359304 | tf_op jit(solution)/shard_map/ppermute | solution.py:19
  150.9 39.3 %collective-permute-start.11 = (bf16[192,2048]{1,0:T(8,128)(2,1)S(1)}, bf16[192,2048]{1,0:T(8,128)(2,1)}, u32[]{:S(2)}, u32[]{:S(2)}) collective-permute-start(bf16[192,2048]{1,0:T(8,128)(2,1)S(1)} %fusion.7), channel_id=1, source_target_pairs={{0,1},{1,2},{2,3},{3,0},{4,5},{5,6},{6,7},{7,4},{8,9},{9,10},{10,1... | collective-permute-start | bytes 2359304 | tf_op jit(solution)/shard_map/ppermute | solution.py:19
  192.0 21.6 %collective-permute-start.12 = (bf16[192,2048]{1,0:T(8,128)(2,1)S(1)}, bf16[192,2048]{1,0:T(8,128)(2,1)S(1)}, u32[]{:S(2)}, u32[]{:S(2)}) collective-permute-start(bf16[192,2048]{1,0:T(8,128)(2,1)S(1)} %fusion.6), channel_id=1, source_target_pairs={{0,1},{1,2},{2,3},{3,0},{4,5},{5,6},{6,7},{7,4},{8,9},{9,10},{10,1... | collective-permute-start | bytes 2359304 | tf_op jit(solution)/shard_map/ppermute | solution.py:19
  210.5 16.4 %collective-permute-start.17 = (bf16[256,768]{1,0:T(8,128)(2,1)S(1)}, bf16[256,768]{1,0:T(8,128)(2,1)S(1)}, u32[]{:S(2)}, u32[]{:S(2)}) collective-permute-start(bf16[256,768]{1,0:T(8,128)(2,1)S(1)} %constant_dynamic-slice_fusion), channel_id=1, source_target_pairs={{0,1},{1,2},{2,3},{3,0},{4,5},{5,6},{6,7},{7,4},{8,9},{9,10},{10,1... | collective-permute-start | bytes 1179656 | tf_op jit(solution)/shard_map/ppermute | solution.py:19
  226.8 13.5 %collective-permute-start.14 = (bf16[256,768]{1,0:T(8,128)(2,1)S(1)}, bf16[256,768]{1,0:T(8,128)(2,1)S(1)}, u32[]{:S(2)}, u32[]{:S(2)}) collective-permute-start(bf16[256,768]{1,0:T(8,128)(2,1)S(1)} %constant_dynamic-slice_fusion.1), channel_id=1, source_target_pairs={{0,1},{1,2},{2,3},{3,0},{4,5},{5,6},{6,7},{7,4},{8,9},{9,10},{10,1... | collective-permute-start | bytes 1179656 | tf_op jit(solution)/shard_map/ppermute | solution.py:19
  226.9 6.2 %collective-permute-start.21 = (f32[16,768]{1,0:T(8,128)}, f32[16,768]{1,0:T(8,128)S(1)}, u32[]{:S(2)}, u32[]{:S(2)}) collective-permute-start(f32[16,768]{1,0:T(8,128)} %get-tuple-element.182), channel_id=1, source_target_pairs={{0,4},{4,0},{8,12},{12,8},{16,20},{20,16},{24,28},{28,24},{1,5},{5... | collective-permute-start | bytes 147464 | tf_op jit(solution)/shard_map/ppermute | solution.py:59
  229.6 10.9 %collective-permute-start.20 = (f32[384,256]{1,0:T(8,128)S(1)}, f32[384,256]{1,0:T(8,128)S(1)}, u32[]{:S(2)}, u32[]{:S(2)}) collective-permute-start(f32[384,256]{1,0:T(8,128)S(1)} %dynamic-slice_bitcast_fusion.2), channel_id=1, source_target_pairs={{0,4},{4,0},{8,12},{12,8},{16,20},{20,16},{24,28},{28,24},{1,5},{5... | collective-permute-start | bytes 1179656 | tf_op jit(solution)/shard_map/ppermute | solution.py:48
  230.9 9.7 %collective-permute-start.19 = (f32[384,384]{1,0:T(8,128)S(1)}, f32[384,384]{1,0:T(8,128)S(1)}, u32[]{:S(2)}, u32[]{:S(2)}) collective-permute-start(f32[384,384]{1,0:T(8,128)S(1)} %dynamic-slice_bitcast_fusion.1), channel_id=1, source_target_pairs={{0,4},{4,0},{8,12},{12,8},{16,20},{20,16},{24,28},{28,24},{1,5},{5... | collective-permute-start | bytes 1769480 | tf_op jit(solution)/shard_map/ppermute | solution.py:48
  231.5 17.2 %collective-permute-start.18 = (bf16[256,768]{1,0:T(8,128)(2,1)S(1)}, bf16[256,768]{1,0:T(8,128)(2,1)S(1)}, u32[]{:S(2)}, u32[]{:S(2)}) collective-permute-start(bf16[256,768]{1,0:T(8,128)(2,1)S(1)} %add_convert_fusion.1), channel_id=1, source_target_pairs={{0,1},{1,2},{2,3},{3,0},{4,5},{5,6},{6,7},{7,4},{8,9},{9,10},{10,1... | collective-permute-start | bytes 1179656 | tf_op jit(solution)/shard_map/ppermute | solution.py:19
  240.5 16.8 %collective-permute-start.15 = (bf16[256,768]{1,0:T(8,128)(2,1)S(1)}, bf16[256,768]{1,0:T(8,128)(2,1)S(1)}, u32[]{:S(2)}, u32[]{:S(2)}) collective-permute-start(bf16[256,768]{1,0:T(8,128)(2,1)S(1)} %add_convert_fusion.3), channel_id=1, source_target_pairs={{0,1},{1,2},{2,3},{3,0},{4,5},{5,6},{6,7},{7,4},{8,9},{9,10},{10,1... | collective-permute-start | bytes 1179656 | tf_op jit(solution)/shard_map/ppermute | solution.py:19
  248.8 4.4 %collective-permute-start.25 = (f32[16,768]{1,0:T(8,128)S(1)}, f32[16,768]{1,0:T(8,128)S(1)}, u32[]{:S(2)}, u32[]{:S(2)}) collective-permute-start(f32[16,768]{1,0:T(8,128)S(1)} %add.326), channel_id=1, source_target_pairs={{0,8},{4,12},{8,0},{12,4},{16,24},{20,28},{24,16},{28,20},{1,9},{5... | collective-permute-start | bytes 147464 | tf_op jit(solution)/shard_map/ppermute | solution.py:59
  249.2 8.1 %collective-permute-start.24 = (f32[192,256]{1,0:T(8,128)S(1)}, f32[192,256]{1,0:T(8,128)S(1)}, u32[]{:S(2)}, u32[]{:S(2)}) collective-permute-start(f32[192,256]{1,0:T(8,128)S(1)} %dynamic-slice_bitcast_fusion.4), channel_id=1, source_target_pairs={{0,8},{4,12},{8,0},{12,4},{16,24},{20,28},{24,16},{28,20},{1,9},{5... | collective-permute-start | bytes 589832 | tf_op jit(solution)/shard_map/ppermute | solution.py:48
  250.9 12.7 %collective-permute-start.23 = (f32[192,384]{1,0:T(8,128)S(1)}, f32[192,384]{1,0:T(8,128)S(1)}, u32[]{:S(2)}, u32[]{:S(2)}) collective-permute-start(f32[192,384]{1,0:T(8,128)S(1)} %dynamic-slice_bitcast_fusion.3), channel_id=1, source_target_pairs={{0,8},{4,12},{8,0},{12,4},{16,24},{20,28},{24,16},{28,20},{1,9},{5... | collective-permute-start | bytes 884744 | tf_op jit(solution)/shard_map/ppermute | solution.py:48
  251.5 14.1 %collective-permute-start.22 = (bf16[256,768]{1,0:T(8,128)(2,1)S(1)}, bf16[256,768]{1,0:T(8,128)(2,1)S(1)}, u32[]{:S(2)}, u32[]{:S(2)}) collective-permute-start(bf16[256,768]{1,0:T(8,128)(2,1)S(1)} %add_convert_fusion), channel_id=1, source_target_pairs={{0,1},{1,2},{2,3},{3,0},{4,5},{5,6},{6,7},{7,4},{8,9},{9,10},{10,1... | collective-permute-start | bytes 1179656 | tf_op jit(solution)/shard_map/ppermute | solution.py:19
  257.4 17.9 %collective-permute-start.16 = (bf16[256,768]{1,0:T(8,128)(2,1)S(1)}, bf16[256,768]{1,0:T(8,128)(2,1)S(1)}, u32[]{:S(2)}, u32[]{:S(2)}) collective-permute-start(bf16[256,768]{1,0:T(8,128)(2,1)S(1)} %add_convert_fusion.2), channel_id=1, source_target_pairs={{0,1},{1,2},{2,3},{3,0},{4,5},{5,6},{6,7},{7,4},{8,9},{9,10},{10,1... | collective-permute-start | bytes 1179656 | tf_op jit(solution)/shard_map/ppermute | solution.py:19
  265.6 7.6 %collective-permute-start.29 = (f32[16,768]{1,0:T(8,128)S(1)}, f32[16,768]{1,0:T(8,128)S(1)}, u32[]{:S(2)}, u32[]{:S(2)}) collective-permute-start(f32[16,768]{1,0:T(8,128)S(1)} %add.333), channel_id=1, source_target_pairs={{0,16},{4,20},{8,24},{12,28},{16,0},{20,4},{24,8},{28,12},{1,17},{... | collective-permute-start | bytes 147464 | tf_op jit(solution)/shard_map/ppermute | solution.py:59
  267.4 5.9 %collective-permute-start.28 = (f32[96,256]{1,0:T(8,128)S(1)}, f32[96,256]{1,0:T(8,128)S(1)}, u32[]{:S(2)}, u32[]{:S(2)}) collective-permute-start(f32[96,256]{1,0:T(8,128)S(1)} %dynamic-slice_bitcast_fusion.6), channel_id=1, source_target_pairs={{0,16},{4,20},{8,24},{12,28},{16,0},{20,4},{24,8},{28,12},{1,17},{... | collective-permute-start | bytes 294920 | tf_op jit(solution)/shard_map/ppermute | solution.py:48
  267.8 7.5 %collective-permute-start.27 = (f32[96,384]{1,0:T(8,128)S(1)}, f32[96,384]{1,0:T(8,128)S(1)}, u32[]{:S(2)}, u32[]{:S(2)}) collective-permute-start(f32[96,384]{1,0:T(8,128)S(1)} %dynamic-slice_bitcast_fusion.5), channel_id=1, source_target_pairs={{0,16},{4,20},{8,24},{12,28},{16,0},{20,4},{24,8},{28,12},{1,17},{... | collective-permute-start | bytes 442376 | tf_op jit(solution)/shard_map/ppermute | solution.py:48
  273.3 13.4 %collective-permute-start.26 = (bf16[256,768]{1,0:T(8,128)(2,1)}, bf16[256,768]{1,0:T(8,128)(2,1)}, u32[]{:S(2)}, u32[]{:S(2)}) collective-permute-start(bf16[256,768]{1,0:T(8,128)(2,1)} %get-tuple-element.188.refs_0_), channel_id=1, source_target_pairs={{0,1},{1,2},{2,3},{3,0},{4,5},{5,6},{6,7},{7,4},{8,9},{9,10},{10,1... | collective-permute-start | bytes 1179656 | tf_op jit(solution)/shard_map/ppermute | solution.py:19
  279.2 29.6 %collective-permute-start.38 = (bf16[256,768]{1,0:T(8,128)(2,1)}, bf16[256,768]{1,0:T(8,128)(2,1)}, u32[]{:S(2)}, u32[]{:S(2)}) collective-permute-start(bf16[256,768]{1,0:T(8,128)(2,1)} %get-tuple-element.203.refs_1_), channel_id=1, source_target_pairs={{0,1},{1,2},{2,3},{3,0},{4,5},{5,6},{6,7},{7,4},{8,9},{9,10},{10,1... | collective-permute-start | bytes 1179656 | tf_op jit(solution)/shard_map/ppermute | solution.py:19
  286.7 10.7 %collective-permute-start.31 = (f32[104,256]{1,0:T(8,128)S(1)}, f32[104,256]{1,0:T(8,128)S(1)}, u32[]{:S(2)}, u32[]{:S(2)}) collective-permute-start(f32[104,256]{1,0:T(8,128)S(1)} %pad_maximum_fusion), channel_id=1, source_target_pairs={{0,1},{1,2},{2,3},{3,0},{4,5},{5,6},{6,7},{7,4},{8,9},{9,10},{10,1... | collective-permute-start | bytes 319496 | tf_op jit(solution)/shard_map/ppermute | solution.py:19
  286.8 21.9 %collective-permute-start.32 = (f32[104,256]{1,0:T(8,128)S(1)}, f32[104,256]{1,0:T(8,128)S(1)}, u32[]{:S(2)}, u32[]{:S(2)}) collective-permute-start(f32[104,256]{1,0:T(8,128)S(1)} %pad_maximum_fusion), channel_id=1, source_target_pairs={{0,2},{1,3},{2,0},{3,1},{4,6},{5,7},{6,4},{7,5},{8,10},{9,11},{10,... | collective-permute-start | bytes 319496 | tf_op jit(solution)/shard_map/ppermute | solution.py:19
  287.3 21.5 %collective-permute-start.33 = (f32[104,256]{1,0:T(8,128)S(1)}, f32[104,256]{1,0:T(8,128)S(1)}, u32[]{:S(2)}, u32[]{:S(2)}) collective-permute-start(f32[104,256]{1,0:T(8,128)S(1)} %pad_maximum_fusion), channel_id=1, source_target_pairs={{0,3},{1,0},{2,1},{3,2},{4,7},{5,4},{6,5},{7,6},{8,11},{9,8},{10,9... | collective-permute-start | bytes 319496 | tf_op jit(solution)/shard_map/ppermute | solution.py:19
  290.6 21.0 %collective-permute-start.30 = (bf16[256,768]{1,0:T(8,128)(2,1)}, bf16[256,768]{1,0:T(8,128)(2,1)S(1)}, u32[]{:S(2)}, u32[]{:S(2)}) collective-permute-start(bf16[256,768]{1,0:T(8,128)(2,1)} %collective-permute-done.26.refs_1_), channel_id=1, source_target_pairs={{0,1},{1,2},{2,3},{3,0},{4,5},{5,6},{6,7},{7,4},{8,9},{9,10},{10,1... | collective-permute-start | bytes 1179656 | tf_op jit(solution)/shard_map/ppermute | solution.py:19
  297.5 16.0 %collective-permute-start.34 = (f32[6,128]{1,0:T(8,128)S(1)}, f32[6,128]{1,0:T(8,128)S(1)}, u32[]{:S(2)}, u32[]{:S(2)}) collective-permute-start(f32[6,128]{1,0:T(8,128)S(1)} %bitcast.110), channel_id=1, source_target_pairs={{0,1},{1,2},{2,3},{3,0},{4,5},{5,6},{6,7},{7,4},{8,9},{9,10},{10,1... | collective-permute-start | bytes 9224 | tf_op jit(solution)/shard_map/ppermute | solution.py:19
  308.7 5.1 %collective-permute-start.35 = (f32[6,128]{1,0:T(8,128)S(1)}, f32[6,128]{1,0:T(8,128)S(1)}, u32[]{:S(2)}, u32[]{:S(2)}) collective-permute-start(f32[6,128]{1,0:T(8,128)S(1)} %bitcast.111), channel_id=1, source_target_pairs={{0,2},{1,3},{2,0},{3,1},{4,6},{5,7},{6,4},{7,5},{8,10},{9,11},{10,... | collective-permute-start | bytes 9224 | tf_op jit(solution)/shard_map/ppermute | solution.py:19
  308.7 5.1 %collective-permute-start.36 = (f32[6,128]{1,0:T(8,128)S(1)}, f32[6,128]{1,0:T(8,128)S(1)}, u32[]{:S(2)}, u32[]{:S(2)}) collective-permute-start(f32[6,128]{1,0:T(8,128)S(1)} %bitcast.112), channel_id=1, source_target_pairs={{0,3},{1,0},{2,1},{3,2},{4,7},{5,4},{6,5},{7,6},{8,11},{9,8},{10,9... | collective-permute-start | bytes 9224 | tf_op jit(solution)/shard_map/ppermute | solution.py:19
  308.8 21.7 %collective-permute-start.39 = (bf16[256,768]{1,0:T(8,128)(2,1)}, bf16[256,768]{1,0:T(8,128)(2,1)S(1)}, u32[]{:S(2)}, u32[]{:S(2)}) collective-permute-start(bf16[256,768]{1,0:T(8,128)(2,1)} %collective-permute-done.38.refs_2_), channel_id=1, source_target_pairs={{0,1},{1,2},{2,3},{3,0},{4,5},{5,6},{6,7},{7,4},{8,9},{9,10},{10,1... | collective-permute-start | bytes 1179656 | tf_op jit(solution)/shard_map/ppermute | solution.py:19
  311.7 18.7 %collective-permute-start.41 = (f32[96,256]{1,0:T(8,128)S(1)}, f32[96,256]{1,0:T(8,128)S(1)}, u32[]{:S(2)}, u32[]{:S(2)}) collective-permute-start(f32[96,256]{1,0:T(8,128)S(1)} %slice.77), channel_id=1, source_target_pairs={{0,16},{4,20},{8,24},{12,28},{16,0},{20,4},{24,8},{28,12},{1,17},{... | collective-permute-start | bytes 294920 | tf_op jit(solution)/shard_map/ppermute | solution.py:53
  313.5 17.0 %collective-permute-start.40 = (f32[96,384]{1,0:T(8,128)S(1)}, f32[96,384]{1,0:T(8,128)S(1)}, u32[]{:S(2)}, u32[]{:S(2)}) collective-permute-start(f32[96,384]{1,0:T(8,128)S(1)} %bitcast_add_fusion.4), channel_id=1, source_target_pairs={{0,16},{4,20},{8,24},{12,28},{16,0},{20,4},{24,8},{28,12},{1,17},{... | collective-permute-start | bytes 442376 | tf_op jit(solution)/shard_map/ppermute | solution.py:53
  313.8 25.6 %collective-permute-start.37 = (bf16[256,768]{1,0:T(8,128)(2,1)S(1)}, bf16[256,768]{1,0:T(8,128)(2,1)S(1)}, u32[]{:S(2)}, u32[]{:S(2)}) collective-permute-start(bf16[256,768]{1,0:T(8,128)(2,1)S(1)} %collective-permute-done.30.refs_2_), channel_id=1, source_target_pairs={{0,1},{1,2},{2,3},{3,0},{4,5},{5,6},{6,7},{7,4},{8,9},{9,10},{10,1... | collective-permute-start | bytes 1179656 | tf_op jit(solution)/shard_map/ppermute | solution.py:19
  330.5 5.7 %collective-permute-start.43 = (f32[192,256]{1,0:T(8,128)S(1)}, f32[192,256]{1,0:T(8,128)S(1)}, u32[]{:S(2)}, u32[]{:S(2)}) collective-permute-start(f32[192,256]{1,0:T(8,128)S(1)} %maximum_select_fusion.5), channel_id=1, source_target_pairs={{0,8},{4,12},{8,0},{12,4},{16,24},{20,28},{24,16},{28,20},{1,9},{5... | collective-permute-start | bytes 589832 | tf_op jit(solution)/shard_map/ppermute | solution.py:53
  330.9 8.4 %collective-permute-start.42 = (f32[192,384]{1,0:T(8,128)S(1)}, f32[192,384]{1,0:T(8,128)S(1)}, u32[]{:S(2)}, u32[]{:S(2)}) collective-permute-start(f32[192,384]{1,0:T(8,128)S(1)} %maximum_select_fusion.4), channel_id=1, source_target_pairs={{0,8},{4,12},{8,0},{12,4},{16,24},{20,28},{24,16},{28,20},{1,9},{5... | collective-permute-start | bytes 884744 | tf_op jit(solution)/shard_map/ppermute | solution.py:53
  333.2 6.9 %collective-permute-start.44 = (f32[6,128]{1,0:T(8,128)S(1)}, f32[6,128]{1,0:T(8,128)S(1)}, u32[]{:S(2)}, u32[]{:S(2)}) collective-permute-start(f32[6,128]{1,0:T(8,128)S(1)} %add_add_fusion.3), channel_id=1, source_target_pairs={{0,4},{4,0},{8,12},{12,8},{16,20},{20,16},{24,28},{28,24},{1,5},{5... | collective-permute-start | bytes 9224 | tf_op jit(solution)/shard_map/ppermute | solution.py:59
  339.4 14.5 %collective-permute-start.47 = (f32[384,384]{1,0:T(8,128)S(1)}, f32[384,384]{1,0:T(8,128)}, u32[]{:S(2)}, u32[]{:S(2)}) collective-permute-start(f32[384,384]{1,0:T(8,128)S(1)} %maximum_select_fusion.2), channel_id=1, source_target_pairs={{0,4},{4,0},{8,12},{12,8},{16,20},{20,16},{24,28},{28,24},{1,5},{5... | collective-permute-start | bytes 1769480 | tf_op jit(solution)/shard_map/ppermute | solution.py:53
  340.6 11.3 %collective-permute-start.48 = (f32[384,256]{1,0:T(8,128)S(1)}, f32[384,256]{1,0:T(8,128)}, u32[]{:S(2)}, u32[]{:S(2)}) collective-permute-start(f32[384,256]{1,0:T(8,128)S(1)} %maximum_select_fusion.3), channel_id=1, source_target_pairs={{0,4},{4,0},{8,12},{12,8},{16,20},{20,16},{24,28},{28,24},{1,5},{5... | collective-permute-start | bytes 1179656 | tf_op jit(solution)/shard_map/ppermute | solution.py:53
  343.6 13.4 %collective-permute-start.46 = (bf16[256,768]{1,0:T(8,128)(2,1)}, bf16[256,768]{1,0:T(8,128)(2,1)S(1)}, u32[]{:S(2)}, u32[]{:S(2)}) collective-permute-start(bf16[256,768]{1,0:T(8,128)(2,1)} %copy-done.15), channel_id=1, source_target_pairs={{0,1},{1,2},{2,3},{3,0},{4,5},{5,6},{6,7},{7,4},{8,9},{9,10},{10,1... | collective-permute-start | bytes 1179656 | tf_op jit(solution)/shard_map/ppermute | solution.py:19
  343.8 7.5 %collective-permute-start.49 = (f32[6,128]{1,0:T(8,128)S(1)}, f32[6,128]{1,0:T(8,128)S(1)}, u32[]{:S(2)}, u32[]{:S(2)}) collective-permute-start(f32[6,128]{1,0:T(8,128)S(1)} %add.349), channel_id=1, source_target_pairs={{0,16},{4,20},{8,24},{12,28},{16,0},{20,4},{24,8},{28,12},{1,17},{... | collective-permute-start | bytes 9224 | tf_op jit(solution)/shard_map/ppermute | solution.py:59
  (31 other events, 322.2 us)
Sparse Core Ops, SparseCore 0:
  137.3 65.4 all-reduce.2
